TPU v7x, 128 devices: a whole 4x4x4 slice. The times are simulated.
128 devices in a mesh: dap: 8 (over y_hi, z), bulk: 16 (over y_lo, x, core).
Axes of the slice: x: 4, y: 4 (y_hi: 2, y_lo: 2; y = y_hi * 2 + y_lo), z: 4, core: 2. Of those that a mesh axis runs over, the one named last changes fastest.
Arguments:
- stacked_relatives_tensor: bfloat16 [128, 1024, 256], P('bulk', 'dap'), may hold values from -6 to 6
- couple_embedding: bfloat16 [1024, 1024, 128], P(('dap', 'bulk')), may hold values from -6 to 6
- relatives_rescaler: float32 [256], replicated, may hold values from 0.25 to 2
- averaged_lhs_weights: bfloat16 [256, 32], replicated, may hold values from -0.375 to 0.375
- averaged_rhs_weights: bfloat16 [256, 32], replicated, may hold values from -0.375 to 0.375
- mean_final_linear: bfloat16 [1024, 128], replicated, may hold values from -0.75 to 0.75
- couple_scale_vector: float32 [128], replicated, may hold values from 0.25 to 2
- first_linear_map: bfloat16 [128, 128], replicated, may hold values from -0.5 to 0.5
- first_sigmoid_factor: bfloat16 [128, 128], replicated, may hold values from -0.5 to 0.5
- second_linear_map: bfloat16 [128, 128], replicated, may hold values from -0.5 to 0.5
- second_sigmoid_factor: bfloat16 [128, 128], replicated, may hold values from -0.5 to 0.5
- final_sigmoid_factor: bfloat16 [128, 128], replicated, may hold values from -0.5 to 0.5
- trio_scale_vector: float32 [128], replicated, may hold values from 0.25 to 2
- trio_final_linear: bfloat16 [128, 128], replicated, may hold values from -0.5 to 0.5
Outputs:
- new_pair: bfloat16 [1024, 1024, 128], P(('dap', 'bulk'))
All inputs are finite; a program needn't handle non-finite values.
Results may differ from a plain program's by a relative error of at most 0.012.
Values may be sent and summed in bfloat16 or wider, within the bound.
No kernel may reach another device: no remote copies, remote signals or barrier semaphores. Data moves between devices by JAX's collectives and lax.ppermute only.
A program may use at most 192 MiB of HBM per device.

v0:
```python
import jax
import jax.numpy as jnp
from jax import lax
from jax.sharding import PartitionSpec as P


def standardize_features(values, gain):
    center = values - jnp.mean(values, axis=-1, keepdims=True)
    spread = jnp.mean(center * center, axis=-1, keepdims=True)
    return center / jnp.sqrt(spread + 1e-05) * gain


def alignment_projector(
    alignment_block, relatives_rescaler, averaged_lhs_weights, averaged_rhs_weights
):
    homolog_standardized = standardize_features(
        alignment_block.astype(jnp.float32), relatives_rescaler
    ).astype(jnp.bfloat16)
    left_alignment_projection = jnp.dot(
        homolog_standardized, averaged_lhs_weights, preferred_element_type=jnp.float32
    ).astype(jnp.bfloat16)
    right_alignment_projection = jnp.dot(
        homolog_standardized, averaged_rhs_weights, preferred_element_type=jnp.float32
    ).astype(jnp.bfloat16)
    return (left_alignment_projection, right_alignment_projection)


def gated_operand(pair_normed, proj_weight, gate_weight):
    linear_part = jnp.dot(pair_normed, proj_weight, preferred_element_type=jnp.float32)
    gate_part = jax.nn.sigmoid(
        jnp.dot(pair_normed, gate_weight, preferred_element_type=jnp.float32)
    )
    return (gate_part * linear_part).astype(jnp.bfloat16)


def body(
    stacked_relatives_tensor,
    couple_embedding,
    relatives_rescaler,
    averaged_lhs_weights,
    averaged_rhs_weights,
    mean_final_linear,
    couple_scale_vector,
    first_linear_map,
    first_sigmoid_factor,
    second_linear_map,
    second_sigmoid_factor,
    final_sigmoid_factor,
    trio_scale_vector,
    trio_final_linear,
):
    hidden_activations = averaged_lhs_weights.shape[1]
    position_axis_list = lax.all_to_all(
        stacked_relatives_tensor, "bulk", split_axis=1, concat_axis=0, tiled=True
    )
    left_alignment_projection, right_alignment_projection = alignment_projector(
        position_axis_list, relatives_rescaler, averaged_lhs_weights, averaged_rhs_weights
    )
    alignment_rows_gathered, local_row_slice, hidden_activations = left_alignment_projection.shape
    left_flattened_rows = left_alignment_projection.transpose(1, 2, 0).reshape(
        local_row_slice * hidden_activations, alignment_rows_gathered
    )
    partial_segment = lax.all_gather(
        right_alignment_projection, ("dap", "bulk"), axis=1, tiled=True
    )
    col_count = partial_segment.shape[1]
    segment_flat = partial_segment.reshape(alignment_rows_gathered, col_count * hidden_activations)
    triangle_products = jnp.dot(
        left_flattened_rows, segment_flat, preferred_element_type=jnp.float32
    ) * (1.0 / alignment_rows_gathered)
    triangle_products = triangle_products.astype(jnp.bfloat16).reshape(
        local_row_slice, hidden_activations, col_count, hidden_activations
    )
    triangle_products = triangle_products.transpose(0, 2, 1, 3).reshape(
        local_row_slice, col_count, hidden_activations * hidden_activations
    )
    opm = jnp.dot(triangle_products, mean_final_linear, preferred_element_type=jnp.float32)
    updated = (couple_embedding.astype(jnp.float32) + opm).astype(jnp.bfloat16)
    pair_normed = standardize_features(updated.astype(jnp.float32), couple_scale_vector).astype(
        jnp.bfloat16
    )
    left_tri = gated_operand(pair_normed, first_linear_map, first_sigmoid_factor)
    right_tri = gated_operand(pair_normed, second_linear_map, second_sigmoid_factor)
    gate = jax.nn.sigmoid(
        jnp.dot(pair_normed, final_sigmoid_factor, preferred_element_type=jnp.float32)
    )
    left_chan = left_tri.transpose(2, 0, 1)
    right_chan = right_tri.transpose(2, 0, 1)
    left_group, right_group = (
        lax.all_to_all(left_chan, "bulk", split_axis=0, concat_axis=1, tiled=True),
        lax.all_to_all(right_chan, "bulk", split_axis=0, concat_axis=1, tiled=True),
    )
    mixed = jnp.einsum(
        "cik,cjk->cij",
        left_group,
        lax.all_gather(right_group, "dap", axis=1, tiled=True),
        preferred_element_type=jnp.float32,
    ).astype(jnp.bfloat16)
    mixed_back = lax.all_to_all(mixed, "bulk", split_axis=1, concat_axis=0, tiled=True)
    mixed_rows = mixed_back.transpose(1, 2, 0).astype(jnp.float32)
    mixed_normed = standardize_features(mixed_rows, trio_scale_vector).astype(jnp.bfloat16)
    output_term = jnp.dot(mixed_normed, trio_final_linear, preferred_element_type=jnp.float32)
    return (updated.astype(jnp.float32) + gate * output_term).astype(jnp.bfloat16)


def solution(mesh):
    return jax.shard_map(
        body,
        mesh=mesh,
        in_specs=(
            P("bulk", "dap", None),
            P(("dap", "bulk"), None, None),
            P(),
            P(),
            P(),
            P(),
            P(),
            P(),
            P(),
            P(),
            P(),
            P(),
            P(),
            P(),
        ),
        out_specs=P(("dap", "bulk"), None, None),
        check_vma=False,
    )
```

profile of v0, /device:TPU:1, one launch (start us, length us, event | category | flops | bytes accessed | tf_op | source)
XLA Modules:
  0.0 667.7 jit_solution(15530014779809084283)
XLA Ops:
  6.5 1.4 copy.184
  7.9 16.5 %all_to_all.54 = bf16[8,128,256]{2,0,1:T(8,128)(2,1)S(1)} all-to-all(bf16[8,128,256]{2,0,1:T(8,128)(2,1)S(1)} %copy.184), channel_id=1, replica_groups=mesh['dap'=8,'bulk'=16] {'bulk'}, dimensions={1} | all-to-all | bytes 1048576 | tf_op jit(solution)/shard_map/all_to_all | solution.py:53
  27.3 2.6 copy.183
  30.4 200.0 %all-gather.3.cloned.1.call-done = bf16[128,1024,32]{0,2,1:T(8,128)(2,1)} async-done(((bf16[128,8,32]{0,2,1:T(8,128)(2,1)}), bf16[128,1024,32]{0,2,1:T(8,128)(2,1)}) %all-gather.3.cloned.1.call-update) | async-done | bytes 8388624 | tf_op jit(solution)/shard_map/all_gather | solution.py:63
  230.4 11.5 %fusion = bf16[256,32768]{1,0:T(8,128)(2,1)} fusion(bf16[256,128]{1,0:T(8,128)(2,1)S(1)} %bitcast.104, bf16[128,32768]{0,1:T(8,128)(2,1)} %bitcast.101), kind=kOutput, calls=%fused_computation.1 | convolution fusion | flops 2164260864 | bytes 25231360 | tf_op jit(solution)/shard_map/dot_general | solution.py:68
  241.9 51.1 %reshape.80 = bf16[8,32,1024,32]{3,2,1,0:T(8,128)(2,1)} reshape(bf16[256,32768]{1,0:T(8,128)(2,1)} %fusion) | data formatting | bytes 33554432 | tf_op jit(solution)/shard_map/reshape | solution.py:71
  293.0 56.4 %copy.196 = bf16[8,1024,32,32]{1,3,2,0:T(8,128)(2,1)} copy(bf16[8,1024,32,32]{3,1,2,0:T(8,128)(2,1)} %bitcast.11) | data formatting | bytes 33554432 | tf_op jit(solution)/shard_map/transpose | solution.py:74
  349.4 11.0 %convert_reduce_fusion = (f32[8,1024]{1,0:T(8,128)S(1)}, bf16[8,1024,128]{1,2,0:T(8,128)(2,1)S(1)}) fusion(bf16[8,1024,1024]{1,2,0:T(8,128)(2,1)} %bitcast.99, bf16[1024,128]{1,0:T(8,128)(2,1)S(1)} %copy-done, bf16[8,1024,128]{1,2,0:T(8,128)(2,1)S(1)} %copy-done.6), kind=kOutput, calls=%fused_computation.4 | convolution fusion | flops 2152718336 | bytes 21266432 | tf_op jit(solution)/shard_map/dot_general | solution.py:77
  362.8 1.7 fusion.15
  364.4 1.2 copy.211
  365.6 31.5 %all_to_all.55 = bf16[128,8,1024]{2,1,0:T(8,128)(2,1)S(1)} all-to-all(bf16[128,8,1024]{2,1,0:T(8,128)(2,1)S(1)} %copy.211), channel_id=1, replica_groups=mesh['dap'=8,'bulk'=16] {'bulk'}, dimensions={0} | all-to-all | bytes 4194304 | tf_op jit(solution)/shard_map/all_to_all | solution.py:91
  397.1 1.5 copy.250
  399.5 1.7 fusion.14
  402.3 34.4 %all_to_all.56 = bf16[128,8,1024]{2,1,0:T(8,128)(2,1)} all-to-all(bf16[128,8,1024]{2,1,0:T(8,128)(2,1)S(1)} %copy.205), channel_id=1, replica_groups=mesh['dap'=8,'bulk'=16] {'bulk'}, dimensions={0} | all-to-all | bytes 4194304 | tf_op jit(solution)/shard_map/all_to_all | solution.py:90
  436.7 162.2 %all-gather.5.cloned.1.call-done = bf16[8,1024,1024]{2,1,0:T(8,128)(2,1)} async-done(((bf16[8,128,1024]{2,1,0:T(8,128)(2,1)}), bf16[8,1024,1024]{2,1,0:T(8,128)(2,1)}) %all-gather.5.cloned.1.call-update) | async-done | bytes 16777232 | tf_op jit(solution)/shard_map/all_gather | solution.py:96
  598.8 13.4 %fusion.11 = bf16[8,128,1024]{2,1,0:T(8,128)(2,1)} fusion(bf16[8,1024,1024]{2,1,0:T(8,128)(2,1)} %all-gather.5.cloned.1.call-done, bf16[16,8,8,1024]{3,2,1,0:T(8,128)(2,1)} %bitcast.100), kind=kOutput, calls=%fused_computation.24 | convolution fusion | flops 2148532224 | bytes 20971520 | tf_op jit(solution)/shard_map/cik,cjk->cij/dot_general | solution.py:93
  612.2 4.1 copy.213
  616.3 5.4 all-to-all-start.3
  621.7 2.8 fusion.29
  624.5 24.6 %all-to-all-done.3 = bf16[8,128,1024]{2,0,1:T(8,128)(2,1)} async-done(((bf16[8,128,1024]{2,0,1:T(8,128)(2,1)}), bf16[8,128,1024]{2,0,1:T(8,128)(2,1)}, u32[]{:S(2)}, u32[]{:S(2)}) %all-to-all-start.3) | async-done | bytes 2097184 | tf_op jit(solution)/shard_map/all_to_all | solution.py:99
  649.1 2.8 convert_bitcast_fusion
  654.8 1.2 copy-done.4
  656.0 2.4 fusion.6
  658.4 2.4 copy.218
  (68 shorter events, 10.3 us)
Async XLA Ops:
  6.5 342.8 %copy-start = (bf16[1024,128]{1,0:T(8,128)(2,1)S(1)}, bf16[1024,128]{1,0:T(8,128)(2,1)}, u32[]{:S(2)}) copy-start(bf16[1024,128]{1,0:T(8,128)(2,1)} %param.19) | copy-start | bytes 786436
  6.5 19.2 %copy-start.12 = (f32[256]{0:T(256)S(1)}, f32[256]{0:T(256)}, u32[]{:S(2)}) copy-start(f32[256]{0:T(256)} %param.16) | copy-start | bytes 3076
  6.5 223.8 %all-gather.3.cloned.1.call-start = ((), (), s32[]{:S(2)}) async-start(), calls=%async_computation.4 | async-start | bytes 8454144 | tf_op jit(solution)/shard_map/all_gather | solution.py:63
  7.9 18.2 %copy-start.10 = (bf16[256,32]{0,1:T(8,128)(2,1)S(1)}, bf16[256,32]{0,1:T(8,128)(2,1)}, u32[]{:S(2)}) copy-start(bf16[256,32]{0,1:T(8,128)(2,1)} %param.18) | copy-start | bytes 49156
  24.5 2.9 copy-start.5
  25.7 4.3 copy-start.11
  27.3 571.6 %all-gather.5.cloned.1.call-start = ((), (), s32[]{:S(2)}) async-start(), calls=%async_computation.5 | async-start | bytes 18874368 | tf_op jit(solution)/shard_map/all_gather | solution.py:96
  293.0 56.4 %copy-start.6 = (bf16[8,1024,128]{1,2,0:T(8,128)(2,1)S(1)}, bf16[8,1024,128]{1,2,0:T(8,128)(2,1)}, u32[]{:S(2)}) copy-start(bf16[8,1024,128]{1,2,0:T(8,128)(2,1)} %copy.183) | copy-start | bytes 6291460
  349.4 11.7 %copy-start.13 = (f32[128]{0:T(128)S(1)}, f32[128]{0:T(128)}, u32[]{:S(2)}) copy-start(f32[128]{0:T(128)} %param.20) | copy-start | bytes 1540
  360.4 2.4 copy-start.2
  360.4 1.5 copy-start.7
  361.9 0.9 copy-start.15
  397.1 1.5 copy-start.8
  398.6 0.9 copy-start.16
  612.2 9.4 %copy-start.9 = (bf16[128,128]{1,0:T(8,128)(2,1)S(1)}, bf16[128,128]{1,0:T(8,128)(2,1)}, u32[]{:S(2)}) copy-start(bf16[128,128]{1,0:T(8,128)(2,1)} %param.25) | copy-start | bytes 98308
  616.3 32.8 %all-to-all-start.3 = ((bf16[8,128,1024]{2,0,1:T(8,128)(2,1)}), bf16[8,128,1024]{2,0,1:T(8,128)(2,1)}, u32[]{:S(2)}, u32[]{:S(2)}) async-start(bf16[8,128,1024]{2,0,1:T(8,128)(2,1)} %copy.213), calls=%async_computation.3 | async-start | bytes 4194304 | tf_op jit(solution)/shard_map/all_to_all | solution.py:99
  652.5 0.7 copy-start.14
  653.2 1.6 copy-start.3
  653.2 2.8 copy-start.4
  653.2 2.8 copy-start.17
  656.0 4.8 copy-start.1
Sparse Core Ops, SparseCore 0:
  27.4 202.9 all-gather.2
  398.7 200.0 all-gather.4
where the time goes:
time: 670 us; the launch traced here: 668 us
  waiting for transfers between devices  387 us (58%)
  local copies, waits for them, and re-layouts  126 us (19%)
  blocking collectives  82.4 us (12%)
  matrix products  46.7 us (7%)
  between operations  13.8 us (2%)
    all_gather x1, waiting for transfers between devices, body(): lax.all_gather(right_alignment_projection, ('dap', 'bulk'), axis=1, tiled...  200 us
    all_gather x1, waiting for transfers between devices, body(): lax.all_gather(right_group, 'dap', axis=1, tiled=True)  162 us
    transpose x1, local copies, waits for them, and re-layouts, body(): triangle_products.transpose(0, 2, 1, 3)  56.4 us
    reshape x1, local copies, waits for them, and re-layouts, body(): triangle_products.astype(jnp.bfloat16)  51.1 us
    all_to_all x1, blocking collectives, body(): lax.all_to_all(left_chan, 'bulk', split_axis=0, concat_axis=1, tiled=True)  34.4 us
    all_to_all x1, blocking collectives, body(): lax.all_to_all(right_chan, 'bulk', split_axis=0, concat_axis=1, tiled=True)  31.5 us
    all_to_all x1, waiting for transfers between devices, body(): lax.all_to_all(mixed, 'bulk', split_axis=1, concat_axis=0, tiled=True)  24.6 us
    all_to_all x1, blocking collectives, body(): lax.all_to_all(stacked_relatives_tensor, 'bulk', split_axis=1, concat_axi...  16.5 us
  transfers between devices with their start and end apart: 3, of which 3 were waited for; matrix products, arithmetic and copies ran while one was open for 1% of the time, Pallas kernels for 0%

commit v1 on v0

v1 whole, which is shorter than its diff:
```python
import jax
import jax.numpy as jnp
from jax import lax
from jax.experimental import pallas as pl
from jax.experimental.pallas import tpu as pltpu
from jax.sharding import Mesh, PartitionSpec as P

ALL = ("dap", "chip", "core")


def standardize_features(values, gain, axis=-1):
    center = values - jnp.mean(values, axis=axis, keepdims=True)
    spread = jnp.mean(center * center, axis=axis, keepdims=True)
    return center / jnp.sqrt(spread + 1e-05) * gain


def opm_kernel(depth, right_ref, left_ref, weight_ref, out_ref, right_rows, mixer):
    groups, chips, _, width = right_ref.shape
    hidden = left_ref.shape[1]
    cols = right_rows.shape[0] // groups
    seqs = width // hidden
    channels = weight_ref.shape[1] // hidden

    @pl.when(pl.program_id(0) == 0)
    def _():
        for chip in range(chips):
            for group in range(groups):
                right_rows[group * cols : (group + 1) * cols, chip * width : (chip + 1) * width] = (
                    right_ref[group, chip, :cols, :]
                )

    expanded = jnp.dot(left_ref[...], weight_ref[...], preferred_element_type=jnp.float32) * (
        1.0 / depth
    )
    pair = left_ref.shape[0] // (chips * seqs)
    step = 16 // seqs
    for row in range(pair):
        for chip in range(chips):
            start = (row * chips + chip) * seqs
            for d in range(0, hidden, step):
                tile = jnp.concatenate(
                    [
                        expanded[start : start + seqs, k * channels : (k + 1) * channels]
                        for k in range(d, d + step)
                    ],
                    axis=0,
                )
                mixer[
                    chip * width + d * seqs : chip * width + (d + step) * seqs,
                    row * channels : (row + 1) * channels,
                ] = tile.astype(jnp.bfloat16)
    out = jnp.dot(right_rows[...], mixer[...], preferred_element_type=jnp.float32)
    for row in range(pair):
        out_ref[row] = out[:, row * channels : (row + 1) * channels].astype(out_ref.dtype)


def opm_rows(right, left, weight, depth, cols, dtype):
    groups, chips, rows_sent, width = right.shape
    rows, _, seqs, hidden = left.shape
    channels = weight.shape[1] // hidden
    flat = left.reshape(rows * chips * seqs, hidden)
    pair = 2
    return pl.pallas_call(
        lambda *refs: opm_kernel(depth, *refs),
        grid=(rows // pair,),
        in_specs=[
            pl.BlockSpec(right.shape, lambda i: (0, 0, 0, 0)),
            pl.BlockSpec((pair * chips * seqs, hidden), lambda i: (i, 0)),
            pl.BlockSpec(weight.shape, lambda i: (0, 0)),
        ],
        out_specs=pl.BlockSpec((pair, groups * cols, channels), lambda i: (i, 0, 0)),
        out_shape=jax.ShapeDtypeStruct((rows, groups * cols, channels), dtype),
        scratch_shapes=[
            pltpu.VMEM((groups * cols, chips * width), jnp.bfloat16),
            pltpu.VMEM((chips * width, pair * channels), jnp.bfloat16),
        ],
        compiler_params=pltpu.CompilerParams(vmem_limit_bytes=40 * 1024 * 1024),
        cost_estimate=pl.CostEstimate(
            flops=2 * rows * groups * cols * chips * width * channels,
            bytes_accessed=right.size * 2 + rows * groups * cols * channels * 4,
            transcendentals=0,
        ),
    )(right, flat, weight)


def gated_operand(pair_normed, proj_weight, gate_weight):
    linear_part = jnp.dot(pair_normed, proj_weight, preferred_element_type=jnp.float32)
    gate_part = jax.nn.sigmoid(
        jnp.dot(pair_normed, gate_weight, preferred_element_type=jnp.float32)
    )
    return (gate_part * linear_part).astype(jnp.bfloat16)


def body(
    stacked_relatives_tensor,
    couple_embedding,
    relatives_rescaler,
    averaged_lhs_weights,
    averaged_rhs_weights,
    mean_final_linear,
    couple_scale_vector,
    first_linear_map,
    first_sigmoid_factor,
    second_linear_map,
    second_sigmoid_factor,
    final_sigmoid_factor,
    trio_scale_vector,
    trio_final_linear,
):
    groups, chips, cores = (lax.axis_size(name) for name in ALL)
    devices = groups * chips * cores
    seqs, cols, features = stacked_relatives_tensor.shape
    hidden = averaged_lhs_weights.shape[1]
    depth = seqs * chips * cores
    rows, length, pair_width = couple_embedding.shape
    core = lax.axis_index("core")

    msa_normed = standardize_features(
        stacked_relatives_tensor.astype(jnp.float32), relatives_rescaler
    ).astype(jnp.bfloat16)
    left_msa = jnp.dot(
        msa_normed, averaged_lhs_weights, preferred_element_type=jnp.float32
    ).astype(jnp.bfloat16)
    right_msa = jnp.dot(
        msa_normed, averaged_rhs_weights, preferred_element_type=jnp.float32
    ).astype(jnp.bfloat16)
    right_send = right_msa.transpose(1, 2, 0).reshape(cols, hidden * seqs)
    left_send = left_msa.transpose(1, 0, 2).reshape(chips, cores * rows, seqs * hidden)
    payload = jnp.concatenate(
        [
            jnp.broadcast_to(right_send, (groups, chips) + right_send.shape),
            jnp.broadcast_to(left_send, (groups,) + left_send.shape),
        ],
        axis=2,
    ).reshape(groups * chips, cols + cores * rows, hidden * seqs)
    gathered = lax.all_to_all(payload, ("dap", "chip"), split_axis=0, concat_axis=0, tiled=True)
    gathered = gathered.reshape(groups, chips, cols + cores * rows, hidden * seqs)
    left_rows = lax.dynamic_index_in_dim(
        gathered[:, :, cols:], lax.axis_index("dap"), 0, keepdims=False
    )
    left_rows = (
        left_rows.reshape(chips, cores, rows, seqs, hidden)
        .transpose(1, 2, 0, 3, 4)
    )
    weight = mean_final_linear.reshape(hidden, hidden * pair_width)
    other_left = lax.dynamic_index_in_dim(left_rows, 1 - core, 0, keepdims=False)
    own_left = lax.dynamic_index_in_dim(left_rows, core, 0, keepdims=False)
    other_part = opm_rows(gathered, other_left, weight, depth, cols, jnp.bfloat16)
    arrived = lax.ppermute(other_part, "core", [(0, 1), (1, 0)])
    own_part = opm_rows(gathered, own_left, weight, depth, cols, jnp.float32)

    updated = (
        couple_embedding.astype(jnp.float32) + (own_part + arrived.astype(jnp.float32))
    ).astype(jnp.bfloat16)
    pair_normed = standardize_features(updated.astype(jnp.float32), couple_scale_vector).astype(
        jnp.bfloat16
    )
    left_tri = gated_operand(pair_normed, first_linear_map, first_sigmoid_factor)
    right_tri = gated_operand(pair_normed, second_linear_map, second_sigmoid_factor)
    gate = jax.nn.sigmoid(
        jnp.dot(pair_normed, final_sigmoid_factor, preferred_element_type=jnp.float32)
    )
    operands = jnp.concatenate(
        [left_tri.transpose(2, 0, 1), right_tri.transpose(2, 0, 1)], axis=1
    )
    operands = lax.all_to_all(operands, ALL, split_axis=0, concat_axis=0, tiled=True)
    left_full = operands[:, :rows].reshape(devices * rows, length)
    right_full = operands[:, rows:].reshape(devices * rows, length)
    mixed = lax.dot_general(
        left_full, right_full, (((1,), (1,)), ((), ())), preferred_element_type=jnp.float32
    ).astype(jnp.bfloat16)
    mixed_back = lax.all_to_all(
        mixed.reshape(devices, rows, length), ALL, split_axis=0, concat_axis=0, tiled=True
    )
    mixed_normed = standardize_features(
        mixed_back.astype(jnp.float32), trio_scale_vector[:, None, None], axis=0
    ).astype(jnp.bfloat16)
    output_term = lax.dot_general(
        mixed_normed, trio_final_linear, (((0,), (0,)), ((), ())), preferred_element_type=jnp.float32
    )
    return (updated.astype(jnp.float32) + gate * output_term).astype(jnp.bfloat16)


def solution(mesh):
    groups, lanes = mesh.shape["dap"], mesh.shape["bulk"]
    fine = Mesh(mesh.devices.reshape(groups, lanes // 2, 2), ALL)
    return jax.shard_map(
        body,
        mesh=fine,
        in_specs=(P(("chip", "core"), "dap", None), P(ALL, None, None)) + (P(),) * 12,
        out_specs=P(ALL, None, None),
        check_vma=False,
    )
```

time: 670 us -> 242 us (0.36)
  waiting for transfers between devices: 387 us -> 61.8 us
  local copies, waits for them, and re-layouts: 126 us -> 9.38 us
  matrix products: 46.7 us -> 24.3 us
  Pallas kernels: 0 us -> 19.3 us
  blocking collectives: 82.4 us -> 96 us
  between operations: 13.8 us -> 0.35 us
  starting transfers between devices: 5.42 us -> 15.9 us
  other arithmetic: 6.5 us -> 14.1 us
    all_gather x2 -> x0, waiting for transfers between devices: 362 us -> none  [the longest x1 200 us: body(): lax.all_gather(right_alignment_projection, ('dap', 'bulk'), axis=1, tiled...]
    transpose x1 -> x0, local copies, waits for them, and re-layouts: 56.4 us -> none  [body(): triangle_products.transpose(0, 2, 1, 3)]
    reshape x1 -> x4, local copies, waits for them, and re-layouts: 51.1 us -> 0.56 us  [the longest x1 0.18 us: body(): left_msa.transpose(1, 0, 2).reshape(chips, cores * rows, seqs * hidden)]
    all_to_all x1, waiting for transfers between devices: 24.6 us -> 61.8 us  [body(): lax.all_to_all(payload, ('dap', 'chip'), split_axis=0, concat_axis=0, til...]
    dot_general x6 -> x4, matrix products: 38.9 us -> 6.83 us  [the longest x1 2.51 us: body(): lax.dot_general(mixed_normed, trio_final_linear, (((0,), (0,)), ((), ()))...]
    pallas_call x0 -> x2, Pallas kernels: none -> 19.3 us  [opm_rows(): pl.pallas_call(lambda *refs: opm_kernel(depth, *refs), grid=(rows // pair...]
    all_to_all x3 -> x2, blocking collectives: 82.4 us -> 96.1 us  [the longest x1 57.4 us: body(): lax.all_to_all(operands, ALL, split_axis=0, concat_axis=0, tiled=True)]
    convert_element_type x8 -> x2, local copies, waits for them, and re-layouts: 10.4 us -> 0.24 us  [the longest x1 0.19 us: body(): left_msa = jnp.dot(msa_normed, averaged_lhs_weights, preferred_element_ty...]
  transfers between devices with their start and end apart: 3 -> 2, of which waited for: 3 -> 1; matrix products, arithmetic and copies ran while one was open for 1% -> 0% of each run, Pallas kernels for 0% -> 4%
where the time goes in v1:
time: 242 us; the launch traced here: 241 us
  blocking collectives  96 us (40%)
  waiting for transfers between devices  61.8 us (26%)
  matrix products  24.3 us (10%)
  Pallas kernels  19.3 us (8%)
  starting transfers between devices  15.9 us (7%)
  other arithmetic  14.1 us (6%)
  local copies, waits for them, and re-layouts  9.38 us (4%)
    all_to_all x1, waiting for transfers between devices, body(): lax.all_to_all(payload, ('dap', 'chip'), split_axis=0, concat_axis=0, til...  61.8 us
    all_to_all x1, blocking collectives, body(): lax.all_to_all(operands, ALL, split_axis=0, concat_axis=0, tiled=True)  57.4 us
    all_to_all x1, blocking collectives, body(): lax.all_to_all(mixed.reshape(devices, rows, length), ALL, split_axis=0, c...  38.7 us
    pallas_call x2, Pallas kernels, opm_rows(): pl.pallas_call(lambda *refs: opm_kernel(depth, *refs), grid=(rows // pair...  19.3 us
    all_to_all x1, starting transfers between devices, body(): lax.all_to_all(payload, ('dap', 'chip'), split_axis=0, concat_axis=0, til...  12.3 us
    dot_general x2, matrix products, gated_operand(): jnp.dot(pair_normed, proj_weight, preferred_element_type=jnp.float32)  7.52 us
    concatenate x1, local copies, waits for them, and re-layouts, body(): jnp.concatenate([left_tri.transpose(2, 0, 1), right_tri.transpose(2, 0, 1...  6.81 us
    dot_general x1, matrix products, body(): jnp.dot(pair_normed, final_sigmoid_factor, preferred_element_type=jnp.flo...  5.26 us
  transfers between devices with their start and end apart: 2, of which 1 were waited for; matrix products, arithmetic and copies ran while one was open for 0% of the time, Pallas kernels for 4%

profile of v1, /device:TPU:1, one launch (start us, length us, event | category | flops | bytes accessed | tf_op | source)
XLA Modules:
  0.0 241.3 jit_solution(16761558405942922320)
XLA Ops:
  0.0 1.3 convert_reduce_fusion.2
  1.3 1.4 fusion.20
  2.7 1.4 fusion.22
  5.1 1.0 fusion.18
  7.1 2.6 %pad_maximum_fusion = bf16[8,8,144,256]{3,2,1,0:T(8,128)(2,1)} fusion(bf16[8,8,16,256]{3,2,1,0:T(8,128)(2,1)S(1)} %broadcast_in_dim.5, bf16[8,8,128,256]{3,2,1,0:T(8,128)(2,1)S(1)} %broadcast_in_dim.4), kind=kLoop, calls=%fused_computation.9 | loop fusion | flops 9437184 | bytes 9437184 | tf_op jit(solution)/shard_map/concatenate | solution.py:129
  9.7 12.3 %all-to-all-start = ((bf16[64,144,256]{2,1,0:T(8,128)(2,1)}), bf16[64,144,256]{2,1,0:T(8,128)(2,1)}, u32[]{:S(2)}, u32[]{:S(2)}) async-start(bf16[64,144,256]{2,1,0:T(8,128)(2,1)} %bitcast.61), calls=%async_computation | async-start | bytes 9437184 | tf_op jit(solution)/shard_map/all_to_all | solution.py:136
  22.2 61.8 %all-to-all-done = bf16[64,144,256]{2,1,0:T(8,128)(2,1)} async-done(((bf16[64,144,256]{2,1,0:T(8,128)(2,1)}), bf16[64,144,256]{2,1,0:T(8,128)(2,1)}, u32[]{:S(2)}, u32[]{:S(2)}) %all-to-all-start) | async-done | bytes 4718624 | tf_op jit(solution)/shard_map/all_to_all | solution.py:136
  84.0 1.1 slice.12
  85.4 9.6 %shard_map.137 = bf16[8,1024,128]{2,1,0:T(8,128)(2,1)S(1)} custom-call(bf16[8,8,144,256]{3,2,1,0:T(8,128)(2,1)} %bitcast.6.refs_0_, bf16[512,32]{1,0:T(8,128)(2,1)S(1)} %bitcast.60, bf16[32,4096]{1,0:T(8,128)(2,1)S(1)} %reshape.81.refs_2_), custom_call_target="tpu_custom_call" | custom-call | flops 4294967296 | bytes 8912896 | tf_op jit(solution)/shard_map/pallas_call | solution.py:63
  94.9 3.6 %collective-permute-start = (bf16[8,1024,128]{2,1,0:T(8,128)(2,1)S(1)}, bf16[8,1024,128]{2,1,0:T(8,128)(2,1)S(1)}, u32[]{:S(2)}, u32[]{:S(2)}) collective-permute-start(bf16[8,1024,128]{2,1,0:T(8,128)(2,1)S(1)} %shard_map.137), channel_id=1, source_target_pairs={{0,1},{1,0},{2,3},{3,2},{4,5},{5,4},{6,7},{7,6},{8,9},{9,8},{10,11... | collective-permute-start | bytes 6291464 | tf_op jit(solution)/shard_map/ppermute | solution.py:149
  98.6 9.7 %shard_map.136 = f32[8,1024,128]{2,1,0:T(8,128)S(1)} custom-call(bf16[8,8,144,256]{3,2,1,0:T(8,128)(2,1)} %bitcast.6.refs_0_, bf16[512,32]{1,0:T(8,128)(2,1)S(1)} %bitcast.59, bf16[32,4096]{1,0:T(8,128)(2,1)S(1)} %reshape.81.refs_2_), custom_call_target="tpu_custom_call" | custom-call | flops 4294967296 | bytes 8912896 | tf_op jit(solution)/shard_map/pallas_call | solution.py:63
  108.4 1.2 convert_reduce_fusion
  109.5 2.4 fusion.4
  112.0 2.4 fusion.28
  114.4 2.4 fusion.25
  116.7 3.8 %fusion.14 = bf16[128,8,1024]{0,2,1:T(8,128)(2,1)S(1)} fusion(f32[8,1024,128]{2,1,0:T(8,128)S(1)} %fusion.28, bf16[128,128]{1,0:T(8,128)(2,1)S(1)} %copy-done.7, bf16[8,1024,128]{2,1,0:T(8,128)(2,1)S(1)} %get-tuple-element.6, f32[128]{0:T(128)S(1)} %copy-done.10, f32[8,1024]{1,0:T(8,128)S(1)} %add_sqrt_fusion.1, f32[8,1024]{1,0:T(8,128)S(1)} %broadcast_multiply_fusion.1), kind=kOutput, calls=%fused_computation.27 | convolution fusion | flops 278921216 | bytes 8487424 | tf_op jit(solution)/shard_map/dot_general | solution.py:87
  120.5 3.8 %fusion.15 = bf16[128,8,1024]{0,2,1:T(8,128)(2,1)S(1)} fusion(f32[8,1024,128]{2,1,0:T(8,128)S(1)} %fusion.25, bf16[128,128]{1,0:T(8,128)(2,1)S(1)} %copy-done.8, bf16[8,1024,128]{2,1,0:T(8,128)(2,1)S(1)} %get-tuple-element.6, f32[128]{0:T(128)S(1)} %copy-done.10, f32[8,1024]{1,0:T(8,128)S(1)} %add_sqrt_fusion.1, f32[8,1024]{1,0:T(8,128)S(1)} %broadcast_multiply_fusion.1), kind=kOutput, calls=%fused_computation.28 | convolution fusion | flops 278921216 | bytes 8487424 | tf_op jit(solution)/shard_map/dot_general | solution.py:87
  124.3 2.3 pad_maximum_fusion.1
  126.6 6.8 %copy.30 = bf16[128,16,1024]{2,1,0:T(8,128)(2,1)} copy(bf16[128,16,1024]{0,2,1:T(8,128)(2,1)} %pad_maximum_fusion.1) | data formatting | bytes 8388608 | tf_op jit(solution)/shard_map/concatenate | solution.py:163
  133.4 57.4 %all_to_all.15 = bf16[128,16,1024]{2,1,0:T(8,128)(2,1)S(1)} all-to-all(bf16[128,16,1024]{2,1,0:T(8,128)(2,1)} %copy.30), channel_id=1, replica_groups=mesh['dap'=8,'chip'=8,'core'=2] {'dap','chip','core'}, dimensions={0} | all-to-all | bytes 8388608 | tf_op jit(solution)/shard_map/all_to_all | solution.py:166
  190.8 2.4 convert_bitcast_fusion
  193.2 38.7 %all_to_all.16 = bf16[128,8,1024]{2,1,0:T(8,128)(2,1)S(1)} all-to-all(bf16[128,8,1024]{2,1,0:T(8,128)(2,1)S(1)} %convert_bitcast_fusion), channel_id=1, replica_groups=mesh['dap'=8,'chip'=8,'core'=2] {'dap','chip','core'}, dimensions={0} | all-to-all | bytes 4194304 | tf_op jit(solution)/shard_map/all_to_all | solution.py:172
  233.5 2.5 %fusion.12 = f32[8,1024,128]{2,1,0:T(8,128)S(1)} fusion(bf16[128,8,1024]{2,1,0:T(8,128)(2,1)S(1)} %fusion.9, bf16[128,128]{1,0:T(8,128)(2,1)S(1)} %copy-done.4), kind=kOutput, calls=%fused_computation.24 | convolution fusion | flops 268435456 | bytes 6324224 | tf_op jit(solution)/shard_map/dot_general | solution.py:178
  236.0 5.3 %fusion.10 = bf16[8,1024,128]{2,1,0:T(8,128)(2,1)} fusion(bf16[8,1024,128]{2,1,0:T(8,128)(2,1)S(1)} %get-tuple-element.6, f32[8,1024,128]{2,1,0:T(8,128)S(1)} %fusion.12, bf16[128,128]{1,0:T(8,128)(2,1)S(1)} %copy-done.9, f32[128]{0:T(128)S(1)} %copy-done.10, f32[8,1024]{1,0:T(8,128)S(1)} %add_sqrt_fusion.1, f32[8,1024]{1,0:T(8,128)S(1)} %broadcast_multiply_fusion.1), kind=kOutput, calls=%fused_computation.16 | convolution fusion | flops 281018368 | bytes 8487424 | tf_op jit(solution)/shard_map/dot_general | solution.py:161
  (45 shorter events, 4.1 us)
Async XLA Ops:
  0.0 111.9 %copy-start = (bf16[128,128]{1,0:T(8,128)(2,1)S(1)}, bf16[128,128]{1,0:T(8,128)(2,1)}, u32[]{:S(2)}) copy-start(bf16[128,128]{1,0:T(8,128)(2,1)} %param.22) | copy-start | bytes 98308
  9.7 12.3 %copy-start.3 = (bf16[1024,128]{1,0:T(8,128)(2,1)S(1)}, bf16[1024,128]{1,0:T(8,128)(2,1)}, u32[]{:S(2)}) copy-start(bf16[1024,128]{1,0:T(8,128)(2,1)} %param.19) | copy-start | bytes 786436
  9.7 74.3 %all-to-all-start = ((bf16[64,144,256]{2,1,0:T(8,128)(2,1)}), bf16[64,144,256]{2,1,0:T(8,128)(2,1)}, u32[]{:S(2)}, u32[]{:S(2)}) async-start(bf16[64,144,256]{2,1,0:T(8,128)(2,1)} %bitcast.61), calls=%async_computation | async-start | bytes 9437184 | tf_op jit(solution)/shard_map/all_to_all | solution.py:136
  94.9 13.4 %collective-permute-start = (bf16[8,1024,128]{2,1,0:T(8,128)(2,1)S(1)}, bf16[8,1024,128]{2,1,0:T(8,128)(2,1)S(1)}, u32[]{:S(2)}, u32[]{:S(2)}) collective-permute-start(bf16[8,1024,128]{2,1,0:T(8,128)(2,1)S(1)} %shard_map.137), channel_id=1, source_target_pairs={{0,1},{1,0},{2,3},{3,2},{4,5},{5,4},{6,7},{7,6},{8,9},{9,8},{10,11... | collective-permute-start | bytes 6291464 | tf_op jit(solution)/shard_map/ppermute | solution.py:149
  98.6 9.8 %copy-start.2 = (bf16[8,1024,128]{2,1,0:T(8,128)(2,1)S(1)}, bf16[8,1024,128]{2,1,0:T(8,128)(2,1)}, u32[]{:S(2)}) copy-start(bf16[8,1024,128]{2,1,0:T(8,128)(2,1)} %param.15) | copy-start | bytes 6291460
  108.3 3.6 %copy-start.10 = (f32[128]{0:T(128)S(1)}, f32[128]{0:T(128)}, u32[]{:S(2)}) copy-start(f32[128]{0:T(128)} %param.20) | copy-start | bytes 1540
  112.0 2.4 copy-start.6
  114.3 2.4 copy-start.7
  116.7 3.8 %copy-start.8 = (bf16[128,128]{1,0:T(8,128)(2,1)S(1)}, bf16[128,128]{1,0:T(8,128)(2,1)}, u32[]{:S(2)}) copy-start(bf16[128,128]{1,0:T(8,128)(2,1)} %param.23) | copy-start | bytes 98308
  193.1 39.7 %copy-start.5 = (f32[128]{0:T(128)S(1)}, f32[128]{0:T(128)}, u32[]{:S(2)}) copy-start(f32[128]{0:T(128)} %param.26) | copy-start | bytes 1540
  231.8 1.7 copy-start.4
  233.5 2.5 %copy-start.9 = (bf16[128,128]{1,0:T(8,128)(2,1)S(1)}, bf16[128,128]{1,0:T(8,128)(2,1)}, u32[]{:S(2)}) copy-start(bf16[128,128]{1,0:T(8,128)(2,1)} %param.25) | copy-start | bytes 98308
  236.0 5.3 %copy-start.1 = (bf16[128,128]{1,0:T(8,128)(2,1)S(1)}, bf16[128,128]{1,0:T(8,128)(2,1)}, u32[]{:S(2)}) copy-start(bf16[128,128]{1,0:T(8,128)(2,1)} %param.22) | copy-start | bytes 98308

commit v2 on v1

v2 whole, which is shorter than its diff:
```python
import functools

import jax
import jax.numpy as jnp
from jax import lax
from jax.experimental import pallas as pl
from jax.experimental.pallas import tpu as pltpu
from jax.sharding import Mesh, PartitionSpec as P

ALL = ("dap", "chip", "core")


def standardize_features(values, gain, axis=-1):
    center = values - jnp.mean(values, axis=axis, keepdims=True)
    spread = jnp.mean(center * center, axis=axis, keepdims=True)
    return center / jnp.sqrt(spread + 1e-05) * gain


MIB = 1024 * 1024


def ones_where(condition):
    return condition.astype(jnp.float32).astype(jnp.bfloat16)


def iota(shape, axis):
    return lax.broadcasted_iota(jnp.int32, shape, axis)


def msa_kernel(msa_ref, gain_ref, left_ref, right_ref, send_ref, block, sems):
    seqs, cols, features = msa_ref.shape
    hidden = left_ref.shape[0]
    width = hidden * seqs
    chips, rows_sent, _ = block.shape
    left_rows = rows_sent - cols
    pairs = width // hidden
    spread = ones_where(iota((hidden, width), 1) // seqs == iota((hidden, width), 0))
    right_copies = lax.dot_general(
        right_ref[...], spread, (((0,), (0,)), ((), ())), preferred_element_type=jnp.float32
    )
    right_lane = iota(right_copies.shape, 1) % seqs
    tiled = ones_where(iota((hidden, width), 1) % hidden == iota((hidden, width), 0))
    left_copies = lax.dot_general(
        left_ref[...], tiled, (((0,), (0,)), ((), ())), preferred_element_type=jnp.float32
    ).astype(jnp.bfloat16)
    own_lane = iota((cols, width), 1) // hidden == iota((cols, width), 0) // 2 % pairs
    place = (chips * left_rows, cols)
    target, source = iota(place, 0), iota(place, 1)
    same_pair = (target // left_rows == source // left_rows) & (
        target // seqs % 2 == source % 2
    )
    right = jnp.zeros((cols, width), jnp.float32)
    left = jnp.zeros((chips * left_rows, width), jnp.float32)
    for s in range(seqs):
        normed = standardize_features(msa_ref[s].astype(jnp.float32), gain_ref[...]).astype(
            jnp.bfloat16
        )
        right = right + jnp.dot(
            normed,
            jnp.where(right_lane == s, right_copies, 0.0).astype(jnp.bfloat16),
            preferred_element_type=jnp.float32,
        )
        products = jnp.dot(normed, left_copies, preferred_element_type=jnp.float32)
        left = left + jnp.dot(
            ones_where(same_pair & (target % seqs == s)),
            jnp.where(own_lane, products, 0.0).astype(jnp.bfloat16),
            preferred_element_type=jnp.float32,
        )
    right = right.astype(jnp.bfloat16)
    left = left.astype(jnp.bfloat16)
    for chip in range(chips):
        block[chip, :cols, :] = right
        block[chip, cols:, :] = left[chip * left_rows : (chip + 1) * left_rows]
    copies = [
        pltpu.make_async_copy(block, send_ref.at[pl.ds(group * chips, chips)], sems.at[group])
        for group in range(send_ref.shape[0] // chips)
    ]
    for copy in copies:
        copy.start()
    for copy in copies:
        copy.wait()


def whole(shape):
    return pl.BlockSpec(shape, lambda *_: (0,) * len(shape))


def msa_payload(msa, gain, left, right, groups, chips, left_rows):
    seqs, cols, features = msa.shape
    width = seqs * left.shape[1]
    operands = (msa, gain.reshape(1, features), left.T, right.T)
    return pl.pallas_call(
        msa_kernel,
        grid=(1,),
        in_specs=[whole(operand.shape) for operand in operands],
        out_specs=pl.BlockSpec(memory_space=pl.ANY),
        out_shape=jax.ShapeDtypeStruct((groups * chips, cols + left_rows, width), jnp.bfloat16),
        scratch_shapes=[
            pltpu.VMEM((chips, cols + left_rows, width), jnp.bfloat16),
            pltpu.SemaphoreType.DMA((groups,)),
        ],
        compiler_params=pltpu.CompilerParams(vmem_limit_bytes=58 * MIB),
    )(*operands)


def opm_kernel(
    own, place_ref, gathered_ref, weight_ref, out_ref, right_rows, left_block, left_rows, mixer, sems
):
    groups, cols, _ = right_rows.shape
    _, chips, _, width = gathered_ref.shape
    pairs, stacked, hidden = left_rows.shape
    seqs = width // hidden
    channels = weight_ref.shape[1] // hidden
    here = out_ref.shape[0] // 2
    copies = [
        pltpu.make_async_copy(
            gathered_ref.at[:, chip, pl.ds(0, cols), :],
            right_rows.at[:, :, pl.ds(chip * width, width)],
            sems.at[chip],
        )
        for chip in range(chips)
    ]
    left_copy = pltpu.make_async_copy(
        gathered_ref.at[place_ref[0], :, pl.ds(cols, 2 * seqs), :], left_block, sems.at[chips]
    )

    @pl.when(pl.program_id(0) == 0)
    def _():
        left_copy.start()
        for copy in copies:
            copy.start()
        left_copy.wait()
        half = place_ref[1] if own else 1 - place_ref[1]
        half = pl.multiple_of(half * (pairs * hidden), pairs * hidden)
        left = left_block[:, :, pl.ds(half, pairs * hidden)].reshape(stacked, pairs * hidden)
        for pair in range(pairs):
            left_rows[pair] = left[:, pair * hidden : (pair + 1) * hidden]

    step = 16 // seqs
    for pair in range(here):
        expanded = jnp.dot(
            left_rows[pl.program_id(0) * here + pair],
            weight_ref[...],
            preferred_element_type=jnp.float32,
        )
        for chip in range(chips):
            for row in range(2):
                start = (chip * 2 + row) * seqs
                column = (pair * 2 + row) * channels
                for d in range(0, hidden, step):
                    tile = jnp.concatenate(
                        [
                            expanded[start : start + seqs, k * channels : (k + 1) * channels]
                            for k in range(d, d + step)
                        ],
                        axis=0,
                    )
                    mixer[
                        chip * width + d * seqs : chip * width + (d + step) * seqs,
                        column : column + channels,
                    ] = tile.astype(jnp.bfloat16)

    @pl.when(pl.program_id(0) == 0)
    def _():
        for copy in copies:
            copy.wait()

    out = jnp.dot(
        right_rows[...].reshape(groups * cols, chips * width),
        mixer[...],
        preferred_element_type=jnp.float32,
    )
    for row in range(out_ref.shape[0]):
        out_ref[row] = out[:, row * channels : (row + 1) * channels].astype(out_ref.dtype)


def opm_rows(own, place, gathered, weight, cols, rows, step_rows=4):
    groups, chips, rows_sent, width = gathered.shape
    hidden = weight.shape[0]
    channels = weight.shape[1] // hidden
    seqs = width // hidden
    return pl.pallas_call(
        functools.partial(opm_kernel, own),
        grid=(rows // step_rows,),
        in_specs=[
            pl.BlockSpec(memory_space=pltpu.SMEM),
            pl.BlockSpec(memory_space=pl.ANY),
            whole(weight.shape),
        ],
        out_specs=pl.BlockSpec((step_rows, groups * cols, channels), lambda i: (i, 0, 0)),
        out_shape=jax.ShapeDtypeStruct((rows, groups * cols, channels), jnp.bfloat16),
        scratch_shapes=[
            pltpu.VMEM((groups, cols, chips * width), jnp.bfloat16),
            pltpu.VMEM((chips, 2 * seqs, width), jnp.bfloat16),
            pltpu.VMEM((rows // 2, chips * 2 * seqs, hidden), jnp.bfloat16),
            pltpu.VMEM((chips * width, step_rows * channels), jnp.bfloat16),
            pltpu.SemaphoreType.DMA((chips + 1,)),
        ],
        compiler_params=pltpu.CompilerParams(vmem_limit_bytes=24 * MIB),
        cost_estimate=pl.CostEstimate(
            flops=2 * rows * groups * cols * chips * width * channels,
            bytes_accessed=gathered.size * 2 + rows * groups * cols * channels * 2,
            transcendentals=0,
        ),
    )(place, gathered, weight)


def half_sigmoid(values):
    return 0.5 * jnp.tanh(0.5 * values) + 0.5


def pair_kernel(
    scale, pair_ref, own_ref, arrived_ref, gain_ref, *rest
):
    *weight_refs, updated_ref, normed_ref, send_ref, rows_buf, weight_buf = rest
    rows, cols, width = pair_ref.shape
    channels = weight_refs[0].shape[1]

    @pl.when(pl.program_id(0) == 0)
    def _():
        for k, weight_ref in enumerate(weight_refs):
            weight_buf[k * channels : (k + 1) * channels, :] = weight_ref[...].T

    for row in range(rows):
        updated = (
            pair_ref[row].astype(jnp.float32)
            + (own_ref[row].astype(jnp.float32) + arrived_ref[row].astype(jnp.float32)) * scale
        ).astype(jnp.bfloat16)
        updated_ref[row] = updated
        normed = standardize_features(updated.astype(jnp.float32), gain_ref[...]).astype(
            jnp.bfloat16
        )
        normed_ref[row] = normed
        products = lax.dot_general(
            weight_buf[...], normed, (((1,), (1,)), ((), ())), preferred_element_type=jnp.float32
        )
        for side in range(2):
            start = 2 * side * channels
            gated = products[start : start + channels] * half_sigmoid(
                products[start + channels : start + 2 * channels]
            )
            for lane in range(0, cols, 128):
                rows_buf[lane // 128, pl.ds(side * rows + row, channels, stride=2 * rows), :] = (
                    gated[:, lane : lane + 128]
                )
    for lane in range(0, cols, 128):
        send_ref[:, :, lane : lane + 128] = (
            rows_buf[lane // 128].reshape(channels, 2 * rows, 128).astype(jnp.bfloat16)
        )


def pair_operands(pair, own, arrived, gain, weights, scale):
    rows, length, width = pair.shape
    channels = weights[0].shape[1]
    cols = 256
    block = pl.BlockSpec((rows, cols, width), lambda i: (0, i, 0))
    return pl.pallas_call(
        functools.partial(pair_kernel, scale),
        grid=(length // cols,),
        in_specs=[
            block,
            block,
            block,
            pl.BlockSpec((1, width), lambda i: (0, 0)),
        ]
        + [whole(weight.shape) for weight in weights],
        out_specs=[
            block,
            block,
            pl.BlockSpec((channels, 2 * rows, cols), lambda i: (0, 0, i)),
        ],
        out_shape=[
            jax.ShapeDtypeStruct(pair.shape, jnp.bfloat16),
            jax.ShapeDtypeStruct(pair.shape, jnp.bfloat16),
            jax.ShapeDtypeStruct((channels, 2 * rows, length), jnp.bfloat16),
        ],
        scratch_shapes=[
            pltpu.VMEM((cols // 128, channels * 2 * rows, 128), jnp.float32),
            pltpu.VMEM((len(weights) * channels, width), jnp.bfloat16),
        ],
        compiler_params=pltpu.CompilerParams(vmem_limit_bytes=18 * MIB),
        cost_estimate=pl.CostEstimate(
            flops=8 * rows * length * width * channels,
            bytes_accessed=rows * length * width * 18,
            transcendentals=2 * rows * length * channels,
        ),
    )(pair, own, arrived, gain.reshape(1, width), *weights)


def result_kernel(mixed_ref, updated_ref, gate_ref, gain_ref, weight_ref, out_ref, rows_buf):
    channels, rows, cols = mixed_ref.shape
    for lane in range(0, cols, 128):
        values = mixed_ref[:, :, lane : lane + 128].astype(jnp.float32)
        center = values - jnp.mean(values, axis=0, keepdims=True)
        spread = jnp.mean(center * center, axis=0, keepdims=True)
        scaled = center * (1.0 / jnp.sqrt(spread + 1e-05))
        rows_buf[...] = scaled.reshape(channels * rows, 128)
        for row in range(rows):
            normed = (rows_buf[pl.ds(row, channels, stride=rows), :] * gain_ref[...]).astype(
                jnp.bfloat16
            )
            term = lax.dot_general(
                normed, weight_ref[...], (((0,), (0,)), ((), ())), preferred_element_type=jnp.float32
            )
            out_ref[row, lane : lane + 128, :] = (
                updated_ref[row, lane : lane + 128, :].astype(jnp.float32)
                + gate_ref[row, lane : lane + 128, :].astype(jnp.float32) * term
            ).astype(jnp.bfloat16)


def result_rows(mixed, updated, gate, gain, weight):
    channels, rows, length = mixed.shape
    width = weight.shape[1]
    cols = 256
    block = pl.BlockSpec((rows, cols, width), lambda i: (0, i, 0))
    return pl.pallas_call(
        result_kernel,
        grid=(length // cols,),
        in_specs=[
            pl.BlockSpec((channels, rows, cols), lambda i: (0, 0, i)),
            block,
            block,
            pl.BlockSpec((channels, 1), lambda i: (0, 0)),
            pl.BlockSpec(weight.shape, lambda i: (0, 0)),
        ],
        out_specs=block,
        out_shape=jax.ShapeDtypeStruct((rows, length, width), jnp.bfloat16),
        scratch_shapes=[pltpu.VMEM((channels * rows, 128), jnp.float32)],
        compiler_params=pltpu.CompilerParams(vmem_limit_bytes=14 * MIB),
        cost_estimate=pl.CostEstimate(
            flops=2 * rows * length * width * channels,
            bytes_accessed=rows * length * width * 10,
            transcendentals=0,
        ),
    )(mixed, updated, gate, gain.reshape(channels, 1), weight)


def body(
    stacked_relatives_tensor,
    couple_embedding,
    relatives_rescaler,
    averaged_lhs_weights,
    averaged_rhs_weights,
    mean_final_linear,
    couple_scale_vector,
    first_linear_map,
    first_sigmoid_factor,
    second_linear_map,
    second_sigmoid_factor,
    final_sigmoid_factor,
    trio_scale_vector,
    trio_final_linear,
):
    groups, chips, cores = (lax.axis_size(name) for name in ALL)
    devices = groups * chips * cores
    seqs, cols, features = stacked_relatives_tensor.shape
    hidden = averaged_lhs_weights.shape[1]
    depth = seqs * chips * cores
    rows, length, pair_width = couple_embedding.shape

    payload = msa_payload(
        stacked_relatives_tensor,
        relatives_rescaler,
        averaged_lhs_weights,
        averaged_rhs_weights,
        groups,
        chips,
        cores * rows,
    )
    gathered = lax.all_to_all(payload, ("dap", "chip"), split_axis=0, concat_axis=0, tiled=True)
    gathered = gathered.reshape(groups, chips, cols + cores * rows, hidden * seqs)
    weight = mean_final_linear.reshape(hidden, hidden * pair_width)
    place = jnp.stack([lax.axis_index("dap"), lax.axis_index("core")])
    other_part = opm_rows(False, place, gathered, weight, cols, rows)
    arrived = lax.ppermute(other_part, "core", [(0, 1), (1, 0)])
    own_part = opm_rows(True, place, gathered, weight, cols, rows)
    tri_weights = (
        first_linear_map, first_sigmoid_factor, second_linear_map, second_sigmoid_factor
    )
    updated, pair_normed, operands = pair_operands(
        couple_embedding, own_part, arrived, couple_scale_vector, tri_weights, 1.0 / depth
    )
    gate = jax.nn.sigmoid(
        jnp.dot(pair_normed, final_sigmoid_factor, preferred_element_type=jnp.float32)
    ).astype(jnp.bfloat16)
    operands = lax.all_to_all(operands, ALL, split_axis=0, concat_axis=0, tiled=True)
    left_full = operands[:, :rows].reshape(devices * rows, length)
    right_full = operands[:, rows:].reshape(devices * rows, length)
    mixed = lax.dot_general(
        left_full, right_full, (((1,), (1,)), ((), ())), preferred_element_type=jnp.float32
    ).astype(jnp.bfloat16)
    mixed_back = lax.all_to_all(
        mixed.reshape(devices, rows, length), ALL, split_axis=0, concat_axis=0, tiled=True
    )
    return result_rows(mixed_back, updated, gate, trio_scale_vector, trio_final_linear)


def solution(mesh):
    groups, lanes = mesh.shape["dap"], mesh.shape["bulk"]
    fine = Mesh(mesh.devices.reshape(groups, lanes // 2, 2), ALL)
    return jax.shard_map(
        body,
        mesh=fine,
        in_specs=(P(("chip", "core"), "dap", None), P(ALL, None, None)) + (P(),) * 12,
        out_specs=P(ALL, None, None),
        check_vma=False,
    )
```

time: 242 us -> 218 us (0.901)
  blocking collectives: 96 us -> 57.2 us
  waiting for transfers between devices: 61.8 us -> 88.2 us
  Pallas kernels: 19.3 us -> 35.9 us
  matrix products: 24.3 us -> 7.86 us
  other arithmetic: 14.1 us -> 0.08 us
  starting transfers between devices: 15.9 us -> 23.9 us
  local copies, waits for them, and re-layouts: 9.38 us -> 4.81 us
    all_to_all x1 -> x0, blocking collectives: 38.7 us -> none  [body(): lax.all_to_all(mixed.reshape(devices, rows, length), ALL, split_axis=0, c...]
    all_to_all x0 -> x1, waiting for transfers between devices: none -> 26.4 us  [body(): lax.all_to_all(mixed.reshape(devices, rows, length), ALL, split_axis=0, c...]
    dot_general x7 -> x0, matrix products: 16.7 us -> none  [the longest x2 7.52 us: gated_operand(): jnp.dot(pair_normed, proj_weight, preferred_element_type=jnp.float32)]
    pallas_call x2 -> x5, Pallas kernels: 19.3 us -> 35.9 us  [the longest x2 16.3 us: opm_rows(): pl.pallas_call(functools.partial(opm_kernel, own), grid=(rows // step_row...]
    all_to_all x0 -> x1, starting transfers between devices: none -> 8.16 us  [body(): lax.all_to_all(mixed.reshape(devices, rows, length), ALL, split_axis=0, c...]
    reduce_sum x6 -> x0, other arithmetic: 7.16 us -> none  [the longest x3 4.37 us: standardize_features(): spread = jnp.mean(center * center, axis=axis, keepdims=True)]
    concatenate x1 -> x0, local copies, waits for them, and re-layouts: 6.81 us -> none  [body(): jnp.concatenate([left_tri.transpose(2, 0, 1), right_tri.transpose(2, 0, 1...]
    concatenate x2 -> x0, other arithmetic: 4.85 us -> none  [the longest x1 2.56 us: body(): jnp.concatenate([jnp.broadcast_to(right_send, (groups, chips) + right_sen...]
  transfers between devices with their start and end apart: 2 -> 3, of which waited for: 1 -> 2; matrix products, arithmetic and copies ran while one was open for 0% -> 2% of each run, Pallas kernels for 4% -> 4%
where the time goes in v2:
time: 218 us
  waiting for transfers between devices  88.2 us (40%)
  blocking collectives  57.2 us (26%)
  Pallas kernels  35.9 us (16%)
  starting transfers between devices  23.9 us (11%)
  matrix products  7.86 us (4%)
  local copies, waits for them, and re-layouts  4.81 us (2%)
    all_to_all x1, waiting for transfers between devices, body(): lax.all_to_all(payload, ('dap', 'chip'), split_axis=0, concat_axis=0, til...  61.7 us
    all_to_all x1, blocking collectives, body(): lax.all_to_all(operands, ALL, split_axis=0, concat_axis=0, tiled=True)  57.2 us
    all_to_all x1, waiting for transfers between devices, body(): lax.all_to_all(mixed.reshape(devices, rows, length), ALL, split_axis=0, c...  26.4 us
    pallas_call x2, Pallas kernels, opm_rows(): pl.pallas_call(functools.partial(opm_kernel, own), grid=(rows // step_row...  16.3 us
    all_to_all x1, starting transfers between devices, body(): lax.all_to_all(payload, ('dap', 'chip'), split_axis=0, concat_axis=0, til...  12.3 us
    pallas_call x1, Pallas kernels, pair_operands(): pl.pallas_call(functools.partial(pair_kernel, scale), grid=(length // col...  9.38 us
    all_to_all x1, starting transfers between devices, body(): lax.all_to_all(mixed.reshape(devices, rows, length), ALL, split_axis=0, c...  8.16 us
    pallas_call x1, Pallas kernels, result_rows(): pl.pallas_call(result_kernel, grid=(length // cols,), in_specs=[pl.BlockS...  5.44 us
  transfers between devices with their start and end apart: 3, of which 2 were waited for; matrix products, arithmetic and copies ran while one was open for 2% of the time, Pallas kernels for 4%

profile of v2, /device:TPU:1, one launch (start us, length us, event | category | flops | bytes accessed | tf_op | source)
XLA Modules:
  0.0 218.1 jit_solution(10365998185501867720)
XLA Ops:
  0.0 4.7 %shard_map.136 = bf16[64,144,256]{2,1,0:T(8,128)(2,1)} custom-call(bf16[8,128,256]{2,1,0:T(8,128)(2,1)} %msa_ref.1, f32[1,256]{1,0:T(1,128)} %bitcast.27, bf16[32,256]{1,0:T(8,128)(2,1)} %bitcast.25, bf16[32,256]{1,0:T(8,128)(2,1)} %bitcast.26), custom_call_target="tpu_custom_call" | custom-call | tf_op jit(solution)/shard_map/pallas_call | solution.py:92
  4.7 0.0 copy-start.12
  4.7 12.3 %all-to-all-start = ((bf16[64,144,256]{2,1,0:T(8,128)(2,1)}), bf16[64,144,256]{2,1,0:T(8,128)(2,1)}, u32[]{:S(2)}, u32[]{:S(2)}) async-start(bf16[64,144,256]{2,1,0:T(8,128)(2,1)} %shard_map.136), calls=%async_computation | async-start | bytes 9437184 | tf_op jit(solution)/shard_map/all_to_all | solution.py:370
  17.1 0.1 reshape.26.weight_ref
  17.2 0.1 pad_add_fusion.place_ref
  17.3 61.7 %all-to-all-done = bf16[64,144,256]{2,1,0:T(8,128)(2,1)} async-done(((bf16[64,144,256]{2,1,0:T(8,128)(2,1)}), bf16[64,144,256]{2,1,0:T(8,128)(2,1)}, u32[]{:S(2)}, u32[]{:S(2)}) %all-to-all-start) | async-done | bytes 4718624 | tf_op jit(solution)/shard_map/all_to_all | solution.py:370
  79.0 8.2 %shard_map.138 = bf16[8,1024,128]{2,1,0:T(8,128)(2,1)S(1)} custom-call(s32[2]{0:T(128)S(1)} %pad_add_fusion.place_ref, bf16[8,8,144,256]{3,2,1,0:T(8,128)(2,1)} %bitcast.5.gathered_ref, bf16[32,4096]{1,0:T(8,128)(2,1)S(1)} %reshape.26.weight_ref), custom_call_target="tpu_custom_call" | custom-call | flops 4294967296 | bytes 6815744 | tf_op jit(solution)/shard_map/pallas_call | solution.py:182
  87.2 0.0 copy-start.5
  87.2 0.0 copy-start.6
  87.3 0.0 copy-start.10
  87.3 3.4 %collective-permute-start = (bf16[8,1024,128]{2,1,0:T(8,128)(2,1)S(1)}, bf16[8,1024,128]{2,1,0:T(8,128)(2,1)S(1)}, u32[]{:S(2)}, u32[]{:S(2)}) collective-permute-start(bf16[8,1024,128]{2,1,0:T(8,128)(2,1)S(1)} %shard_map.138), channel_id=1, source_target_pairs={{0,1},{1,0},{2,3},{3,2},{4,5},{5,4},{6,7},{7,6},{8,9},{9,8},{10,11... | collective-permute-start | bytes 6291464 | tf_op jit(solution)/shard_map/ppermute | solution.py:375
  90.7 8.2 %shard_map.137.own_ref = bf16[8,1024,128]{2,1,0:T(8,128)(2,1)S(1)} custom-call(s32[2]{0:T(128)S(1)} %pad_add_fusion.place_ref, bf16[8,8,144,256]{3,2,1,0:T(8,128)(2,1)} %bitcast.5.gathered_ref, bf16[32,4096]{1,0:T(8,128)(2,1)S(1)} %reshape.26.weight_ref), custom_call_target="tpu_custom_call" | custom-call | flops 4294967296 | bytes 6815744 | tf_op jit(solution)/shard_map/pallas_call | solution.py:182
  99.0 9.4 %shard_map.139 = (bf16[8,1024,128]{2,1,0:T(8,128)(2,1)S(1)}, bf16[8,1024,128]{2,1,0:T(8,128)(2,1)S(1)}, bf16[128,16,1024]{2,1,0:T(8,128)(2,1)S(1)}) custom-call(bf16[8,1024,128]{2,1,0:T(8,128)(2,1)S(1)} %copy-done.1, bf16[8,1024,128]{2,1,0:T(8,128)(2,1)S(1)} %shard_map.137.own_ref, bf16[8,1024,128]{2,1,0:T(8,128)(2,1)S(1)} %collective-permute-done.arrived_ref, ...), custom_call_target="tpu_custom_call" | custom-call | flops 1073741824 | bytes 18874368 | tf_op jit(solution)/shard_map/pallas_call | solution.py:257
  108.4 1.3 copy-done.2
  109.7 57.2 %all_to_all.15 = bf16[128,16,1024]{2,1,0:T(8,128)(2,1)S(1)} all-to-all(bf16[128,16,1024]{2,1,0:T(8,128)(2,1)S(1)} %get-tuple-element.8), channel_id=1, replica_groups=mesh['dap'=8,'chip'=8,'core'=2] {'dap','chip','core'}, dimensions={0} | all-to-all | bytes 8388608 | tf_op jit(solution)/shard_map/all_to_all | solution.py:386
  166.9 3.7 %convert_bitcast_fusion = bf16[128,8,1024]{2,1,0:T(8,128)(2,1)} fusion(bf16[128,16,1024]{2,1,0:T(8,128)(2,1)S(1)} %all_to_all.15), kind=kOutput, calls=%fused_computation.4 | convolution fusion | flops 2148532224 | bytes 6291456 | tf_op jit(solution)/shard_map/dot_general | solution.py:389
  170.6 8.2 %all-to-all-start.2 = ((bf16[128,8,1024]{2,1,0:T(8,128)(2,1)}), bf16[128,8,1024]{2,1,0:T(8,128)(2,1)S(1)}, u32[]{:S(2)}, u32[]{:S(2)}) async-start(bf16[128,8,1024]{2,1,0:T(8,128)(2,1)} %convert_bitcast_fusion), calls=%async_computation.2 | async-start | bytes 4194304 | tf_op jit(solution)/shard_map/all_to_all | solution.py:392
  178.7 0.1 copy.15.gain_ref
  178.8 0.0 copy-start.9
  178.9 4.2 %divide_convert_fusion.gate_ref = bf16[8,1024,128]{2,1,0:T(8,128)(2,1)} fusion(bf16[8,1024,128]{2,1,0:T(8,128)(2,1)} %copy-done.11, bf16[128,128]{1,0:T(8,128)(2,1)S(1)} %copy-done), kind=kOutput, calls=%fused_computation | convolution fusion | flops 272629760 | bytes 4227072 | tf_op jit(solution)/shard_map/dot_general | solution.py:384
  183.0 26.4 %all-to-all-done.2.mixed_ref = bf16[128,8,1024]{2,1,0:T(8,128)(2,1)S(1)} async-done(((bf16[128,8,1024]{2,1,0:T(8,128)(2,1)}), bf16[128,8,1024]{2,1,0:T(8,128)(2,1)S(1)}, u32[]{:S(2)}, u32[]{:S(2)}) %all-to-all-start.2) | async-done | bytes 2097184 | tf_op jit(solution)/shard_map/all_to_all | solution.py:392
  209.4 1.6 copy-done.3
  211.0 1.6 copy-done.4
  212.6 5.4 %shard_map.140 = bf16[8,1024,128]{2,1,0:T(8,128)(2,1)} custom-call(bf16[128,8,1024]{2,1,0:T(8,128)(2,1)S(1)} %all-to-all-done.2.mixed_ref, bf16[8,1024,128]{2,1,0:T(8,128)(2,1)S(1)} %copy-done.3, bf16[8,1024,128]{2,1,0:T(8,128)(2,1)S(1)} %copy-done.4, f32[128,1]{1,0:T(8,128)S(1)} %copy.15.gain_ref, bf16[128,128]{1,0:T(8,128)(2,1)S(1)} %copy-done.9), custom_call_target="tpu_custom_call" | custom-call | flops 268435456 | bytes 10485760 | tf_op jit(solution)/shard_map/pallas_call | solution.py:316
  (21 shorter events, 0.0 us)
Async XLA Ops:
  0.0 178.8 %copy-start = (bf16[128,128]{1,0:T(8,128)(2,1)S(1)}, bf16[128,128]{1,0:T(8,128)(2,1)}, u32[]{:S(2)}) copy-start(bf16[128,128]{1,0:T(8,128)(2,1)} %param.25) | copy-start | bytes 98308
  4.7 12.4 %copy-start.12 = (bf16[1024,128]{1,0:T(8,128)(2,1)S(1)}, bf16[1024,128]{1,0:T(8,128)(2,1)}, u32[]{:S(2)}) copy-start(bf16[1024,128]{1,0:T(8,128)(2,1)} %param.19) | copy-start | bytes 786436
  4.7 74.3 %all-to-all-start = ((bf16[64,144,256]{2,1,0:T(8,128)(2,1)}), bf16[64,144,256]{2,1,0:T(8,128)(2,1)}, u32[]{:S(2)}, u32[]{:S(2)}) async-start(bf16[64,144,256]{2,1,0:T(8,128)(2,1)} %shard_map.136), calls=%async_computation | async-start | bytes 9437184 | tf_op jit(solution)/shard_map/all_to_all | solution.py:370
  87.2 11.7 %copy-start.1 = (bf16[8,1024,128]{2,1,0:T(8,128)(2,1)S(1)}, bf16[8,1024,128]{2,1,0:T(8,128)(2,1)}, u32[]{:S(2)}) copy-start(bf16[8,1024,128]{2,1,0:T(8,128)(2,1)} %pair_ref.1) | copy-start | bytes 6291460
  87.2 11.7 %copy-start.5 = (bf16[128,128]{1,0:T(8,128)(2,1)S(1)}, bf16[128,128]{1,0:T(8,128)(2,1)}, u32[]{:S(2)}) copy-start(bf16[128,128]{1,0:T(8,128)(2,1)} %rest_0_.1) | copy-start | bytes 98308
  87.2 11.7 %copy-start.6 = (bf16[128,128]{1,0:T(8,128)(2,1)S(1)}, bf16[128,128]{1,0:T(8,128)(2,1)}, u32[]{:S(2)}) copy-start(bf16[128,128]{1,0:T(8,128)(2,1)} %rest_1_.1) | copy-start | bytes 98308
  87.3 11.7 %copy-start.7 = (bf16[128,128]{1,0:T(8,128)(2,1)S(1)}, bf16[128,128]{1,0:T(8,128)(2,1)}, u32[]{:S(2)}) copy-start(bf16[128,128]{1,0:T(8,128)(2,1)} %rest_2_.1) | copy-start | bytes 98308
  87.3 11.7 %copy-start.8 = (bf16[128,128]{1,0:T(8,128)(2,1)S(1)}, bf16[128,128]{1,0:T(8,128)(2,1)}, u32[]{:S(2)}) copy-start(bf16[128,128]{1,0:T(8,128)(2,1)} %rest_3_.1) | copy-start | bytes 98308
  87.3 11.7 %copy-start.10 = (f32[128]{0:T(128)S(1)}, f32[128]{0:T(128)}, u32[]{:S(2)}) copy-start(f32[128]{0:T(128)} %param.20) | copy-start | bytes 1540
  87.3 11.6 %collective-permute-start = (bf16[8,1024,128]{2,1,0:T(8,128)(2,1)S(1)}, bf16[8,1024,128]{2,1,0:T(8,128)(2,1)S(1)}, u32[]{:S(2)}, u32[]{:S(2)}) collective-permute-start(bf16[8,1024,128]{2,1,0:T(8,128)(2,1)S(1)} %shard_map.138), channel_id=1, source_target_pairs={{0,1},{1,0},{2,3},{3,2},{4,5},{5,4},{6,7},{7,6},{8,9},{9,8},{10,11... | collective-permute-start | bytes 6291464 | tf_op jit(solution)/shard_map/ppermute | solution.py:375
  108.3 1.3 copy-start.2
  109.7 57.2 %copy-start.11 = (bf16[8,1024,128]{2,1,0:T(8,128)(2,1)}, bf16[8,1024,128]{2,1,0:T(8,128)(2,1)S(1)}, u32[]{:S(2)}) copy-start(bf16[8,1024,128]{2,1,0:T(8,128)(2,1)S(1)} %get-tuple-element.10) | copy-start | bytes 6291460
  170.5 8.2 %copy-start.13 = (f32[128]{0:T(128)S(1)}, f32[128]{0:T(128)}, u32[]{:S(2)}) copy-start(f32[128]{0:T(128)} %param.26) | copy-start | bytes 1540
  170.6 38.9 %all-to-all-start.2 = ((bf16[128,8,1024]{2,1,0:T(8,128)(2,1)}), bf16[128,8,1024]{2,1,0:T(8,128)(2,1)S(1)}, u32[]{:S(2)}, u32[]{:S(2)}) async-start(bf16[128,8,1024]{2,1,0:T(8,128)(2,1)} %convert_bitcast_fusion), calls=%async_computation.2 | async-start | bytes 4194304 | tf_op jit(solution)/shard_map/all_to_all | solution.py:392
  178.8 30.6 %copy-start.9 = (bf16[128,128]{1,0:T(8,128)(2,1)S(1)}, bf16[128,128]{1,0:T(8,128)(2,1)}, u32[]{:S(2)}) copy-start(bf16[128,128]{1,0:T(8,128)(2,1)} %weight_ref.1) | copy-start | bytes 98308
  209.4 1.6 copy-start.3
  211.0 1.6 copy-start.4

commit v3 on v2

--- a/solution.py
+++ b/solution.py
@@ -27,12 +27,12 @@
     return lax.broadcasted_iota(jnp.int32, shape, axis)
 
 
-def msa_kernel(msa_ref, gain_ref, left_ref, right_ref, send_ref, block, sems):
+def msa_kernel(msa_ref, gain_ref, left_ref, right_ref, first_ref, second_ref, first, second, sems):
     seqs, cols, features = msa_ref.shape
     hidden = left_ref.shape[0]
     width = hidden * seqs
-    chips, rows_sent, _ = block.shape
-    left_rows = rows_sent - cols
+    chips, part, _ = second.shape
+    left_rows = first.shape[1] - part
     pairs = width // hidden
     spread = ones_where(iota((hidden, width), 1) // seqs == iota((hidden, width), 0))
     right_copies = lax.dot_general(
@@ -69,11 +69,15 @@
     right = right.astype(jnp.bfloat16)
     left = left.astype(jnp.bfloat16)
     for chip in range(chips):
-        block[chip, :cols, :] = right
-        block[chip, cols:, :] = left[chip * left_rows : (chip + 1) * left_rows]
+        first[chip, :part, :] = right[:part]
+        first[chip, part:, :] = left[chip * left_rows : (chip + 1) * left_rows]
+        second[chip] = right[part:]
     copies = [
-        pltpu.make_async_copy(block, send_ref.at[pl.ds(group * chips, chips)], sems.at[group])
-        for group in range(send_ref.shape[0] // chips)
+        pltpu.make_async_copy(
+            block, send_ref.at[pl.ds(group * chips, chips)], sems.at[k, group]
+        )
+        for k, (block, send_ref) in enumerate(((first, first_ref), (second, second_ref)))
+        for group in range(first_ref.shape[0] // chips)
     ]
     for copy in copies:
         copy.start()
@@ -93,18 +97,22 @@
         msa_kernel,
         grid=(1,),
         in_specs=[whole(operand.shape) for operand in operands],
-        out_specs=pl.BlockSpec(memory_space=pl.ANY),
-        out_shape=jax.ShapeDtypeStruct((groups * chips, cols + left_rows, width), jnp.bfloat16),
+        out_specs=[pl.BlockSpec(memory_space=pl.ANY)] * 2,
+        out_shape=[
+            jax.ShapeDtypeStruct((groups * chips, count, width), jnp.bfloat16)
+            for count in (cols // 2 + left_rows, cols // 2)
+        ],
         scratch_shapes=[
-            pltpu.VMEM((chips, cols + left_rows, width), jnp.bfloat16),
-            pltpu.SemaphoreType.DMA((groups,)),
+            pltpu.VMEM((chips, cols // 2 + left_rows, width), jnp.bfloat16),
+            pltpu.VMEM((chips, cols // 2, width), jnp.bfloat16),
+            pltpu.SemaphoreType.DMA((2, groups)),
         ],
         compiler_params=pltpu.CompilerParams(vmem_limit_bytes=58 * MIB),
     )(*operands)
 
 
 def opm_kernel(
-    own, place_ref, gathered_ref, weight_ref, out_ref, right_rows, left_block, left_rows, mixer, sems
+    own, place_ref, gathered_ref, left_ref, weight_ref, out_ref, right_rows, left_block, left_rows, mixer, sems
 ):
     groups, cols, _ = right_rows.shape
     _, chips, _, width = gathered_ref.shape
@@ -121,7 +129,9 @@
         for chip in range(chips)
     ]
     left_copy = pltpu.make_async_copy(
-        gathered_ref.at[place_ref[0], :, pl.ds(cols, 2 * seqs), :], left_block, sems.at[chips]
+        left_ref.at[place_ref[0], :, pl.ds(left_ref.shape[2] - 2 * seqs, 2 * seqs), :],
+        left_block,
+        sems.at[chips],
     )
 
     @pl.when(pl.program_id(0) == 0)
@@ -174,7 +184,7 @@
         out_ref[row] = out[:, row * channels : (row + 1) * channels].astype(out_ref.dtype)
 
 
-def opm_rows(own, place, gathered, weight, cols, rows, step_rows=4):
+def opm_rows(own, place, gathered, left, weight, cols, rows, step_rows=4):
     groups, chips, rows_sent, width = gathered.shape
     hidden = weight.shape[0]
     channels = weight.shape[1] // hidden
@@ -185,6 +195,7 @@
         in_specs=[
             pl.BlockSpec(memory_space=pltpu.SMEM),
             pl.BlockSpec(memory_space=pl.ANY),
+            pl.BlockSpec(memory_space=pl.ANY),
             whole(weight.shape),
         ],
         out_specs=pl.BlockSpec((step_rows, groups * cols, channels), lambda i: (i, 0, 0)),
@@ -202,7 +213,7 @@
             bytes_accessed=gathered.size * 2 + rows * groups * cols * channels * 2,
             transcendentals=0,
         ),
-    )(place, gathered, weight)
+    )(place, gathered, left, weight)
 
 
 def half_sigmoid(values):
@@ -213,7 +224,7 @@
     scale, pair_ref, own_ref, arrived_ref, gain_ref, *rest
 ):
     *weight_refs, updated_ref, normed_ref, send_ref, rows_buf, weight_buf = rest
-    rows, cols, width = pair_ref.shape
+    rows, cols, width = own_ref.shape
     channels = weight_refs[0].shape[1]
 
     @pl.when(pl.program_id(0) == 0)
@@ -223,7 +234,7 @@
 
     for row in range(rows):
         updated = (
-            pair_ref[row].astype(jnp.float32)
+            pair_ref[row].reshape(cols, width).astype(jnp.float32)
             + (own_ref[row].astype(jnp.float32) + arrived_ref[row].astype(jnp.float32)) * scale
         ).astype(jnp.bfloat16)
         updated_ref[row] = updated
@@ -249,8 +260,10 @@
         )
 
 
-def pair_operands(pair, own, arrived, gain, weights, scale):
-    rows, length, width = pair.shape
+def pair_operands(half, pair, own, arrived, gain, weights, scale):
+    rows, length, width = own.shape
+    groups = pair.shape[1]
+    part = length // groups
     channels = weights[0].shape[1]
     cols = 256
     block = pl.BlockSpec((rows, cols, width), lambda i: (0, i, 0))
@@ -258,7 +271,7 @@
         functools.partial(pair_kernel, scale),
         grid=(length // cols,),
         in_specs=[
-            block,
+            pl.BlockSpec((rows, cols // part, part, width), lambda i: (0, i, half, 0)),
             block,
             block,
             pl.BlockSpec((1, width), lambda i: (0, 0)),
@@ -270,8 +283,8 @@
             pl.BlockSpec((channels, 2 * rows, cols), lambda i: (0, 0, i)),
         ],
         out_shape=[
-            jax.ShapeDtypeStruct(pair.shape, jnp.bfloat16),
-            jax.ShapeDtypeStruct(pair.shape, jnp.bfloat16),
+            jax.ShapeDtypeStruct(own.shape, jnp.bfloat16),
+            jax.ShapeDtypeStruct(own.shape, jnp.bfloat16),
             jax.ShapeDtypeStruct((channels, 2 * rows, length), jnp.bfloat16),
         ],
         scratch_shapes=[
@@ -287,7 +300,8 @@
     )(pair, own, arrived, gain.reshape(1, width), *weights)
 
 
-def result_kernel(mixed_ref, updated_ref, gate_ref, gain_ref, weight_ref, out_ref, rows_buf):
+def result_kernel(mixed_ref, *refs):
+    *halves, gain_ref, weight_ref, out_ref, rows_buf = refs
     channels, rows, cols = mixed_ref.shape
     for lane in range(0, cols, 128):
         values = mixed_ref[:, :, lane : lane + 128].astype(jnp.float32)
@@ -302,37 +316,37 @@
             term = lax.dot_general(
                 normed, weight_ref[...], (((0,), (0,)), ((), ())), preferred_element_type=jnp.float32
             )
-            out_ref[row, lane : lane + 128, :] = (
-                updated_ref[row, lane : lane + 128, :].astype(jnp.float32)
-                + gate_ref[row, lane : lane + 128, :].astype(jnp.float32) * term
-            ).astype(jnp.bfloat16)
-
-
-def result_rows(mixed, updated, gate, gain, weight):
+            for half in range(2):
+                updated_ref, gate_ref = halves[2 * half : 2 * half + 2]
+                place = pl.ds(lane // 2, 64)
+                out_ref[row, lane + 64 * half : lane + 64 * half + 64, :] = (
+                    updated_ref[row, place, :].astype(jnp.float32)
+                    + gate_ref[row, place, :].astype(jnp.float32)
+                    * term[64 * half : 64 * half + 64]
+                ).astype(jnp.bfloat16)
+
+
+def result_rows(mixed, halves, gain, weight):
     channels, rows, length = mixed.shape
     width = weight.shape[1]
     cols = 256
-    block = pl.BlockSpec((rows, cols, width), lambda i: (0, i, 0))
+    half_block = pl.BlockSpec((rows, cols // 2, width), lambda i: (0, i, 0))
     return pl.pallas_call(
         result_kernel,
         grid=(length // cols,),
-        in_specs=[
-            pl.BlockSpec((channels, rows, cols), lambda i: (0, 0, i)),
-            block,
-            block,
-            pl.BlockSpec((channels, 1), lambda i: (0, 0)),
-            pl.BlockSpec(weight.shape, lambda i: (0, 0)),
-        ],
-        out_specs=block,
+        in_specs=[pl.BlockSpec((channels, rows, cols), lambda i: (0, 0, i))]
+        + [half_block] * len(halves)
+        + [whole((channels, 1)), whole(weight.shape)],
+        out_specs=pl.BlockSpec((rows, cols, width), lambda i: (0, i, 0)),
         out_shape=jax.ShapeDtypeStruct((rows, length, width), jnp.bfloat16),
         scratch_shapes=[pltpu.VMEM((channels * rows, 128), jnp.float32)],
         compiler_params=pltpu.CompilerParams(vmem_limit_bytes=14 * MIB),
         cost_estimate=pl.CostEstimate(
             flops=2 * rows * length * width * channels,
-            bytes_accessed=rows * length * width * 10,
+            bytes_accessed=rows * length * width * 8,
             transcendentals=0,
         ),
-    )(mixed, updated, gate, gain.reshape(channels, 1), weight)
+    )(mixed, *halves, gain.reshape(channels, 1), weight)
 
 
 def body(
@@ -358,7 +372,7 @@
     depth = seqs * chips * cores
     rows, length, pair_width = couple_embedding.shape
 
-    payload = msa_payload(
+    payloads = msa_payload(
         stacked_relatives_tensor,
         relatives_rescaler,
         averaged_lhs_weights,
@@ -367,32 +381,45 @@
         chips,
         cores * rows,
     )
-    gathered = lax.all_to_all(payload, ("dap", "chip"), split_axis=0, concat_axis=0, tiled=True)
-    gathered = gathered.reshape(groups, chips, cols + cores * rows, hidden * seqs)
+    part = cols // 2
+    gathered = [
+        lax.all_to_all(
+            payload, ("dap", "chip"), split_axis=0, concat_axis=0, tiled=True
+        ).reshape(groups, chips, *payload.shape[1:])
+        for payload in payloads
+    ]
     weight = mean_final_linear.reshape(hidden, hidden * pair_width)
     place = jnp.stack([lax.axis_index("dap"), lax.axis_index("core")])
-    other_part = opm_rows(False, place, gathered, weight, cols, rows)
-    arrived = lax.ppermute(other_part, "core", [(0, 1), (1, 0)])
-    own_part = opm_rows(True, place, gathered, weight, cols, rows)
+    pair = couple_embedding.reshape(rows, groups, cols, pair_width)
     tri_weights = (
         first_linear_map, first_sigmoid_factor, second_linear_map, second_sigmoid_factor
     )
-    updated, pair_normed, operands = pair_operands(
-        couple_embedding, own_part, arrived, couple_scale_vector, tri_weights, 1.0 / depth
-    )
-    gate = jax.nn.sigmoid(
-        jnp.dot(pair_normed, final_sigmoid_factor, preferred_element_type=jnp.float32)
-    ).astype(jnp.bfloat16)
-    operands = lax.all_to_all(operands, ALL, split_axis=0, concat_axis=0, tiled=True)
-    left_full = operands[:, :rows].reshape(devices * rows, length)
-    right_full = operands[:, rows:].reshape(devices * rows, length)
-    mixed = lax.dot_general(
-        left_full, right_full, (((1,), (1,)), ((), ())), preferred_element_type=jnp.float32
+    halves, operands = [], []
+    for half in range(2):
+        other_part = opm_rows(False, place, gathered[half], gathered[0], weight, part, rows)
+        arrived = lax.ppermute(other_part, "core", [(0, 1), (1, 0)])
+        own_part = opm_rows(True, place, gathered[half], gathered[0], weight, part, rows)
+        updated, pair_normed, send = pair_operands(
+            half, pair, own_part, arrived, couple_scale_vector, tri_weights, 1.0 / depth
+        )
+        gate = jax.nn.sigmoid(
+            jnp.dot(pair_normed, final_sigmoid_factor, preferred_element_type=jnp.float32)
+        ).astype(jnp.bfloat16)
+        halves += [updated, gate]
+        operands.append(lax.all_to_all(send, ALL, split_axis=0, concat_axis=0, tiled=True))
+    mixed = sum(
+        lax.dot_general(
+            operand[:, :rows].reshape(devices * rows, length // 2),
+            operand[:, rows:].reshape(devices * rows, length // 2),
+            (((1,), (1,)), ((), ())),
+            preferred_element_type=jnp.float32,
+        )
+        for operand in operands
     ).astype(jnp.bfloat16)
     mixed_back = lax.all_to_all(
         mixed.reshape(devices, rows, length), ALL, split_axis=0, concat_axis=0, tiled=True
     )
-    return result_rows(mixed_back, updated, gate, trio_scale_vector, trio_final_linear)
+    return result_rows(mixed_back, halves, trio_scale_vector, trio_final_linear)
 
 
 def solution(mesh):

time: 218 us -> 208 us (0.954)
  waiting for transfers between devices: 88.2 us -> 67.3 us
  blocking collectives: 57.2 us -> 46.8 us
  local copies, waits for them, and re-layouts: 4.81 us -> 13 us
  matrix products: 7.86 us -> 14.3 us
  Pallas kernels: 35.9 us -> 40.1 us
    all_to_all x1, waiting for transfers between devices: 61.7 us -> 6.8 us  [body(): lax.all_to_all(payload, ('dap', 'chip'), split_axis=0, concat_axis=0, til...]
    all_to_all x0 -> x2, waiting for transfers between devices: none -> 34.4 us  [body(): lax.all_to_all(send, ALL, split_axis=0, concat_axis=0, tiled=True)]
    all_to_all x0 -> x2, starting transfers between devices: none -> 12 us  [body(): lax.all_to_all(send, ALL, split_axis=0, concat_axis=0, tiled=True)]
    all_to_all x1, blocking collectives: 57.2 us -> 46.8 us  [body(): lax.all_to_all(payload, ('dap', 'chip'), split_axis=0, concat_axis=0, til...]
    unnamed x28 -> x46, local copies, waits for them, and re-layouts: 4.58 us -> 12.8 us
    all_to_all x1, starting transfers between devices: 12.3 us -> 5.69 us  [body(): lax.all_to_all(payload, ('dap', 'chip'), split_axis=0, concat_axis=0, til...]
    dot_general x1 -> x2, matrix products: 3.69 us -> 9.59 us  [body(): lax.dot_general(operand[:, :rows].reshape(devices * rows, length // 2), o...]
    pallas_call x2 -> x4, Pallas kernels: 16.3 us -> 20.6 us  [opm_rows(): pl.pallas_call(functools.partial(opm_kernel, own), grid=(rows // step_row...]
  transfers between devices with their start and end apart: 3 -> 6, of which waited for: 2 -> 4; matrix products, arithmetic and copies ran while one was open for 2% -> 5% of each run, Pallas kernels for 4% -> 14%
where the time goes in v3:
time: 208 us
  waiting for transfers between devices  67.3 us (32%)
  blocking collectives  46.8 us (22%)
  Pallas kernels  40.1 us (19%)
  starting transfers between devices  25.7 us (12%)
  matrix products  14.3 us (7%)
  local copies, waits for them, and re-layouts  13 us (6%)
    all_to_all x1, blocking collectives, body(): lax.all_to_all(payload, ('dap', 'chip'), split_axis=0, concat_axis=0, til...  46.8 us
    all_to_all x2, waiting for transfers between devices, body(): lax.all_to_all(send, ALL, split_axis=0, concat_axis=0, tiled=True)  34.4 us
    all_to_all x1, waiting for transfers between devices, body(): lax.all_to_all(mixed.reshape(devices, rows, length), ALL, split_axis=0, c...  26 us
    pallas_call x4, Pallas kernels, opm_rows(): pl.pallas_call(functools.partial(opm_kernel, own), grid=(rows // step_row...  20.6 us
    unnamed x46, local copies, waits for them, and re-layouts  12.8 us
    all_to_all x2, starting transfers between devices, body(): lax.all_to_all(send, ALL, split_axis=0, concat_axis=0, tiled=True)  12 us
    dot_general x2, matrix products, body(): lax.dot_general(operand[:, :rows].reshape(devices * rows, length // 2), o...  9.59 us
    pallas_call x2, Pallas kernels, pair_operands(): pl.pallas_call(functools.partial(pair_kernel, scale), grid=(length // col...  9.27 us
  transfers between devices with their start and end apart: 6, of which 4 were waited for; matrix products, arithmetic and copies ran while one was open for 5% of the time, Pallas kernels for 14%

profile of v3, /device:TPU:1, one launch (start us, length us, event | category | flops | bytes accessed | tf_op | source)
XLA Modules:
  0.0 207.5 jit_solution(13558497660262554348)
XLA Ops:
  0.0 4.8 %shard_map.136 = (bf16[64,80,256]{2,1,0:T(8,128)(2,1)}, bf16[64,64,256]{2,1,0:T(8,128)(2,1)}) custom-call(bf16[8,128,256]{2,1,0:T(8,128)(2,1)} %msa_ref.1, f32[1,256]{1,0:T(1,128)} %bitcast.43, bf16[32,256]{1,0:T(8,128)(2,1)} %bitcast.41, bf16[32,256]{1,0:T(8,128)(2,1)} %bitcast.42), custom_call_target="tpu_custom_call" | custom-call | tf_op jit(solution)/shard_map/pallas_call | solution.py:96
  4.8 46.8 %all_to_all.25 = bf16[64,80,256]{2,1,0:T(8,128)(2,1)S(1)} all-to-all(bf16[64,80,256]{2,1,0:T(8,128)(2,1)} %get-tuple-element.13), channel_id=1, replica_groups=mesh['dap'=8,'chip'=8,'core'=2] {'dap','chip'}, dimensions={0} | all-to-all | bytes 5242880 | tf_op jit(solution)/shard_map/all_to_all | solution.py:386
  51.5 5.7 %all-to-all-start.2 = ((bf16[64,64,256]{2,1,0:T(8,128)(2,1)}), bf16[64,64,256]{2,1,0:T(8,128)(2,1)}, u32[]{:S(2)}, u32[]{:S(2)}) async-start(bf16[64,64,256]{2,1,0:T(8,128)(2,1)} %get-tuple-element.15), calls=%async_computation.2 | async-start | bytes 4194304 | tf_op jit(solution)/shard_map/all_to_all | solution.py:386
  57.5 4.9 %shard_map.138 = bf16[8,512,128]{2,1,0:T(8,128)(2,1)S(1)} custom-call(s32[2]{0:T(128)S(1)} %pad_add_fusion.place_ref, bf16[8,8,80,256]{3,2,1,0:T(8,128)(2,1)S(1)} %bitcast.33, bf16[8,8,80,256]{3,2,1,0:T(8,128)(2,1)S(1)} %bitcast.34, bf16[32,4096]{1,0:T(8,128)(2,1)S(1)} %reshape.40.weight_ref), custom_call_target="tpu_custom_call" | custom-call | flops 2147483648 | bytes 3670016 | tf_op jit(solution)/shard_map/pallas_call | solution.py:192
  62.4 2.1 collective-permute-start
  64.5 1.7 copy-done.3
  66.3 5.0 %shard_map.137.own_ref = bf16[8,512,128]{2,1,0:T(8,128)(2,1)S(1)} custom-call(s32[2]{0:T(128)S(1)} %pad_add_fusion.place_ref, bf16[8,8,80,256]{3,2,1,0:T(8,128)(2,1)S(1)} %bitcast.35, bf16[8,8,80,256]{3,2,1,0:T(8,128)(2,1)S(1)} %bitcast.36, bf16[32,4096]{1,0:T(8,128)(2,1)S(1)} %reshape.40.weight_ref), custom_call_target="tpu_custom_call" | custom-call | flops 2147483648 | bytes 3670016 | tf_op jit(solution)/shard_map/pallas_call | solution.py:192
  71.3 4.6 %shard_map.139 = (bf16[8,512,128]{2,1,0:T(8,128)(2,1)S(1)}, bf16[8,512,128]{2,1,0:T(8,128)(2,1)S(1)}, bf16[128,16,512]{2,1,0:T(8,128)(2,1)S(1)}) custom-call(bf16[8,8,128,128]{3,2,1,0:T(8,128)(2,1)S(1)} %bitcast.31, bf16[8,512,128]{2,1,0:T(8,128)(2,1)S(1)} %shard_map.137.own_ref, bf16[8,512,128]{2,1,0:T(8,128)(2,1)S(1)} %collective-permute-done.arrived_ref, ...), custom_call_target="tpu_custom_call" | custom-call | flops 536870912 | bytes 9437184 | tf_op jit(solution)/shard_map/pallas_call | solution.py:270
  78.3 6.8 %all-to-all-done.2 = bf16[64,64,256]{2,1,0:T(8,128)(2,1)} async-done(((bf16[64,64,256]{2,1,0:T(8,128)(2,1)}), bf16[64,64,256]{2,1,0:T(8,128)(2,1)}, u32[]{:S(2)}, u32[]{:S(2)}) %all-to-all-start.2) | async-done | bytes 2097184 | tf_op jit(solution)/shard_map/all_to_all | solution.py:386
  85.1 7.6 %all-to-all-start.1 = ((bf16[128,16,512]{2,1,0:T(8,128)(2,1)}), bf16[128,16,512]{2,1,0:T(8,128)(2,1)}, u32[]{:S(2)}, u32[]{:S(2)}) async-start(bf16[128,16,512]{2,1,0:T(8,128)(2,1)} %copy-done.5), calls=%async_computation.1 | async-start | bytes 4194304 | tf_op jit(solution)/shard_map/all_to_all | solution.py:409
  92.7 1.7 copy-done.4
  94.4 5.4 %shard_map.141 = bf16[8,512,128]{2,1,0:T(8,128)(2,1)S(1)} custom-call(s32[2]{0:T(128)S(1)} %pad_add_fusion.place_ref, bf16[8,8,64,256]{3,2,1,0:T(8,128)(2,1)} %bitcast.10.gathered_ref, bf16[8,8,80,256]{3,2,1,0:T(8,128)(2,1)S(1)} %bitcast.37, bf16[32,4096]{1,0:T(8,128)(2,1)S(1)} %reshape.40.weight_ref), custom_call_target="tpu_custom_call" | custom-call | flops 2147483648 | bytes 3145728 | tf_op jit(solution)/shard_map/pallas_call | solution.py:192
  101.3 5.4 %shard_map.140.own_ref = bf16[8,512,128]{2,1,0:T(8,128)(2,1)S(1)} custom-call(s32[2]{0:T(128)S(1)} %pad_add_fusion.place_ref, bf16[8,8,64,256]{3,2,1,0:T(8,128)(2,1)} %bitcast.10.gathered_ref, bf16[8,8,80,256]{3,2,1,0:T(8,128)(2,1)S(1)} %bitcast.38, bf16[32,4096]{1,0:T(8,128)(2,1)S(1)} %reshape.40.weight_ref), custom_call_target="tpu_custom_call" | custom-call | flops 2147483648 | bytes 3145728 | tf_op jit(solution)/shard_map/pallas_call | solution.py:192
  106.7 4.6 %shard_map.142 = (bf16[8,512,128]{2,1,0:T(8,128)(2,1)S(1)}, bf16[8,512,128]{2,1,0:T(8,128)(2,1)S(1)}, bf16[128,16,512]{2,1,0:T(8,128)(2,1)S(1)}) custom-call(bf16[8,8,128,128]{3,2,1,0:T(8,128)(2,1)S(1)} %bitcast.32, bf16[8,512,128]{2,1,0:T(8,128)(2,1)S(1)} %shard_map.140.own_ref, bf16[8,512,128]{2,1,0:T(8,128)(2,1)S(1)} %collective-permute-done.1.arrived_ref, ...), custom_call_target="tpu_custom_call" | custom-call | flops 536870912 | bytes 9437184 | tf_op jit(solution)/shard_map/pallas_call | solution.py:270
  114.7 8.5 %all-to-all-done.1 = bf16[128,16,512]{2,1,0:T(8,128)(2,1)} async-done(((bf16[128,16,512]{2,1,0:T(8,128)(2,1)}), bf16[128,16,512]{2,1,0:T(8,128)(2,1)}, u32[]{:S(2)}, u32[]{:S(2)}) %all-to-all-start.1) | async-done | bytes 2097184 | tf_op jit(solution)/shard_map/all_to_all | solution.py:409
  123.2 4.4 %all-to-all-start.3 = ((bf16[128,16,512]{2,1,0:T(8,128)(2,1)}), bf16[128,16,512]{2,1,0:T(8,128)(2,1)S(1)}, u32[]{:S(2)}, u32[]{:S(2)}) async-start(bf16[128,16,512]{2,1,0:T(8,128)(2,1)} %copy-done.6), calls=%async_computation.3 | async-start | bytes 4194304 | tf_op jit(solution)/shard_map/all_to_all | solution.py:409
  127.6 4.8 %fusion.1 = f32[1024,1024]{1,0:T(8,128)} fusion(bf16[128,16,512]{2,1,0:T(8,128)(2,1)} %all-to-all-done.1), kind=kOutput, calls=%fused_computation.7 | convolution fusion | flops 1073741824 | bytes 6291456 | tf_op jit(solution)/shard_map/dot_general | solution.py:411
  132.4 25.9 %all-to-all-done.3 = bf16[128,16,512]{2,1,0:T(8,128)(2,1)S(1)} async-done(((bf16[128,16,512]{2,1,0:T(8,128)(2,1)}), bf16[128,16,512]{2,1,0:T(8,128)(2,1)S(1)}, u32[]{:S(2)}, u32[]{:S(2)}) %all-to-all-start.3) | async-done | bytes 2097184 | tf_op jit(solution)/shard_map/all_to_all | solution.py:409
  158.3 4.8 %fusion = bf16[128,8,1024]{2,1,0:T(8,128)(2,1)} fusion(f32[1024,1024]{1,0:T(8,128)} %fusion.1, bf16[128,16,512]{2,1,0:T(8,128)(2,1)S(1)} %all-to-all-done.3), kind=kOutput, calls=%fused_computation.3 | convolution fusion | flops 1075838976 | bytes 8388608 | tf_op jit(solution)/shard_map/dot_general | solution.py:411
  163.1 4.4 %all-to-all-start.4 = ((bf16[128,8,1024]{2,1,0:T(8,128)(2,1)}), bf16[128,8,1024]{2,1,0:T(8,128)(2,1)S(1)}, u32[]{:S(2)}, u32[]{:S(2)}) async-start(bf16[128,8,1024]{2,1,0:T(8,128)(2,1)} %fusion), calls=%async_computation.4 | async-start | bytes 4194304 | tf_op jit(solution)/shard_map/all_to_all | solution.py:419
  167.7 3.0 %divide_convert_fusion.refs_3_ = bf16[8,512,128]{2,1,0:T(8,128)(2,1)} fusion(bf16[8,512,128]{2,1,0:T(8,128)(2,1)} %copy-done.20, bf16[128,128]{1,0:T(8,128)(2,1)S(1)} %copy-done), kind=kOutput, calls=%fused_computation.1 | convolution fusion | flops 136314880 | bytes 2129920 | tf_op jit(solution)/shard_map/dot_general | solution.py:406
  170.7 1.7 divide_convert_fusion.1.refs_1_
  172.4 26.0 %all-to-all-done.4.mixed_ref = bf16[128,8,1024]{2,1,0:T(8,128)(2,1)S(1)} async-done(((bf16[128,8,1024]{2,1,0:T(8,128)(2,1)}), bf16[128,8,1024]{2,1,0:T(8,128)(2,1)S(1)}, u32[]{:S(2)}, u32[]{:S(2)}) %all-to-all-start.4) | async-done | bytes 2097184 | tf_op jit(solution)/shard_map/all_to_all | solution.py:419
  202.1 5.5 %shard_map.143 = bf16[8,1024,128]{2,1,0:T(8,128)(2,1)} custom-call(bf16[128,8,1024]{2,1,0:T(8,128)(2,1)S(1)} %all-to-all-done.4.mixed_ref, bf16[8,512,128]{2,1,0:T(8,128)(2,1)S(1)} %get-tuple-element.17.refs_0_, bf16[8,512,128]{2,1,0:T(8,128)(2,1)S(1)} %copy-done.10, bf16[8,512,128]{2,1,0:T(8,128)(2,1)S(1)} %copy-done.8, bf16[8,512,128]{2,1,0:T(8,128)(2,1)S(1)} %copy-done.9, ...), custom_call_target="tpu_custom_call" | custom-call | flops 268435456 | bytes 8388608 | tf_op jit(solution)/shard_map/pallas_call | solution.py:334
  (50 shorter events, 11.2 us)
Async XLA Ops:
  0.0 167.7 %copy-start = (bf16[128,128]{1,0:T(8,128)(2,1)S(1)}, bf16[128,128]{1,0:T(8,128)(2,1)}, u32[]{:S(2)}) copy-start(bf16[128,128]{1,0:T(8,128)(2,1)} %param.25) | copy-start | bytes 98308
  51.5 5.9 %copy-start.2 = (bf16[64,80,256]{2,1,0:T(8,128)(2,1)}, bf16[64,80,256]{2,1,0:T(8,128)(2,1)S(1)}, u32[]{:S(2)}) copy-start(bf16[64,80,256]{2,1,0:T(8,128)(2,1)S(1)} %all_to_all.25) | copy-start | bytes 7864324
  51.5 5.7 %copy-start.21 = (bf16[1024,128]{1,0:T(8,128)(2,1)S(1)}, bf16[1024,128]{1,0:T(8,128)(2,1)}, u32[]{:S(2)}) copy-start(bf16[1024,128]{1,0:T(8,128)(2,1)} %param.19) | copy-start | bytes 786436
  51.5 33.6 %all-to-all-start.2 = ((bf16[64,64,256]{2,1,0:T(8,128)(2,1)}), bf16[64,64,256]{2,1,0:T(8,128)(2,1)}, u32[]{:S(2)}, u32[]{:S(2)}) async-start(bf16[64,64,256]{2,1,0:T(8,128)(2,1)} %get-tuple-element.15), calls=%async_computation.2 | async-start | bytes 4194304 | tf_op jit(solution)/shard_map/all_to_all | solution.py:386
  62.4 8.8 %copy-start.1 = (bf16[8,1024,128]{2,1,0:T(8,128)(2,1)S(1)}, bf16[8,1024,128]{2,1,0:T(8,128)(2,1)}, u32[]{:S(2)}) copy-start(bf16[8,1024,128]{2,1,0:T(8,128)(2,1)} %param.15) | copy-start | bytes 6291460
  62.4 8.8 %collective-permute-start = (bf16[8,512,128]{2,1,0:T(8,128)(2,1)S(1)}, bf16[8,512,128]{2,1,0:T(8,128)(2,1)S(1)}, u32[]{:S(2)}, u32[]{:S(2)}) collective-permute-start(bf16[8,512,128]{2,1,0:T(8,128)(2,1)S(1)} %shard_map.138), channel_id=1, source_target_pairs={{0,1},{1,0},{2,3},{3,2},{4,5},{5,4},{6,7},{7,6},{8,9},{9,8},{10,11... | collective-permute-start | bytes 3145736 | tf_op jit(solution)/shard_map/ppermute | solution.py:400
  64.5 1.7 copy-start.3
  66.2 5.0 %copy-start.11 = (bf16[128,128]{1,0:T(8,128)(2,1)S(1)}, bf16[128,128]{1,0:T(8,128)(2,1)}, u32[]{:S(2)}) copy-start(bf16[128,128]{1,0:T(8,128)(2,1)} %rest_0_.3) | copy-start | bytes 98308
  66.2 5.0 %copy-start.12 = (bf16[128,128]{1,0:T(8,128)(2,1)S(1)}, bf16[128,128]{1,0:T(8,128)(2,1)}, u32[]{:S(2)}) copy-start(bf16[128,128]{1,0:T(8,128)(2,1)} %rest_1_.3) | copy-start | bytes 98308
  66.2 5.0 %copy-start.13 = (bf16[128,128]{1,0:T(8,128)(2,1)S(1)}, bf16[128,128]{1,0:T(8,128)(2,1)}, u32[]{:S(2)}) copy-start(bf16[128,128]{1,0:T(8,128)(2,1)} %rest_2_.3) | copy-start | bytes 98308
  66.2 5.0 %copy-start.14 = (bf16[128,128]{1,0:T(8,128)(2,1)S(1)}, bf16[128,128]{1,0:T(8,128)(2,1)}, u32[]{:S(2)}) copy-start(bf16[128,128]{1,0:T(8,128)(2,1)} %rest_3_.3) | copy-start | bytes 98308
  66.3 5.0 %copy-start.17 = (f32[128]{0:T(128)S(1)}, f32[128]{0:T(128)}, u32[]{:S(2)}) copy-start(f32[128]{0:T(128)} %param.20) | copy-start | bytes 1540
  76.0 1.4 copy-start.5
  85.1 38.1 %all-to-all-start.1 = ((bf16[128,16,512]{2,1,0:T(8,128)(2,1)}), bf16[128,16,512]{2,1,0:T(8,128)(2,1)}, u32[]{:S(2)}, u32[]{:S(2)}) async-start(bf16[128,16,512]{2,1,0:T(8,128)(2,1)} %copy-done.5), calls=%async_computation.1 | async-start | bytes 4194304 | tf_op jit(solution)/shard_map/all_to_all | solution.py:409
  92.7 1.7 copy-start.4
  99.8 6.9 %copy-start.15 = (bf16[128,128]{1,0:T(8,128)(2,1)S(1)}, bf16[128,128]{1,0:T(8,128)(2,1)}, u32[]{:S(2)}) copy-start(bf16[128,128]{1,0:T(8,128)(2,1)} %rest_3_.3) | copy-start | bytes 98308
  99.8 6.9 %collective-permute-start.1 = (bf16[8,512,128]{2,1,0:T(8,128)(2,1)S(1)}, bf16[8,512,128]{2,1,0:T(8,128)(2,1)S(1)}, u32[]{:S(2)}, u32[]{:S(2)}) collective-permute-start(bf16[8,512,128]{2,1,0:T(8,128)(2,1)S(1)} %shard_map.141), channel_id=1, source_target_pairs={{0,1},{1,0},{2,3},{3,2},{4,5},{5,4},{6,7},{7,6},{8,9},{9,8},{10,11... | collective-permute-start | bytes 3145736 | tf_op jit(solution)/shard_map/ppermute | solution.py:400
  111.4 1.3 copy-start.6
  123.2 35.1 %all-to-all-start.3 = ((bf16[128,16,512]{2,1,0:T(8,128)(2,1)}), bf16[128,16,512]{2,1,0:T(8,128)(2,1)S(1)}, u32[]{:S(2)}, u32[]{:S(2)}) async-start(bf16[128,16,512]{2,1,0:T(8,128)(2,1)} %copy-done.6), calls=%async_computation.3 | async-start | bytes 4194304 | tf_op jit(solution)/shard_map/all_to_all | solution.py:409
  163.1 4.4 %copy-start.22 = (f32[128]{0:T(128)S(1)}, f32[128]{0:T(128)}, u32[]{:S(2)}) copy-start(f32[128]{0:T(128)} %param.26) | copy-start | bytes 1540
  163.1 35.3 %all-to-all-start.4 = ((bf16[128,8,1024]{2,1,0:T(8,128)(2,1)}), bf16[128,8,1024]{2,1,0:T(8,128)(2,1)S(1)}, u32[]{:S(2)}, u32[]{:S(2)}) async-start(bf16[128,8,1024]{2,1,0:T(8,128)(2,1)} %fusion), calls=%async_computation.4 | async-start | bytes 4194304 | tf_op jit(solution)/shard_map/all_to_all | solution.py:419
  167.7 3.0 %copy-start.19 = (bf16[8,512,128]{2,1,0:T(8,128)(2,1)S(1)}, bf16[8,512,128]{2,1,0:T(8,128)(2,1)}, u32[]{:S(2)}) copy-start(bf16[8,512,128]{2,1,0:T(8,128)(2,1)} %copy-done.18) | copy-start | bytes 3145732
  170.7 27.7 %copy-start.16 = (bf16[128,128]{1,0:T(8,128)(2,1)S(1)}, bf16[128,128]{1,0:T(8,128)(2,1)}, u32[]{:S(2)}) copy-start(bf16[128,128]{1,0:T(8,128)(2,1)} %refs_5_.1) | copy-start | bytes 98308
  198.4 1.2 copy-start.8
  (5 other events, 5.4 us)

commit v4 on v3

--- a/solution.py
+++ b/solution.py
@@ -309,21 +309,21 @@
         spread = jnp.mean(center * center, axis=0, keepdims=True)
         scaled = center * (1.0 / jnp.sqrt(spread + 1e-05))
         rows_buf[...] = scaled.reshape(channels * rows, 128)
-        for row in range(rows):
-            normed = (rows_buf[pl.ds(row, channels, stride=rows), :] * gain_ref[...]).astype(
-                jnp.bfloat16
-            )
-            term = lax.dot_general(
-                normed, weight_ref[...], (((0,), (0,)), ((), ())), preferred_element_type=jnp.float32
-            )
-            for half in range(2):
-                updated_ref, gate_ref = halves[2 * half : 2 * half + 2]
-                place = pl.ds(lane // 2, 64)
-                out_ref[row, lane + 64 * half : lane + 64 * half + 64, :] = (
-                    updated_ref[row, place, :].astype(jnp.float32)
-                    + gate_ref[row, place, :].astype(jnp.float32)
-                    * term[64 * half : 64 * half + 64]
-                ).astype(jnp.bfloat16)
+        normed = jnp.concatenate(
+            [rows_buf[pl.ds(row, channels, stride=rows), :] * gain_ref[...] for row in range(rows)],
+            axis=1,
+        ).astype(jnp.bfloat16)
+        term = lax.dot_general(
+            normed, weight_ref[...], (((0,), (0,)), ((), ())), preferred_element_type=jnp.float32
+        ).reshape(rows, 128, -1)
+        for half in range(2):
+            updated_ref, gate_ref = halves[2 * half : 2 * half + 2]
+            place = pl.ds(lane // 2, 64)
+            out_ref[:, lane + 64 * half : lane + 64 * half + 64, :] = (
+                updated_ref[:, place, :].astype(jnp.float32)
+                + gate_ref[:, place, :].astype(jnp.float32)
+                * term[:, 64 * half : 64 * half + 64]
+            ).astype(jnp.bfloat16)
 
 
 def result_rows(mixed, halves, gain, weight):
@@ -340,7 +340,7 @@
         out_specs=pl.BlockSpec((rows, cols, width), lambda i: (0, i, 0)),
         out_shape=jax.ShapeDtypeStruct((rows, length, width), jnp.bfloat16),
         scratch_shapes=[pltpu.VMEM((channels * rows, 128), jnp.float32)],
-        compiler_params=pltpu.CompilerParams(vmem_limit_bytes=14 * MIB),
+        compiler_params=pltpu.CompilerParams(vmem_limit_bytes=62 * MIB),
         cost_estimate=pl.CostEstimate(
             flops=2 * rows * length * width * channels,
             bytes_accessed=rows * length * width * 8,
@@ -407,15 +407,18 @@
         ).astype(jnp.bfloat16)
         halves += [updated, gate]
         operands.append(lax.all_to_all(send, ALL, split_axis=0, concat_axis=0, tiled=True))
-    mixed = sum(
-        lax.dot_general(
+    products = [
+        functools.partial(
+            lax.dot_general,
             operand[:, :rows].reshape(devices * rows, length // 2),
             operand[:, rows:].reshape(devices * rows, length // 2),
             (((1,), (1,)), ((), ())),
             preferred_element_type=jnp.float32,
         )
         for operand in operands
-    ).astype(jnp.bfloat16)
+    ]
+    first_half = lax.optimization_barrier(products[0]().astype(jnp.bfloat16))
+    mixed = (first_half.astype(jnp.float32) + products[1]()).astype(jnp.bfloat16)
     mixed_back = lax.all_to_all(
         mixed.reshape(devices, rows, length), ALL, split_axis=0, concat_axis=0, tiled=True
     )

time: 208 us -> 207 us (level)
  local copies, waits for them, and re-layouts: 13 us -> 6.37 us
  waiting for transfers between devices: 67.3 us -> 70 us
  Pallas kernels: 40.1 us -> 42.8 us
    unnamed x46 -> x28, local copies, waits for them, and re-layouts: 12.8 us -> 5.51 us
  transfers between devices with their start and end apart: 6 -> 6, of which waited for: 4 -> 4; matrix products, arithmetic and copies ran while one was open for 5% -> 4% of each run, Pallas kernels for 14% -> 15%
where the time goes in v4:
time: 207 us; the launch traced here: 206 us
  waiting for transfers between devices  70 us (34%)
  blocking collectives  46.9 us (23%)
  Pallas kernels  42.8 us (21%)
  starting transfers between devices  27.6 us (13%)
  matrix products  12.4 us (6%)
  local copies, waits for them, and re-layouts  6.37 us (3%)
    all_to_all x1, blocking collectives, body(): lax.all_to_all(payload, ('dap', 'chip'), split_axis=0, concat_axis=0, til...  46.9 us
    all_to_all x2, waiting for transfers between devices, body(): lax.all_to_all(send, ALL, split_axis=0, concat_axis=0, tiled=True)  36.4 us
    all_to_all x1, waiting for transfers between devices, body(): lax.all_to_all(mixed.reshape(devices, rows, length), ALL, split_axis=0, c...  26.3 us
    pallas_call x4, Pallas kernels, opm_rows(): pl.pallas_call(functools.partial(opm_kernel, own), grid=(rows // step_row...  20.6 us
    all_to_all x2, starting transfers between devices, body(): lax.all_to_all(send, ALL, split_axis=0, concat_axis=0, tiled=True)  12.9 us
    pallas_call x2, Pallas kernels, pair_operands(): pl.pallas_call(functools.partial(pair_kernel, scale), grid=(length // col...  11 us
    all_to_all x1, waiting for transfers between devices, body(): lax.all_to_all(payload, ('dap', 'chip'), split_axis=0, concat_axis=0, til...  7.23 us
    pallas_call x1, Pallas kernels, result_rows(): pl.pallas_call(result_kernel, grid=(length // cols,), in_specs=[pl.BlockS...  6.43 us
  transfers between devices with their start and end apart: 6, of which 4 were waited for; matrix products, arithmetic and copies ran while one was open for 4% of the time, Pallas kernels for 15%

profile of v4, /device:TPU:1, one launch (start us, length us, event | category | flops | bytes accessed | tf_op | source)
XLA Modules:
  0.0 206.4 jit_solution(5183075308590088836)
XLA Ops:
  0.0 4.8 %shard_map.136 = (bf16[64,80,256]{2,1,0:T(8,128)(2,1)}, bf16[64,64,256]{2,1,0:T(8,128)(2,1)}) custom-call(bf16[8,128,256]{2,1,0:T(8,128)(2,1)} %msa_ref.1, f32[1,256]{1,0:T(1,128)} %bitcast.43, bf16[32,256]{1,0:T(8,128)(2,1)} %bitcast.41, bf16[32,256]{1,0:T(8,128)(2,1)} %bitcast.42), custom_call_target="tpu_custom_call" | custom-call | tf_op jit(solution)/shard_map/pallas_call | solution.py:96
  4.8 46.9 %all_to_all.25 = bf16[64,80,256]{2,1,0:T(8,128)(2,1)} all-to-all(bf16[64,80,256]{2,1,0:T(8,128)(2,1)} %get-tuple-element.13), channel_id=1, replica_groups=mesh['dap'=8,'chip'=8,'core'=2] {'dap','chip'}, dimensions={0} | all-to-all | bytes 5242880 | tf_op jit(solution)/shard_map/all_to_all | solution.py:386
  51.6 5.7 %all-to-all-start.2 = ((bf16[64,64,256]{2,1,0:T(8,128)(2,1)}), bf16[64,64,256]{2,1,0:T(8,128)(2,1)}, u32[]{:S(2)}, u32[]{:S(2)}) async-start(bf16[64,64,256]{2,1,0:T(8,128)(2,1)} %get-tuple-element.15), calls=%async_computation.2 | async-start | bytes 4194304 | tf_op jit(solution)/shard_map/all_to_all | solution.py:386
  57.6 1.7 copy-done.3
  59.3 4.9 %shard_map.138 = bf16[8,512,128]{2,1,0:T(8,128)(2,1)S(1)} custom-call(s32[2]{0:T(128)S(1)} %pad_add_fusion.place_ref, bf16[8,8,80,256]{3,2,1,0:T(8,128)(2,1)S(1)} %bitcast.33, bf16[8,8,80,256]{3,2,1,0:T(8,128)(2,1)S(1)} %bitcast.34, bf16[32,4096]{1,0:T(8,128)(2,1)S(1)} %reshape.40.weight_ref), custom_call_target="tpu_custom_call" | custom-call | flops 2147483648 | bytes 3670016 | tf_op jit(solution)/shard_map/pallas_call | solution.py:192
  64.3 2.1 collective-permute-start
  66.4 4.9 %shard_map.137.own_ref = bf16[8,512,128]{2,1,0:T(8,128)(2,1)S(1)} custom-call(s32[2]{0:T(128)S(1)} %pad_add_fusion.place_ref, bf16[8,8,80,256]{3,2,1,0:T(8,128)(2,1)S(1)} %bitcast.35, bf16[8,8,80,256]{3,2,1,0:T(8,128)(2,1)S(1)} %bitcast.36, bf16[32,4096]{1,0:T(8,128)(2,1)S(1)} %reshape.40.weight_ref), custom_call_target="tpu_custom_call" | custom-call | flops 2147483648 | bytes 3670016 | tf_op jit(solution)/shard_map/pallas_call | solution.py:192
  71.4 5.5 %shard_map.139 = (bf16[8,512,128]{2,1,0:T(8,128)(2,1)S(1)}, bf16[8,512,128]{2,1,0:T(8,128)(2,1)S(1)}, bf16[128,16,512]{2,1,0:T(8,128)(2,1)}) custom-call(bf16[8,8,128,128]{3,2,1,0:T(8,128)(2,1)S(1)} %bitcast.31, bf16[8,512,128]{2,1,0:T(8,128)(2,1)S(1)} %shard_map.137.own_ref, bf16[8,512,128]{2,1,0:T(8,128)(2,1)S(1)} %collective-permute-done.arrived_ref, ...), custom_call_target="tpu_custom_call" | custom-call | flops 536870912 | bytes 9437184 | tf_op jit(solution)/shard_map/pallas_call | solution.py:270
  78.0 7.2 %all-to-all-done.2 = bf16[64,64,256]{2,1,0:T(8,128)(2,1)} async-done(((bf16[64,64,256]{2,1,0:T(8,128)(2,1)}), bf16[64,64,256]{2,1,0:T(8,128)(2,1)}, u32[]{:S(2)}, u32[]{:S(2)}) %all-to-all-start.2) | async-done | bytes 2097184 | tf_op jit(solution)/shard_map/all_to_all | solution.py:386
  85.2 7.6 %all-to-all-start.1 = ((bf16[128,16,512]{2,1,0:T(8,128)(2,1)}), bf16[128,16,512]{2,1,0:T(8,128)(2,1)}, u32[]{:S(2)}, u32[]{:S(2)}) async-start(bf16[128,16,512]{2,1,0:T(8,128)(2,1)} %get-tuple-element.14), calls=%async_computation.1 | async-start | bytes 4194304 | tf_op jit(solution)/shard_map/all_to_all | solution.py:409
  92.8 1.7 copy-done.4
  94.5 5.4 %shard_map.141 = bf16[8,512,128]{2,1,0:T(8,128)(2,1)S(1)} custom-call(s32[2]{0:T(128)S(1)} %pad_add_fusion.place_ref, bf16[8,8,64,256]{3,2,1,0:T(8,128)(2,1)} %bitcast.10.gathered_ref, bf16[8,8,80,256]{3,2,1,0:T(8,128)(2,1)S(1)} %bitcast.37, bf16[32,4096]{1,0:T(8,128)(2,1)S(1)} %reshape.40.weight_ref), custom_call_target="tpu_custom_call" | custom-call | flops 2147483648 | bytes 3145728 | tf_op jit(solution)/shard_map/pallas_call | solution.py:192
  101.5 5.3 %shard_map.140.own_ref = bf16[8,512,128]{2,1,0:T(8,128)(2,1)S(1)} custom-call(s32[2]{0:T(128)S(1)} %pad_add_fusion.place_ref, bf16[8,8,64,256]{3,2,1,0:T(8,128)(2,1)} %bitcast.10.gathered_ref, bf16[8,8,80,256]{3,2,1,0:T(8,128)(2,1)S(1)} %bitcast.38, bf16[32,4096]{1,0:T(8,128)(2,1)S(1)} %reshape.40.weight_ref), custom_call_target="tpu_custom_call" | custom-call | flops 2147483648 | bytes 3145728 | tf_op jit(solution)/shard_map/pallas_call | solution.py:192
  106.8 5.5 %shard_map.142 = (bf16[8,512,128]{2,1,0:T(8,128)(2,1)S(1)}, bf16[8,512,128]{2,1,0:T(8,128)(2,1)S(1)}, bf16[128,16,512]{2,1,0:T(8,128)(2,1)}) custom-call(bf16[8,8,128,128]{3,2,1,0:T(8,128)(2,1)S(1)} %bitcast.32, bf16[8,512,128]{2,1,0:T(8,128)(2,1)S(1)} %shard_map.140.own_ref, bf16[8,512,128]{2,1,0:T(8,128)(2,1)S(1)} %collective-permute-done.1.arrived_ref, ...), custom_call_target="tpu_custom_call" | custom-call | flops 536870912 | bytes 9437184 | tf_op jit(solution)/shard_map/pallas_call | solution.py:270
  113.3 10.0 %all-to-all-done.1 = bf16[128,16,512]{2,1,0:T(8,128)(2,1)} async-done(((bf16[128,16,512]{2,1,0:T(8,128)(2,1)}), bf16[128,16,512]{2,1,0:T(8,128)(2,1)}, u32[]{:S(2)}, u32[]{:S(2)}) %all-to-all-start.1) | async-done | bytes 2097184 | tf_op jit(solution)/shard_map/all_to_all | solution.py:409
  123.3 5.3 %all-to-all-start.3 = ((bf16[128,16,512]{2,1,0:T(8,128)(2,1)}), bf16[128,16,512]{2,1,0:T(8,128)(2,1)}, u32[]{:S(2)}, u32[]{:S(2)}) async-start(bf16[128,16,512]{2,1,0:T(8,128)(2,1)} %get-tuple-element.16), calls=%async_computation.3 | async-start | bytes 4194304 | tf_op jit(solution)/shard_map/all_to_all | solution.py:409
  128.6 4.1 %convolution_convert_fusion = bf16[1024,1024]{1,0:T(8,128)(2,1)} fusion(bf16[128,16,512]{2,1,0:T(8,128)(2,1)} %all-to-all-done.1), kind=kOutput, calls=%fused_computation.3 | convolution fusion | flops 1074790400 | bytes 4194304 | tf_op jit(solution)/shard_map/dot_general | solution.py:420
  132.8 26.4 %all-to-all-done.3 = bf16[128,16,512]{2,1,0:T(8,128)(2,1)} async-done(((bf16[128,16,512]{2,1,0:T(8,128)(2,1)}), bf16[128,16,512]{2,1,0:T(8,128)(2,1)}, u32[]{:S(2)}, u32[]{:S(2)}) %all-to-all-start.3) | async-done | bytes 2097184 | tf_op jit(solution)/shard_map/all_to_all | solution.py:409
  159.1 4.9 %fusion = bf16[128,8,1024]{2,1,0:T(8,128)(2,1)} fusion(bf16[1024,1024]{1,0:T(8,128)(2,1)} %convolution_convert_fusion, bf16[128,16,512]{2,1,0:T(8,128)(2,1)} %all-to-all-done.3), kind=kOutput, calls=%fused_computation.4 | convolution fusion | flops 1076887552 | bytes 6291456 | tf_op jit(solution)/shard_map/dot_general | solution.py:421
  164.0 5.4 %all-to-all-start.4 = ((bf16[128,8,1024]{2,1,0:T(8,128)(2,1)}), bf16[128,8,1024]{2,1,0:T(8,128)(2,1)}, u32[]{:S(2)}, u32[]{:S(2)}) async-start(bf16[128,8,1024]{2,1,0:T(8,128)(2,1)} %fusion), calls=%async_computation.4 | async-start | bytes 4194304 | tf_op jit(solution)/shard_map/all_to_all | solution.py:422
  170.2 1.7 divide_convert_fusion.refs_3_
  171.9 1.7 divide_convert_fusion.1.refs_1_
  173.6 26.3 %all-to-all-done.4.mixed_ref = bf16[128,8,1024]{2,1,0:T(8,128)(2,1)} async-done(((bf16[128,8,1024]{2,1,0:T(8,128)(2,1)}), bf16[128,8,1024]{2,1,0:T(8,128)(2,1)}, u32[]{:S(2)}, u32[]{:S(2)}) %all-to-all-start.4) | async-done | bytes 2097184 | tf_op jit(solution)/shard_map/all_to_all | solution.py:422
  200.0 6.4 %shard_map.143 = bf16[8,1024,128]{2,1,0:T(8,128)(2,1)} custom-call(bf16[128,8,1024]{2,1,0:T(8,128)(2,1)} %all-to-all-done.4.mixed_ref, bf16[8,512,128]{2,1,0:T(8,128)(2,1)} %copy-done.5, bf16[8,512,128]{2,1,0:T(8,128)(2,1)} %divide_convert_fusion.1.refs_1_, bf16[8,512,128]{2,1,0:T(8,128)(2,1)} %copy-done.6, bf16[8,512,128]{2,1,0:T(8,128)(2,1)} %divide_convert_fusion.refs_3_, ...), custom_call_target="tpu_custom_call" | custom-call | flops 268435456 | bytes 8388608 | tf_op jit(solution)/shard_map/pallas_call | solution.py:334
  (32 shorter events, 4.5 us)
Async XLA Ops:
  0.0 170.2 %copy-start = (bf16[128,128]{1,0:T(8,128)(2,1)S(1)}, bf16[128,128]{1,0:T(8,128)(2,1)}, u32[]{:S(2)}) copy-start(bf16[128,128]{1,0:T(8,128)(2,1)} %param.25) | copy-start | bytes 98308
  51.6 5.7 %copy-start.12 = (bf16[1024,128]{1,0:T(8,128)(2,1)S(1)}, bf16[1024,128]{1,0:T(8,128)(2,1)}, u32[]{:S(2)}) copy-start(bf16[1024,128]{1,0:T(8,128)(2,1)} %param.19) | copy-start | bytes 786436
  51.6 33.6 %all-to-all-start.2 = ((bf16[64,64,256]{2,1,0:T(8,128)(2,1)}), bf16[64,64,256]{2,1,0:T(8,128)(2,1)}, u32[]{:S(2)}, u32[]{:S(2)}) async-start(bf16[64,64,256]{2,1,0:T(8,128)(2,1)} %get-tuple-element.15), calls=%async_computation.2 | async-start | bytes 4194304 | tf_op jit(solution)/shard_map/all_to_all | solution.py:386
  57.6 1.7 copy-start.3
  64.3 7.1 %copy-start.1 = (bf16[8,1024,128]{2,1,0:T(8,128)(2,1)S(1)}, bf16[8,1024,128]{2,1,0:T(8,128)(2,1)}, u32[]{:S(2)}) copy-start(bf16[8,1024,128]{2,1,0:T(8,128)(2,1)} %param.15) | copy-start | bytes 6291460
  64.3 7.1 %copy-start.7 = (bf16[128,128]{1,0:T(8,128)(2,1)S(1)}, bf16[128,128]{1,0:T(8,128)(2,1)}, u32[]{:S(2)}) copy-start(bf16[128,128]{1,0:T(8,128)(2,1)} %rest_0_.3) | copy-start | bytes 98308
  64.3 7.1 %copy-start.8 = (bf16[128,128]{1,0:T(8,128)(2,1)S(1)}, bf16[128,128]{1,0:T(8,128)(2,1)}, u32[]{:S(2)}) copy-start(bf16[128,128]{1,0:T(8,128)(2,1)} %rest_1_.3) | copy-start | bytes 98308
  64.3 7.1 %copy-start.9 = (bf16[128,128]{1,0:T(8,128)(2,1)S(1)}, bf16[128,128]{1,0:T(8,128)(2,1)}, u32[]{:S(2)}) copy-start(bf16[128,128]{1,0:T(8,128)(2,1)} %rest_2_.3) | copy-start | bytes 98308
  64.3 7.1 %copy-start.10 = (bf16[128,128]{1,0:T(8,128)(2,1)S(1)}, bf16[128,128]{1,0:T(8,128)(2,1)}, u32[]{:S(2)}) copy-start(bf16[128,128]{1,0:T(8,128)(2,1)} %rest_3_.3) | copy-start | bytes 98308
  64.3 7.1 %copy-start.11 = (f32[128]{0:T(128)S(1)}, f32[128]{0:T(128)}, u32[]{:S(2)}) copy-start(f32[128]{0:T(128)} %param.20) | copy-start | bytes 1540
  64.3 7.0 %collective-permute-start = (bf16[8,512,128]{2,1,0:T(8,128)(2,1)S(1)}, bf16[8,512,128]{2,1,0:T(8,128)(2,1)S(1)}, u32[]{:S(2)}, u32[]{:S(2)}) collective-permute-start(bf16[8,512,128]{2,1,0:T(8,128)(2,1)S(1)} %shard_map.138), channel_id=1, source_target_pairs={{0,1},{1,0},{2,3},{3,2},{4,5},{5,4},{6,7},{7,6},{8,9},{9,8},{10,11... | collective-permute-start | bytes 3145736 | tf_op jit(solution)/shard_map/ppermute | solution.py:400
  77.0 1.0 copy-start.5
  85.2 38.1 %all-to-all-start.1 = ((bf16[128,16,512]{2,1,0:T(8,128)(2,1)}), bf16[128,16,512]{2,1,0:T(8,128)(2,1)}, u32[]{:S(2)}, u32[]{:S(2)}) async-start(bf16[128,16,512]{2,1,0:T(8,128)(2,1)} %get-tuple-element.14), calls=%async_computation.1 | async-start | bytes 4194304 | tf_op jit(solution)/shard_map/all_to_all | solution.py:409
  92.8 1.7 copy-start.4
  99.9 6.9 %copy-start.2 = (bf16[8,1024,128]{2,1,0:T(8,128)(2,1)S(1)}, bf16[8,1024,128]{2,1,0:T(8,128)(2,1)}, u32[]{:S(2)}) copy-start(bf16[8,1024,128]{2,1,0:T(8,128)(2,1)} %param.15) | copy-start | bytes 6291460
  99.9 6.9 %collective-permute-start.1 = (bf16[8,512,128]{2,1,0:T(8,128)(2,1)S(1)}, bf16[8,512,128]{2,1,0:T(8,128)(2,1)S(1)}, u32[]{:S(2)}, u32[]{:S(2)}) collective-permute-start(bf16[8,512,128]{2,1,0:T(8,128)(2,1)S(1)} %shard_map.141), channel_id=1, source_target_pairs={{0,1},{1,0},{2,3},{3,2},{4,5},{5,4},{6,7},{7,6},{8,9},{9,8},{10,11... | collective-permute-start | bytes 3145736 | tf_op jit(solution)/shard_map/ppermute | solution.py:400
  112.3 1.0 copy-start.6
  123.3 35.8 %all-to-all-start.3 = ((bf16[128,16,512]{2,1,0:T(8,128)(2,1)}), bf16[128,16,512]{2,1,0:T(8,128)(2,1)}, u32[]{:S(2)}, u32[]{:S(2)}) async-start(bf16[128,16,512]{2,1,0:T(8,128)(2,1)} %get-tuple-element.16), calls=%async_computation.3 | async-start | bytes 4194304 | tf_op jit(solution)/shard_map/all_to_all | solution.py:409
  164.0 5.5 %copy-start.13 = (f32[128]{0:T(128)S(1)}, f32[128]{0:T(128)}, u32[]{:S(2)}) copy-start(f32[128]{0:T(128)} %param.26) | copy-start | bytes 1540
  164.0 36.0 %all-to-all-start.4 = ((bf16[128,8,1024]{2,1,0:T(8,128)(2,1)}), bf16[128,8,1024]{2,1,0:T(8,128)(2,1)}, u32[]{:S(2)}, u32[]{:S(2)}) async-start(bf16[128,8,1024]{2,1,0:T(8,128)(2,1)} %fusion), calls=%async_computation.4 | async-start | bytes 4194304 | tf_op jit(solution)/shard_map/all_to_all | solution.py:422

commit v5 on v4

--- a/solution.py
+++ b/solution.py
@@ -340,7 +340,7 @@
         out_specs=pl.BlockSpec((rows, cols, width), lambda i: (0, i, 0)),
         out_shape=jax.ShapeDtypeStruct((rows, length, width), jnp.bfloat16),
         scratch_shapes=[pltpu.VMEM((channels * rows, 128), jnp.float32)],
-        compiler_params=pltpu.CompilerParams(vmem_limit_bytes=62 * MIB),
+        compiler_params=pltpu.CompilerParams(vmem_limit_bytes=56 * MIB),
         cost_estimate=pl.CostEstimate(
             flops=2 * rows * length * width * channels,
             bytes_accessed=rows * length * width * 8,

time: 207 us -> 206 us (level)
  local copies, waits for them, and re-layouts: 6.37 us -> 11.4 us
    unnamed x28 -> x38, local copies, waits for them, and re-layouts: 5.51 us -> 10.5 us
where the time goes in v5:
time: 206 us
  waiting for transfers between devices  68.6 us (33%)
  blocking collectives  46.8 us (23%)
  Pallas kernels  41.1 us (20%)
  starting transfers between devices  25.7 us (12%)
  matrix products  11.8 us (6%)
  local copies, waits for them, and re-layouts  11.4 us (6%)
    all_to_all x1, blocking collectives, body(): lax.all_to_all(payload, ('dap', 'chip'), split_axis=0, concat_axis=0, til...  46.8 us
    all_to_all x2, waiting for transfers between devices, body(): lax.all_to_all(send, ALL, split_axis=0, concat_axis=0, tiled=True)  36.1 us
    all_to_all x1, waiting for transfers between devices, body(): lax.all_to_all(mixed.reshape(devices, rows, length), ALL, split_axis=0, c...  26.7 us
    pallas_call x4, Pallas kernels, opm_rows(): pl.pallas_call(functools.partial(opm_kernel, own), grid=(rows // step_row...  20.6 us
    all_to_all x2, starting transfers between devices, body(): lax.all_to_all(send, ALL, split_axis=0, concat_axis=0, tiled=True)  12 us
    unnamed x38, local copies, waits for them, and re-layouts  10.5 us
    pallas_call x2, Pallas kernels, pair_operands(): pl.pallas_call(functools.partial(pair_kernel, scale), grid=(length // col...  9.26 us
    pallas_call x1, Pallas kernels, result_rows(): pl.pallas_call(result_kernel, grid=(length // cols,), in_specs=[pl.BlockS...  6.42 us
  transfers between devices with their start and end apart: 6, of which 4 were waited for; matrix products, arithmetic and copies ran while one was open for 4% of the time, Pallas kernels for 15%

profile of v5, /device:TPU:1, one launch (start us, length us, event | category | flops | bytes accessed | tf_op | source)
XLA Modules:
  0.0 205.6 jit_solution(6162716074618248690)
XLA Ops:
  0.0 4.8 %shard_map.136 = (bf16[64,80,256]{2,1,0:T(8,128)(2,1)}, bf16[64,64,256]{2,1,0:T(8,128)(2,1)}) custom-call(bf16[8,128,256]{2,1,0:T(8,128)(2,1)} %msa_ref.1, f32[1,256]{1,0:T(1,128)} %bitcast.43, bf16[32,256]{1,0:T(8,128)(2,1)} %bitcast.41, bf16[32,256]{1,0:T(8,128)(2,1)} %bitcast.42), custom_call_target="tpu_custom_call" | custom-call | tf_op jit(solution)/shard_map/pallas_call | solution.py:96
  4.8 46.8 %all_to_all.25 = bf16[64,80,256]{2,1,0:T(8,128)(2,1)S(1)} all-to-all(bf16[64,80,256]{2,1,0:T(8,128)(2,1)} %get-tuple-element.13), channel_id=1, replica_groups=mesh['dap'=8,'chip'=8,'core'=2] {'dap','chip'}, dimensions={0} | all-to-all | bytes 5242880 | tf_op jit(solution)/shard_map/all_to_all | solution.py:386
  51.5 5.7 %all-to-all-start.2 = ((bf16[64,64,256]{2,1,0:T(8,128)(2,1)}), bf16[64,64,256]{2,1,0:T(8,128)(2,1)}, u32[]{:S(2)}, u32[]{:S(2)}) async-start(bf16[64,64,256]{2,1,0:T(8,128)(2,1)} %get-tuple-element.15), calls=%async_computation.2 | async-start | bytes 4194304 | tf_op jit(solution)/shard_map/all_to_all | solution.py:386
  57.5 4.9 %shard_map.138 = bf16[8,512,128]{2,1,0:T(8,128)(2,1)S(1)} custom-call(s32[2]{0:T(128)S(1)} %pad_add_fusion.place_ref, bf16[8,8,80,256]{3,2,1,0:T(8,128)(2,1)S(1)} %bitcast.33, bf16[8,8,80,256]{3,2,1,0:T(8,128)(2,1)S(1)} %bitcast.34, bf16[32,4096]{1,0:T(8,128)(2,1)S(1)} %reshape.40.weight_ref), custom_call_target="tpu_custom_call" | custom-call | flops 2147483648 | bytes 3670016 | tf_op jit(solution)/shard_map/pallas_call | solution.py:192
  62.4 2.1 %collective-permute-start = (bf16[8,512,128]{2,1,0:T(8,128)(2,1)S(1)}, bf16[8,512,128]{2,1,0:T(8,128)(2,1)S(1)}, u32[]{:S(2)}, u32[]{:S(2)}) collective-permute-start(bf16[8,512,128]{2,1,0:T(8,128)(2,1)S(1)} %shard_map.138), channel_id=1, source_target_pairs={{0,1},{1,0},{2,3},{3,2},{4,5},{5,4},{6,7},{7,6},{8,9},{9,8},{10,11... | collective-permute-start | bytes 3145736 | tf_op jit(solution)/shard_map/ppermute | solution.py:400
  64.5 1.7 copy-done.3
  66.3 5.0 %shard_map.137.own_ref = bf16[8,512,128]{2,1,0:T(8,128)(2,1)S(1)} custom-call(s32[2]{0:T(128)S(1)} %pad_add_fusion.place_ref, bf16[8,8,80,256]{3,2,1,0:T(8,128)(2,1)S(1)} %bitcast.35, bf16[8,8,80,256]{3,2,1,0:T(8,128)(2,1)S(1)} %bitcast.36, bf16[32,4096]{1,0:T(8,128)(2,1)S(1)} %reshape.40.weight_ref), custom_call_target="tpu_custom_call" | custom-call | flops 2147483648 | bytes 3670016 | tf_op jit(solution)/shard_map/pallas_call | solution.py:192
  71.3 4.6 %shard_map.139 = (bf16[8,512,128]{2,1,0:T(8,128)(2,1)S(1)}, bf16[8,512,128]{2,1,0:T(8,128)(2,1)S(1)}, bf16[128,16,512]{2,1,0:T(8,128)(2,1)S(1)}) custom-call(bf16[8,8,128,128]{3,2,1,0:T(8,128)(2,1)S(1)} %bitcast.31, bf16[8,512,128]{2,1,0:T(8,128)(2,1)S(1)} %shard_map.137.own_ref, bf16[8,512,128]{2,1,0:T(8,128)(2,1)S(1)} %collective-permute-done.arrived_ref, ...), custom_call_target="tpu_custom_call" | custom-call | flops 536870912 | bytes 9437184 | tf_op jit(solution)/shard_map/pallas_call | solution.py:270
  79.3 5.8 %all-to-all-done.2 = bf16[64,64,256]{2,1,0:T(8,128)(2,1)} async-done(((bf16[64,64,256]{2,1,0:T(8,128)(2,1)}), bf16[64,64,256]{2,1,0:T(8,128)(2,1)}, u32[]{:S(2)}, u32[]{:S(2)}) %all-to-all-start.2) | async-done | bytes 2097184 | tf_op jit(solution)/shard_map/all_to_all | solution.py:386
  85.1 7.6 %all-to-all-start.1 = ((bf16[128,16,512]{2,1,0:T(8,128)(2,1)}), bf16[128,16,512]{2,1,0:T(8,128)(2,1)}, u32[]{:S(2)}, u32[]{:S(2)}) async-start(bf16[128,16,512]{2,1,0:T(8,128)(2,1)} %copy-done.5), calls=%async_computation.1 | async-start | bytes 4194304 | tf_op jit(solution)/shard_map/all_to_all | solution.py:409
  92.7 1.7 copy-done.4
  94.4 5.4 %shard_map.141 = bf16[8,512,128]{2,1,0:T(8,128)(2,1)S(1)} custom-call(s32[2]{0:T(128)S(1)} %pad_add_fusion.place_ref, bf16[8,8,64,256]{3,2,1,0:T(8,128)(2,1)} %bitcast.10.gathered_ref, bf16[8,8,80,256]{3,2,1,0:T(8,128)(2,1)S(1)} %bitcast.37, bf16[32,4096]{1,0:T(8,128)(2,1)S(1)} %reshape.40.weight_ref), custom_call_target="tpu_custom_call" | custom-call | flops 2147483648 | bytes 3145728 | tf_op jit(solution)/shard_map/pallas_call | solution.py:192
  101.3 5.4 %shard_map.140.own_ref = bf16[8,512,128]{2,1,0:T(8,128)(2,1)S(1)} custom-call(s32[2]{0:T(128)S(1)} %pad_add_fusion.place_ref, bf16[8,8,64,256]{3,2,1,0:T(8,128)(2,1)} %bitcast.10.gathered_ref, bf16[8,8,80,256]{3,2,1,0:T(8,128)(2,1)S(1)} %bitcast.38, bf16[32,4096]{1,0:T(8,128)(2,1)S(1)} %reshape.40.weight_ref), custom_call_target="tpu_custom_call" | custom-call | flops 2147483648 | bytes 3145728 | tf_op jit(solution)/shard_map/pallas_call | solution.py:192
  106.7 4.6 %shard_map.142 = (bf16[8,512,128]{2,1,0:T(8,128)(2,1)S(1)}, bf16[8,512,128]{2,1,0:T(8,128)(2,1)S(1)}, bf16[128,16,512]{2,1,0:T(8,128)(2,1)S(1)}) custom-call(bf16[8,8,128,128]{3,2,1,0:T(8,128)(2,1)S(1)} %bitcast.32, bf16[8,512,128]{2,1,0:T(8,128)(2,1)S(1)} %shard_map.140.own_ref, bf16[8,512,128]{2,1,0:T(8,128)(2,1)S(1)} %collective-permute-done.1.arrived_ref, ...), custom_call_target="tpu_custom_call" | custom-call | flops 536870912 | bytes 9437184 | tf_op jit(solution)/shard_map/pallas_call | solution.py:270
  113.7 9.5 %all-to-all-done.1 = bf16[128,16,512]{2,1,0:T(8,128)(2,1)} async-done(((bf16[128,16,512]{2,1,0:T(8,128)(2,1)}), bf16[128,16,512]{2,1,0:T(8,128)(2,1)}, u32[]{:S(2)}, u32[]{:S(2)}) %all-to-all-start.1) | async-done | bytes 2097184 | tf_op jit(solution)/shard_map/all_to_all | solution.py:409
  123.2 4.4 %all-to-all-start.3 = ((bf16[128,16,512]{2,1,0:T(8,128)(2,1)}), bf16[128,16,512]{2,1,0:T(8,128)(2,1)S(1)}, u32[]{:S(2)}, u32[]{:S(2)}) async-start(bf16[128,16,512]{2,1,0:T(8,128)(2,1)} %copy-done.6), calls=%async_computation.3 | async-start | bytes 4194304 | tf_op jit(solution)/shard_map/all_to_all | solution.py:409
  127.6 4.1 %convolution_convert_fusion = bf16[1024,1024]{1,0:T(8,128)(2,1)} fusion(bf16[128,16,512]{2,1,0:T(8,128)(2,1)} %all-to-all-done.1), kind=kOutput, calls=%fused_computation.3 | convolution fusion | flops 1074790400 | bytes 4194304 | tf_op jit(solution)/shard_map/dot_general | solution.py:420
  131.8 26.6 %all-to-all-done.3 = bf16[128,16,512]{2,1,0:T(8,128)(2,1)S(1)} async-done(((bf16[128,16,512]{2,1,0:T(8,128)(2,1)}), bf16[128,16,512]{2,1,0:T(8,128)(2,1)S(1)}, u32[]{:S(2)}, u32[]{:S(2)}) %all-to-all-start.3) | async-done | bytes 2097184 | tf_op jit(solution)/shard_map/all_to_all | solution.py:409
  158.3 4.2 %fusion = bf16[128,8,1024]{2,1,0:T(8,128)(2,1)} fusion(bf16[1024,1024]{1,0:T(8,128)(2,1)} %convolution_convert_fusion, bf16[128,16,512]{2,1,0:T(8,128)(2,1)S(1)} %all-to-all-done.3), kind=kOutput, calls=%fused_computation.4 | convolution fusion | flops 1076887552 | bytes 6291456 | tf_op jit(solution)/shard_map/dot_general | solution.py:421
  162.6 4.4 %all-to-all-start.4 = ((bf16[128,8,1024]{2,1,0:T(8,128)(2,1)}), bf16[128,8,1024]{2,1,0:T(8,128)(2,1)S(1)}, u32[]{:S(2)}, u32[]{:S(2)}) async-start(bf16[128,8,1024]{2,1,0:T(8,128)(2,1)} %fusion), calls=%async_computation.4 | async-start | bytes 4194304 | tf_op jit(solution)/shard_map/all_to_all | solution.py:422
  167.7 1.7 divide_convert_fusion.refs_3_
  169.4 1.7 divide_convert_fusion.1.refs_1_
  171.1 26.7 %all-to-all-done.4.mixed_ref = bf16[128,8,1024]{2,1,0:T(8,128)(2,1)S(1)} async-done(((bf16[128,8,1024]{2,1,0:T(8,128)(2,1)}), bf16[128,8,1024]{2,1,0:T(8,128)(2,1)S(1)}, u32[]{:S(2)}, u32[]{:S(2)}) %all-to-all-start.4) | async-done | bytes 2097184 | tf_op jit(solution)/shard_map/all_to_all | solution.py:422
  199.2 6.4 %shard_map.143 = bf16[8,1024,128]{2,1,0:T(8,128)(2,1)} custom-call(bf16[128,8,1024]{2,1,0:T(8,128)(2,1)} %copy-done.16, bf16[8,512,128]{2,1,0:T(8,128)(2,1)} %copy-done.7, bf16[8,512,128]{2,1,0:T(8,128)(2,1)} %divide_convert_fusion.1.refs_1_, bf16[8,512,128]{2,1,0:T(8,128)(2,1)} %copy-done.8, bf16[8,512,128]{2,1,0:T(8,128)(2,1)} %divide_convert_fusion.refs_3_, ...), custom_call_target="tpu_custom_call" | custom-call | flops 268435456 | bytes 8388608 | tf_op jit(solution)/shard_map/pallas_call | solution.py:334
  (42 shorter events, 9.5 us)
Async XLA Ops:
  0.0 167.7 %copy-start = (bf16[128,128]{1,0:T(8,128)(2,1)S(1)}, bf16[128,128]{1,0:T(8,128)(2,1)}, u32[]{:S(2)}) copy-start(bf16[128,128]{1,0:T(8,128)(2,1)} %param.25) | copy-start | bytes 98308
  51.5 5.9 %copy-start.2 = (bf16[64,80,256]{2,1,0:T(8,128)(2,1)}, bf16[64,80,256]{2,1,0:T(8,128)(2,1)S(1)}, u32[]{:S(2)}) copy-start(bf16[64,80,256]{2,1,0:T(8,128)(2,1)S(1)} %all_to_all.25) | copy-start | bytes 7864324
  51.5 5.7 %copy-start.17 = (bf16[1024,128]{1,0:T(8,128)(2,1)S(1)}, bf16[1024,128]{1,0:T(8,128)(2,1)}, u32[]{:S(2)}) copy-start(bf16[1024,128]{1,0:T(8,128)(2,1)} %param.19) | copy-start | bytes 786436
  51.5 33.6 %all-to-all-start.2 = ((bf16[64,64,256]{2,1,0:T(8,128)(2,1)}), bf16[64,64,256]{2,1,0:T(8,128)(2,1)}, u32[]{:S(2)}, u32[]{:S(2)}) async-start(bf16[64,64,256]{2,1,0:T(8,128)(2,1)} %get-tuple-element.15), calls=%async_computation.2 | async-start | bytes 4194304 | tf_op jit(solution)/shard_map/all_to_all | solution.py:386
  62.4 8.8 %copy-start.1 = (bf16[8,1024,128]{2,1,0:T(8,128)(2,1)S(1)}, bf16[8,1024,128]{2,1,0:T(8,128)(2,1)}, u32[]{:S(2)}) copy-start(bf16[8,1024,128]{2,1,0:T(8,128)(2,1)} %param.15) | copy-start | bytes 6291460
  62.4 8.8 %collective-permute-start = (bf16[8,512,128]{2,1,0:T(8,128)(2,1)S(1)}, bf16[8,512,128]{2,1,0:T(8,128)(2,1)S(1)}, u32[]{:S(2)}, u32[]{:S(2)}) collective-permute-start(bf16[8,512,128]{2,1,0:T(8,128)(2,1)S(1)} %shard_map.138), channel_id=1, source_target_pairs={{0,1},{1,0},{2,3},{3,2},{4,5},{5,4},{6,7},{7,6},{8,9},{9,8},{10,11... | collective-permute-start | bytes 3145736 | tf_op jit(solution)/shard_map/ppermute | solution.py:400
  64.5 1.7 copy-start.3
  66.2 5.0 %copy-start.9 = (bf16[128,128]{1,0:T(8,128)(2,1)S(1)}, bf16[128,128]{1,0:T(8,128)(2,1)}, u32[]{:S(2)}) copy-start(bf16[128,128]{1,0:T(8,128)(2,1)} %rest_0_.3) | copy-start | bytes 98308
  66.2 5.0 %copy-start.10 = (bf16[128,128]{1,0:T(8,128)(2,1)S(1)}, bf16[128,128]{1,0:T(8,128)(2,1)}, u32[]{:S(2)}) copy-start(bf16[128,128]{1,0:T(8,128)(2,1)} %rest_1_.3) | copy-start | bytes 98308
  66.2 5.0 %copy-start.11 = (bf16[128,128]{1,0:T(8,128)(2,1)S(1)}, bf16[128,128]{1,0:T(8,128)(2,1)}, u32[]{:S(2)}) copy-start(bf16[128,128]{1,0:T(8,128)(2,1)} %rest_2_.3) | copy-start | bytes 98308
  66.3 5.0 %copy-start.12 = (bf16[128,128]{1,0:T(8,128)(2,1)S(1)}, bf16[128,128]{1,0:T(8,128)(2,1)}, u32[]{:S(2)}) copy-start(bf16[128,128]{1,0:T(8,128)(2,1)} %rest_3_.3) | copy-start | bytes 98308
  66.3 5.0 %copy-start.13 = (f32[128]{0:T(128)S(1)}, f32[128]{0:T(128)}, u32[]{:S(2)}) copy-start(f32[128]{0:T(128)} %param.20) | copy-start | bytes 1540
  75.9 1.4 copy-start.5
  78.3 1.0 copy-start.14
  85.1 38.1 %all-to-all-start.1 = ((bf16[128,16,512]{2,1,0:T(8,128)(2,1)}), bf16[128,16,512]{2,1,0:T(8,128)(2,1)}, u32[]{:S(2)}, u32[]{:S(2)}) async-start(bf16[128,16,512]{2,1,0:T(8,128)(2,1)} %copy-done.5), calls=%async_computation.1 | async-start | bytes 4194304 | tf_op jit(solution)/shard_map/all_to_all | solution.py:409
  92.7 1.7 copy-start.4
  99.8 6.9 %collective-permute-start.1 = (bf16[8,512,128]{2,1,0:T(8,128)(2,1)S(1)}, bf16[8,512,128]{2,1,0:T(8,128)(2,1)S(1)}, u32[]{:S(2)}, u32[]{:S(2)}) collective-permute-start(bf16[8,512,128]{2,1,0:T(8,128)(2,1)S(1)} %shard_map.141), channel_id=1, source_target_pairs={{0,1},{1,0},{2,3},{3,2},{4,5},{5,4},{6,7},{7,6},{8,9},{9,8},{10,11... | collective-permute-start | bytes 3145736 | tf_op jit(solution)/shard_map/ppermute | solution.py:400
  111.4 1.3 copy-start.6
  112.7 1.0 copy-start.8
  123.2 35.1 %all-to-all-start.3 = ((bf16[128,16,512]{2,1,0:T(8,128)(2,1)}), bf16[128,16,512]{2,1,0:T(8,128)(2,1)S(1)}, u32[]{:S(2)}, u32[]{:S(2)}) async-start(bf16[128,16,512]{2,1,0:T(8,128)(2,1)} %copy-done.6), calls=%async_computation.3 | async-start | bytes 4194304 | tf_op jit(solution)/shard_map/all_to_all | solution.py:409
  162.6 4.4 %copy-start.18 = (f32[128]{0:T(128)S(1)}, f32[128]{0:T(128)}, u32[]{:S(2)}) copy-start(f32[128]{0:T(128)} %param.26) | copy-start | bytes 1540
  162.6 35.3 %all-to-all-start.4 = ((bf16[128,8,1024]{2,1,0:T(8,128)(2,1)}), bf16[128,8,1024]{2,1,0:T(8,128)(2,1)S(1)}, u32[]{:S(2)}, u32[]{:S(2)}) async-start(bf16[128,8,1024]{2,1,0:T(8,128)(2,1)} %fusion), calls=%async_computation.4 | async-start | bytes 4194304 | tf_op jit(solution)/shard_map/all_to_all | solution.py:422
  167.7 1.7 copy-start.15
  197.8 1.3 copy-start.16
  (1 other events, 1.0 us)

commit v6 on v5

--- a/solution.py
+++ b/solution.py
@@ -256,7 +256,9 @@
                 )
     for lane in range(0, cols, 128):
         send_ref[:, :, lane : lane + 128] = (
-            rows_buf[lane // 128].reshape(channels, 2 * rows, 128).astype(jnp.bfloat16)
+            rows_buf[lane // 128, : channels * 2 * rows, :]
+            .reshape(channels, 2 * rows, 128)
+            .astype(jnp.bfloat16)
         )
 
 
@@ -288,7 +290,7 @@
             jax.ShapeDtypeStruct((channels, 2 * rows, length), jnp.bfloat16),
         ],
         scratch_shapes=[
-            pltpu.VMEM((cols // 128, channels * 2 * rows, 128), jnp.float32),
+            pltpu.VMEM((cols // 128, (channels + 1) * 2 * rows, 128), jnp.float32),
             pltpu.VMEM((len(weights) * channels, width), jnp.bfloat16),
         ],
         compiler_params=pltpu.CompilerParams(vmem_limit_bytes=18 * MIB),
@@ -308,7 +310,7 @@
         center = values - jnp.mean(values, axis=0, keepdims=True)
         spread = jnp.mean(center * center, axis=0, keepdims=True)
         scaled = center * (1.0 / jnp.sqrt(spread + 1e-05))
-        rows_buf[...] = scaled.reshape(channels * rows, 128)
+        rows_buf[: channels * rows, :] = scaled.reshape(channels * rows, 128)
         normed = jnp.concatenate(
             [rows_buf[pl.ds(row, channels, stride=rows), :] * gain_ref[...] for row in range(rows)],
             axis=1,
@@ -339,7 +341,7 @@
         + [whole((channels, 1)), whole(weight.shape)],
         out_specs=pl.BlockSpec((rows, cols, width), lambda i: (0, i, 0)),
         out_shape=jax.ShapeDtypeStruct((rows, length, width), jnp.bfloat16),
-        scratch_shapes=[pltpu.VMEM((channels * rows, 128), jnp.float32)],
+        scratch_shapes=[pltpu.VMEM(((channels + 1) * rows, 128), jnp.float32)],
         compiler_params=pltpu.CompilerParams(vmem_limit_bytes=56 * MIB),
         cost_estimate=pl.CostEstimate(
             flops=2 * rows * length * width * channels,

time: 206 us -> 206 us (level)
  no operation moved by 1% of the time
where the time goes in v6:
time: 206 us
  waiting for transfers between devices  68.6 us (33%)
  blocking collectives  46.8 us (23%)
  Pallas kernels  41.1 us (20%)
  starting transfers between devices  25.7 us (12%)
  matrix products  11.8 us (6%)
  local copies, waits for them, and re-layouts  11.4 us (6%)
    all_to_all x1, blocking collectives, body(): lax.all_to_all(payload, ('dap', 'chip'), split_axis=0, concat_axis=0, til...  46.8 us
    all_to_all x2, waiting for transfers between devices, body(): lax.all_to_all(send, ALL, split_axis=0, concat_axis=0, tiled=True)  36.1 us
    all_to_all x1, waiting for transfers between devices, body(): lax.all_to_all(mixed.reshape(devices, rows, length), ALL, split_axis=0, c...  26.7 us
    pallas_call x4, Pallas kernels, opm_rows(): pl.pallas_call(functools.partial(opm_kernel, own), grid=(rows // step_row...  20.6 us
    all_to_all x2, starting transfers between devices, body(): lax.all_to_all(send, ALL, split_axis=0, concat_axis=0, tiled=True)  12 us
    unnamed x38, local copies, waits for them, and re-layouts  10.5 us
    pallas_call x2, Pallas kernels, pair_operands(): pl.pallas_call(functools.partial(pair_kernel, scale), grid=(length // col...  9.28 us
    pallas_call x1, Pallas kernels, result_rows(): pl.pallas_call(result_kernel, grid=(length // cols,), in_specs=[pl.BlockS...  6.42 us
  transfers between devices with their start and end apart: 6, of which 4 were waited for; matrix products, arithmetic and copies ran while one was open for 4% of the time, Pallas kernels for 15%

profile of v6, /device:TPU:1, one launch (start us, length us, event | category | flops | bytes accessed | tf_op | source)
XLA Modules:
  0.0 205.6 jit_solution(2527571081531896953)
XLA Ops:
  0.0 4.8 %shard_map.136 = (bf16[64,80,256]{2,1,0:T(8,128)(2,1)}, bf16[64,64,256]{2,1,0:T(8,128)(2,1)}) custom-call(bf16[8,128,256]{2,1,0:T(8,128)(2,1)} %msa_ref.1, f32[1,256]{1,0:T(1,128)} %bitcast.43, bf16[32,256]{1,0:T(8,128)(2,1)} %bitcast.41, bf16[32,256]{1,0:T(8,128)(2,1)} %bitcast.42), custom_call_target="tpu_custom_call" | custom-call | tf_op jit(solution)/shard_map/pallas_call | solution.py:96
  4.8 46.8 %all_to_all.25 = bf16[64,80,256]{2,1,0:T(8,128)(2,1)S(1)} all-to-all(bf16[64,80,256]{2,1,0:T(8,128)(2,1)} %get-tuple-element.13), channel_id=1, replica_groups=mesh['dap'=8,'chip'=8,'core'=2] {'dap','chip'}, dimensions={0} | all-to-all | bytes 5242880 | tf_op jit(solution)/shard_map/all_to_all | solution.py:388
  51.5 5.7 %all-to-all-start.2 = ((bf16[64,64,256]{2,1,0:T(8,128)(2,1)}), bf16[64,64,256]{2,1,0:T(8,128)(2,1)}, u32[]{:S(2)}, u32[]{:S(2)}) async-start(bf16[64,64,256]{2,1,0:T(8,128)(2,1)} %get-tuple-element.15), calls=%async_computation.2 | async-start | bytes 4194304 | tf_op jit(solution)/shard_map/all_to_all | solution.py:388
  57.5 4.9 %shard_map.138 = bf16[8,512,128]{2,1,0:T(8,128)(2,1)S(1)} custom-call(s32[2]{0:T(128)S(1)} %pad_add_fusion.place_ref, bf16[8,8,80,256]{3,2,1,0:T(8,128)(2,1)S(1)} %bitcast.33, bf16[8,8,80,256]{3,2,1,0:T(8,128)(2,1)S(1)} %bitcast.34, bf16[32,4096]{1,0:T(8,128)(2,1)S(1)} %reshape.40.weight_ref), custom_call_target="tpu_custom_call" | custom-call | flops 2147483648 | bytes 3670016 | tf_op jit(solution)/shard_map/pallas_call | solution.py:192
  62.4 2.1 %collective-permute-start = (bf16[8,512,128]{2,1,0:T(8,128)(2,1)S(1)}, bf16[8,512,128]{2,1,0:T(8,128)(2,1)S(1)}, u32[]{:S(2)}, u32[]{:S(2)}) collective-permute-start(bf16[8,512,128]{2,1,0:T(8,128)(2,1)S(1)} %shard_map.138), channel_id=1, source_target_pairs={{0,1},{1,0},{2,3},{3,2},{4,5},{5,4},{6,7},{7,6},{8,9},{9,8},{10,11... | collective-permute-start | bytes 3145736 | tf_op jit(solution)/shard_map/ppermute | solution.py:402
  64.5 1.7 copy-done.3
  66.3 5.0 %shard_map.137.own_ref = bf16[8,512,128]{2,1,0:T(8,128)(2,1)S(1)} custom-call(s32[2]{0:T(128)S(1)} %pad_add_fusion.place_ref, bf16[8,8,80,256]{3,2,1,0:T(8,128)(2,1)S(1)} %bitcast.35, bf16[8,8,80,256]{3,2,1,0:T(8,128)(2,1)S(1)} %bitcast.36, bf16[32,4096]{1,0:T(8,128)(2,1)S(1)} %reshape.40.weight_ref), custom_call_target="tpu_custom_call" | custom-call | flops 2147483648 | bytes 3670016 | tf_op jit(solution)/shard_map/pallas_call | solution.py:192
  71.3 4.6 %shard_map.139 = (bf16[8,512,128]{2,1,0:T(8,128)(2,1)S(1)}, bf16[8,512,128]{2,1,0:T(8,128)(2,1)S(1)}, bf16[128,16,512]{2,1,0:T(8,128)(2,1)S(1)}) custom-call(bf16[8,8,128,128]{3,2,1,0:T(8,128)(2,1)S(1)} %bitcast.31, bf16[8,512,128]{2,1,0:T(8,128)(2,1)S(1)} %shard_map.137.own_ref, bf16[8,512,128]{2,1,0:T(8,128)(2,1)S(1)} %collective-permute-done.arrived_ref, ...), custom_call_target="tpu_custom_call" | custom-call | flops 536870912 | bytes 9437184 | tf_op jit(solution)/shard_map/pallas_call | solution.py:272
  79.3 5.8 %all-to-all-done.2 = bf16[64,64,256]{2,1,0:T(8,128)(2,1)} async-done(((bf16[64,64,256]{2,1,0:T(8,128)(2,1)}), bf16[64,64,256]{2,1,0:T(8,128)(2,1)}, u32[]{:S(2)}, u32[]{:S(2)}) %all-to-all-start.2) | async-done | bytes 2097184 | tf_op jit(solution)/shard_map/all_to_all | solution.py:388
  85.1 7.6 %all-to-all-start.1 = ((bf16[128,16,512]{2,1,0:T(8,128)(2,1)}), bf16[128,16,512]{2,1,0:T(8,128)(2,1)}, u32[]{:S(2)}, u32[]{:S(2)}) async-start(bf16[128,16,512]{2,1,0:T(8,128)(2,1)} %copy-done.5), calls=%async_computation.1 | async-start | bytes 4194304 | tf_op jit(solution)/shard_map/all_to_all | solution.py:411
  92.7 1.7 copy-done.4
  94.4 5.4 %shard_map.141 = bf16[8,512,128]{2,1,0:T(8,128)(2,1)S(1)} custom-call(s32[2]{0:T(128)S(1)} %pad_add_fusion.place_ref, bf16[8,8,64,256]{3,2,1,0:T(8,128)(2,1)} %bitcast.10.gathered_ref, bf16[8,8,80,256]{3,2,1,0:T(8,128)(2,1)S(1)} %bitcast.37, bf16[32,4096]{1,0:T(8,128)(2,1)S(1)} %reshape.40.weight_ref), custom_call_target="tpu_custom_call" | custom-call | flops 2147483648 | bytes 3145728 | tf_op jit(solution)/shard_map/pallas_call | solution.py:192
  101.3 5.4 %shard_map.140.own_ref = bf16[8,512,128]{2,1,0:T(8,128)(2,1)S(1)} custom-call(s32[2]{0:T(128)S(1)} %pad_add_fusion.place_ref, bf16[8,8,64,256]{3,2,1,0:T(8,128)(2,1)} %bitcast.10.gathered_ref, bf16[8,8,80,256]{3,2,1,0:T(8,128)(2,1)S(1)} %bitcast.38, bf16[32,4096]{1,0:T(8,128)(2,1)S(1)} %reshape.40.weight_ref), custom_call_target="tpu_custom_call" | custom-call | flops 2147483648 | bytes 3145728 | tf_op jit(solution)/shard_map/pallas_call | solution.py:192
  106.7 4.6 %shard_map.142 = (bf16[8,512,128]{2,1,0:T(8,128)(2,1)S(1)}, bf16[8,512,128]{2,1,0:T(8,128)(2,1)S(1)}, bf16[128,16,512]{2,1,0:T(8,128)(2,1)S(1)}) custom-call(bf16[8,8,128,128]{3,2,1,0:T(8,128)(2,1)S(1)} %bitcast.32, bf16[8,512,128]{2,1,0:T(8,128)(2,1)S(1)} %shard_map.140.own_ref, bf16[8,512,128]{2,1,0:T(8,128)(2,1)S(1)} %collective-permute-done.1.arrived_ref, ...), custom_call_target="tpu_custom_call" | custom-call | flops 536870912 | bytes 9437184 | tf_op jit(solution)/shard_map/pallas_call | solution.py:272
  113.7 9.5 %all-to-all-done.1 = bf16[128,16,512]{2,1,0:T(8,128)(2,1)} async-done(((bf16[128,16,512]{2,1,0:T(8,128)(2,1)}), bf16[128,16,512]{2,1,0:T(8,128)(2,1)}, u32[]{:S(2)}, u32[]{:S(2)}) %all-to-all-start.1) | async-done | bytes 2097184 | tf_op jit(solution)/shard_map/all_to_all | solution.py:411
  123.2 4.4 %all-to-all-start.3 = ((bf16[128,16,512]{2,1,0:T(8,128)(2,1)}), bf16[128,16,512]{2,1,0:T(8,128)(2,1)S(1)}, u32[]{:S(2)}, u32[]{:S(2)}) async-start(bf16[128,16,512]{2,1,0:T(8,128)(2,1)} %copy-done.6), calls=%async_computation.3 | async-start | bytes 4194304 | tf_op jit(solution)/shard_map/all_to_all | solution.py:411
  127.6 4.1 %convolution_convert_fusion = bf16[1024,1024]{1,0:T(8,128)(2,1)} fusion(bf16[128,16,512]{2,1,0:T(8,128)(2,1)} %all-to-all-done.1), kind=kOutput, calls=%fused_computation.3 | convolution fusion | flops 1074790400 | bytes 4194304 | tf_op jit(solution)/shard_map/dot_general | solution.py:422
  131.8 26.6 %all-to-all-done.3 = bf16[128,16,512]{2,1,0:T(8,128)(2,1)S(1)} async-done(((bf16[128,16,512]{2,1,0:T(8,128)(2,1)}), bf16[128,16,512]{2,1,0:T(8,128)(2,1)S(1)}, u32[]{:S(2)}, u32[]{:S(2)}) %all-to-all-start.3) | async-done | bytes 2097184 | tf_op jit(solution)/shard_map/all_to_all | solution.py:411
  158.3 4.2 %fusion = bf16[128,8,1024]{2,1,0:T(8,128)(2,1)} fusion(bf16[1024,1024]{1,0:T(8,128)(2,1)} %convolution_convert_fusion, bf16[128,16,512]{2,1,0:T(8,128)(2,1)S(1)} %all-to-all-done.3), kind=kOutput, calls=%fused_computation.4 | convolution fusion | flops 1076887552 | bytes 6291456 | tf_op jit(solution)/shard_map/dot_general | solution.py:423
  162.6 4.4 %all-to-all-start.4 = ((bf16[128,8,1024]{2,1,0:T(8,128)(2,1)}), bf16[128,8,1024]{2,1,0:T(8,128)(2,1)S(1)}, u32[]{:S(2)}, u32[]{:S(2)}) async-start(bf16[128,8,1024]{2,1,0:T(8,128)(2,1)} %fusion), calls=%async_computation.4 | async-start | bytes 4194304 | tf_op jit(solution)/shard_map/all_to_all | solution.py:424
  167.7 1.7 divide_convert_fusion.refs_3_
  169.4 1.7 divide_convert_fusion.1.refs_1_
  171.1 26.7 %all-to-all-done.4.mixed_ref = bf16[128,8,1024]{2,1,0:T(8,128)(2,1)S(1)} async-done(((bf16[128,8,1024]{2,1,0:T(8,128)(2,1)}), bf16[128,8,1024]{2,1,0:T(8,128)(2,1)S(1)}, u32[]{:S(2)}, u32[]{:S(2)}) %all-to-all-start.4) | async-done | bytes 2097184 | tf_op jit(solution)/shard_map/all_to_all | solution.py:424
  199.2 6.4 %shard_map.143 = bf16[8,1024,128]{2,1,0:T(8,128)(2,1)} custom-call(bf16[128,8,1024]{2,1,0:T(8,128)(2,1)} %copy-done.16, bf16[8,512,128]{2,1,0:T(8,128)(2,1)} %copy-done.7, bf16[8,512,128]{2,1,0:T(8,128)(2,1)} %divide_convert_fusion.1.refs_1_, bf16[8,512,128]{2,1,0:T(8,128)(2,1)} %copy-done.8, bf16[8,512,128]{2,1,0:T(8,128)(2,1)} %divide_convert_fusion.refs_3_, ...), custom_call_target="tpu_custom_call" | custom-call | flops 268435456 | bytes 8388608 | tf_op jit(solution)/shard_map/pallas_call | solution.py:336
  (42 shorter events, 9.5 us)
Async XLA Ops:
  0.0 167.7 %copy-start = (bf16[128,128]{1,0:T(8,128)(2,1)S(1)}, bf16[128,128]{1,0:T(8,128)(2,1)}, u32[]{:S(2)}) copy-start(bf16[128,128]{1,0:T(8,128)(2,1)} %param.25) | copy-start | bytes 98308
  51.5 5.9 %copy-start.2 = (bf16[64,80,256]{2,1,0:T(8,128)(2,1)}, bf16[64,80,256]{2,1,0:T(8,128)(2,1)S(1)}, u32[]{:S(2)}) copy-start(bf16[64,80,256]{2,1,0:T(8,128)(2,1)S(1)} %all_to_all.25) | copy-start | bytes 7864324
  51.5 5.7 %copy-start.17 = (bf16[1024,128]{1,0:T(8,128)(2,1)S(1)}, bf16[1024,128]{1,0:T(8,128)(2,1)}, u32[]{:S(2)}) copy-start(bf16[1024,128]{1,0:T(8,128)(2,1)} %param.19) | copy-start | bytes 786436
  51.5 33.6 %all-to-all-start.2 = ((bf16[64,64,256]{2,1,0:T(8,128)(2,1)}), bf16[64,64,256]{2,1,0:T(8,128)(2,1)}, u32[]{:S(2)}, u32[]{:S(2)}) async-start(bf16[64,64,256]{2,1,0:T(8,128)(2,1)} %get-tuple-element.15), calls=%async_computation.2 | async-start | bytes 4194304 | tf_op jit(solution)/shard_map/all_to_all | solution.py:388
  62.4 8.8 %copy-start.1 = (bf16[8,1024,128]{2,1,0:T(8,128)(2,1)S(1)}, bf16[8,1024,128]{2,1,0:T(8,128)(2,1)}, u32[]{:S(2)}) copy-start(bf16[8,1024,128]{2,1,0:T(8,128)(2,1)} %param.15) | copy-start | bytes 6291460
  62.4 8.8 %collective-permute-start = (bf16[8,512,128]{2,1,0:T(8,128)(2,1)S(1)}, bf16[8,512,128]{2,1,0:T(8,128)(2,1)S(1)}, u32[]{:S(2)}, u32[]{:S(2)}) collective-permute-start(bf16[8,512,128]{2,1,0:T(8,128)(2,1)S(1)} %shard_map.138), channel_id=1, source_target_pairs={{0,1},{1,0},{2,3},{3,2},{4,5},{5,4},{6,7},{7,6},{8,9},{9,8},{10,11... | collective-permute-start | bytes 3145736 | tf_op jit(solution)/shard_map/ppermute | solution.py:402
  64.5 1.7 copy-start.3
  66.2 5.0 %copy-start.9 = (bf16[128,128]{1,0:T(8,128)(2,1)S(1)}, bf16[128,128]{1,0:T(8,128)(2,1)}, u32[]{:S(2)}) copy-start(bf16[128,128]{1,0:T(8,128)(2,1)} %rest_0_.3) | copy-start | bytes 98308
  66.2 5.0 %copy-start.10 = (bf16[128,128]{1,0:T(8,128)(2,1)S(1)}, bf16[128,128]{1,0:T(8,128)(2,1)}, u32[]{:S(2)}) copy-start(bf16[128,128]{1,0:T(8,128)(2,1)} %rest_1_.3) | copy-start | bytes 98308
  66.2 5.0 %copy-start.11 = (bf16[128,128]{1,0:T(8,128)(2,1)S(1)}, bf16[128,128]{1,0:T(8,128)(2,1)}, u32[]{:S(2)}) copy-start(bf16[128,128]{1,0:T(8,128)(2,1)} %rest_2_.3) | copy-start | bytes 98308
  66.3 5.0 %copy-start.12 = (bf16[128,128]{1,0:T(8,128)(2,1)S(1)}, bf16[128,128]{1,0:T(8,128)(2,1)}, u32[]{:S(2)}) copy-start(bf16[128,128]{1,0:T(8,128)(2,1)} %rest_3_.3) | copy-start | bytes 98308
  66.3 5.0 %copy-start.13 = (f32[128]{0:T(128)S(1)}, f32[128]{0:T(128)}, u32[]{:S(2)}) copy-start(f32[128]{0:T(128)} %param.20) | copy-start | bytes 1540
  76.0 1.4 copy-start.5
  78.3 1.0 copy-start.14
  85.1 38.1 %all-to-all-start.1 = ((bf16[128,16,512]{2,1,0:T(8,128)(2,1)}), bf16[128,16,512]{2,1,0:T(8,128)(2,1)}, u32[]{:S(2)}, u32[]{:S(2)}) async-start(bf16[128,16,512]{2,1,0:T(8,128)(2,1)} %copy-done.5), calls=%async_computation.1 | async-start | bytes 4194304 | tf_op jit(solution)/shard_map/all_to_all | solution.py:411
  92.7 1.7 copy-start.4
  99.8 6.9 %collective-permute-start.1 = (bf16[8,512,128]{2,1,0:T(8,128)(2,1)S(1)}, bf16[8,512,128]{2,1,0:T(8,128)(2,1)S(1)}, u32[]{:S(2)}, u32[]{:S(2)}) collective-permute-start(bf16[8,512,128]{2,1,0:T(8,128)(2,1)S(1)} %shard_map.141), channel_id=1, source_target_pairs={{0,1},{1,0},{2,3},{3,2},{4,5},{5,4},{6,7},{7,6},{8,9},{9,8},{10,11... | collective-permute-start | bytes 3145736 | tf_op jit(solution)/shard_map/ppermute | solution.py:402
  111.4 1.3 copy-start.6
  112.7 1.0 copy-start.8
  123.2 35.1 %all-to-all-start.3 = ((bf16[128,16,512]{2,1,0:T(8,128)(2,1)}), bf16[128,16,512]{2,1,0:T(8,128)(2,1)S(1)}, u32[]{:S(2)}, u32[]{:S(2)}) async-start(bf16[128,16,512]{2,1,0:T(8,128)(2,1)} %copy-done.6), calls=%async_computation.3 | async-start | bytes 4194304 | tf_op jit(solution)/shard_map/all_to_all | solution.py:411
  162.6 4.4 %copy-start.18 = (f32[128]{0:T(128)S(1)}, f32[128]{0:T(128)}, u32[]{:S(2)}) copy-start(f32[128]{0:T(128)} %param.26) | copy-start | bytes 1540
  162.6 35.3 %all-to-all-start.4 = ((bf16[128,8,1024]{2,1,0:T(8,128)(2,1)}), bf16[128,8,1024]{2,1,0:T(8,128)(2,1)S(1)}, u32[]{:S(2)}, u32[]{:S(2)}) async-start(bf16[128,8,1024]{2,1,0:T(8,128)(2,1)} %fusion), calls=%async_computation.4 | async-start | bytes 4194304 | tf_op jit(solution)/shard_map/all_to_all | solution.py:424
  167.7 1.7 copy-start.15
  197.8 1.3 copy-start.16
  (1 other events, 1.0 us)

commit v7 on v6

--- a/solution.py
+++ b/solution.py
@@ -49,39 +49,49 @@
     same_pair = (target // left_rows == source // left_rows) & (
         target // seqs % 2 == source % 2
     )
+    def replicated(block, send_ref, k):
+        return [
+            pltpu.make_async_copy(
+                block, send_ref.at[pl.ds(group * chips, chips)], sems.at[k, group]
+            )
+            for group in range(send_ref.shape[0] // chips)
+        ]
+
     right = jnp.zeros((cols, width), jnp.float32)
+    normed = []
+    for s in range(seqs):
+        normed.append(
+            standardize_features(msa_ref[s].astype(jnp.float32), gain_ref[...]).astype(
+                jnp.bfloat16
+            )
+        )
+        right = right + jnp.dot(
+            normed[s],
+            jnp.where(right_lane == s, right_copies, 0.0).astype(jnp.bfloat16),
+            preferred_element_type=jnp.float32,
+        )
+    right = right.astype(jnp.bfloat16)
+    for chip in range(chips):
+        second[chip] = right[part:]
+    second_copies = replicated(second, second_ref, 1)
+    for copy in second_copies:
+        copy.start()
     left = jnp.zeros((chips * left_rows, width), jnp.float32)
     for s in range(seqs):
-        normed = standardize_features(msa_ref[s].astype(jnp.float32), gain_ref[...]).astype(
-            jnp.bfloat16
-        )
-        right = right + jnp.dot(
-            normed,
-            jnp.where(right_lane == s, right_copies, 0.0).astype(jnp.bfloat16),
-            preferred_element_type=jnp.float32,
-        )
-        products = jnp.dot(normed, left_copies, preferred_element_type=jnp.float32)
+        products = jnp.dot(normed[s], left_copies, preferred_element_type=jnp.float32)
         left = left + jnp.dot(
             ones_where(same_pair & (target % seqs == s)),
             jnp.where(own_lane, products, 0.0).astype(jnp.bfloat16),
             preferred_element_type=jnp.float32,
         )
-    right = right.astype(jnp.bfloat16)
     left = left.astype(jnp.bfloat16)
     for chip in range(chips):
         first[chip, :part, :] = right[:part]
         first[chip, part:, :] = left[chip * left_rows : (chip + 1) * left_rows]
-        second[chip] = right[part:]
-    copies = [
-        pltpu.make_async_copy(
-            block, send_ref.at[pl.ds(group * chips, chips)], sems.at[k, group]
-        )
-        for k, (block, send_ref) in enumerate(((first, first_ref), (second, second_ref)))
-        for group in range(first_ref.shape[0] // chips)
-    ]
-    for copy in copies:
+    first_copies = replicated(first, first_ref, 0)
+    for copy in first_copies:
         copy.start()
-    for copy in copies:
+    for copy in second_copies + first_copies:
         copy.wait()
 
 

time: 206 us -> 206 us (level)
  no operation moved by 1% of the time
where the time goes in v7:
time: 206 us; the launch traced here: 205 us
  waiting for transfers between devices  68.5 us (33%)
  blocking collectives  46.8 us (23%)
  Pallas kernels  40.7 us (20%)
  starting transfers between devices  25.8 us (13%)
  matrix products  11.8 us (6%)
  local copies, waits for them, and re-layouts  11.4 us (6%)
    all_to_all x1, blocking collectives, body(): lax.all_to_all(payload, ('dap', 'chip'), split_axis=0, concat_axis=0, til...  46.8 us
    all_to_all x2, waiting for transfers between devices, body(): lax.all_to_all(send, ALL, split_axis=0, concat_axis=0, tiled=True)  36.1 us
    all_to_all x1, waiting for transfers between devices, body(): lax.all_to_all(mixed.reshape(devices, rows, length), ALL, split_axis=0, c...  26.7 us
    pallas_call x4, Pallas kernels, opm_rows(): pl.pallas_call(functools.partial(opm_kernel, own), grid=(rows // step_row...  20.6 us
    all_to_all x2, starting transfers between devices, body(): lax.all_to_all(send, ALL, split_axis=0, concat_axis=0, tiled=True)  12 us
    unnamed x38, local copies, waits for them, and re-layouts  10.5 us
    pallas_call x2, Pallas kernels, pair_operands(): pl.pallas_call(functools.partial(pair_kernel, scale), grid=(length // col...  9.3 us
    pallas_call x1, Pallas kernels, result_rows(): pl.pallas_call(result_kernel, grid=(length // cols,), in_specs=[pl.BlockS...  6.42 us
  transfers between devices with their start and end apart: 6, of which 4 were waited for; matrix products, arithmetic and copies ran while one was open for 4% of the time, Pallas kernels for 15%

profile of v7, /device:TPU:1, one launch (start us, length us, event | category | flops | bytes accessed | tf_op | source)
XLA Modules:
  0.0 205.2 jit_solution(7202168900366187373)
XLA Ops:
  0.0 4.3 %shard_map.136 = (bf16[64,80,256]{2,1,0:T(8,128)(2,1)}, bf16[64,64,256]{2,1,0:T(8,128)(2,1)}) custom-call(bf16[8,128,256]{2,1,0:T(8,128)(2,1)} %msa_ref.1, f32[1,256]{1,0:T(1,128)} %bitcast.43, bf16[32,256]{1,0:T(8,128)(2,1)} %bitcast.41, bf16[32,256]{1,0:T(8,128)(2,1)} %bitcast.42), custom_call_target="tpu_custom_call" | custom-call | tf_op jit(solution)/shard_map/pallas_call | solution.py:106
  4.4 46.8 %all_to_all.25 = bf16[64,80,256]{2,1,0:T(8,128)(2,1)S(1)} all-to-all(bf16[64,80,256]{2,1,0:T(8,128)(2,1)} %get-tuple-element.13), channel_id=1, replica_groups=mesh['dap'=8,'chip'=8,'core'=2] {'dap','chip'}, dimensions={0} | all-to-all | bytes 5242880 | tf_op jit(solution)/shard_map/all_to_all | solution.py:398
  51.1 5.7 %all-to-all-start.2 = ((bf16[64,64,256]{2,1,0:T(8,128)(2,1)}), bf16[64,64,256]{2,1,0:T(8,128)(2,1)}, u32[]{:S(2)}, u32[]{:S(2)}) async-start(bf16[64,64,256]{2,1,0:T(8,128)(2,1)} %get-tuple-element.15), calls=%async_computation.2 | async-start | bytes 4194304 | tf_op jit(solution)/shard_map/all_to_all | solution.py:398
  57.1 4.9 %shard_map.138 = bf16[8,512,128]{2,1,0:T(8,128)(2,1)S(1)} custom-call(s32[2]{0:T(128)S(1)} %pad_add_fusion.place_ref, bf16[8,8,80,256]{3,2,1,0:T(8,128)(2,1)S(1)} %bitcast.33, bf16[8,8,80,256]{3,2,1,0:T(8,128)(2,1)S(1)} %bitcast.34, bf16[32,4096]{1,0:T(8,128)(2,1)S(1)} %reshape.40.weight_ref), custom_call_target="tpu_custom_call" | custom-call | flops 2147483648 | bytes 3670016 | tf_op jit(solution)/shard_map/pallas_call | solution.py:202
  62.0 2.1 %collective-permute-start = (bf16[8,512,128]{2,1,0:T(8,128)(2,1)S(1)}, bf16[8,512,128]{2,1,0:T(8,128)(2,1)S(1)}, u32[]{:S(2)}, u32[]{:S(2)}) collective-permute-start(bf16[8,512,128]{2,1,0:T(8,128)(2,1)S(1)} %shard_map.138), channel_id=1, source_target_pairs={{0,1},{1,0},{2,3},{3,2},{4,5},{5,4},{6,7},{7,6},{8,9},{9,8},{10,11... | collective-permute-start | bytes 3145736 | tf_op jit(solution)/shard_map/ppermute | solution.py:412
  64.1 1.7 copy-done.3
  65.9 5.0 %shard_map.137.own_ref = bf16[8,512,128]{2,1,0:T(8,128)(2,1)S(1)} custom-call(s32[2]{0:T(128)S(1)} %pad_add_fusion.place_ref, bf16[8,8,80,256]{3,2,1,0:T(8,128)(2,1)S(1)} %bitcast.35, bf16[8,8,80,256]{3,2,1,0:T(8,128)(2,1)S(1)} %bitcast.36, bf16[32,4096]{1,0:T(8,128)(2,1)S(1)} %reshape.40.weight_ref), custom_call_target="tpu_custom_call" | custom-call | flops 2147483648 | bytes 3670016 | tf_op jit(solution)/shard_map/pallas_call | solution.py:202
  70.9 4.6 %shard_map.139 = (bf16[8,512,128]{2,1,0:T(8,128)(2,1)S(1)}, bf16[8,512,128]{2,1,0:T(8,128)(2,1)S(1)}, bf16[128,16,512]{2,1,0:T(8,128)(2,1)S(1)}) custom-call(bf16[8,8,128,128]{3,2,1,0:T(8,128)(2,1)S(1)} %bitcast.31, bf16[8,512,128]{2,1,0:T(8,128)(2,1)S(1)} %shard_map.137.own_ref, bf16[8,512,128]{2,1,0:T(8,128)(2,1)S(1)} %collective-permute-done.arrived_ref, ...), custom_call_target="tpu_custom_call" | custom-call | flops 536870912 | bytes 9437184 | tf_op jit(solution)/shard_map/pallas_call | solution.py:282
  78.9 5.8 %all-to-all-done.2 = bf16[64,64,256]{2,1,0:T(8,128)(2,1)} async-done(((bf16[64,64,256]{2,1,0:T(8,128)(2,1)}), bf16[64,64,256]{2,1,0:T(8,128)(2,1)}, u32[]{:S(2)}, u32[]{:S(2)}) %all-to-all-start.2) | async-done | bytes 2097184 | tf_op jit(solution)/shard_map/all_to_all | solution.py:398
  84.7 7.6 %all-to-all-start.1 = ((bf16[128,16,512]{2,1,0:T(8,128)(2,1)}), bf16[128,16,512]{2,1,0:T(8,128)(2,1)}, u32[]{:S(2)}, u32[]{:S(2)}) async-start(bf16[128,16,512]{2,1,0:T(8,128)(2,1)} %copy-done.5), calls=%async_computation.1 | async-start | bytes 4194304 | tf_op jit(solution)/shard_map/all_to_all | solution.py:421
  92.3 1.7 copy-done.4
  94.0 5.3 %shard_map.141 = bf16[8,512,128]{2,1,0:T(8,128)(2,1)S(1)} custom-call(s32[2]{0:T(128)S(1)} %pad_add_fusion.place_ref, bf16[8,8,64,256]{3,2,1,0:T(8,128)(2,1)} %bitcast.10.gathered_ref, bf16[8,8,80,256]{3,2,1,0:T(8,128)(2,1)S(1)} %bitcast.37, bf16[32,4096]{1,0:T(8,128)(2,1)S(1)} %reshape.40.weight_ref), custom_call_target="tpu_custom_call" | custom-call | flops 2147483648 | bytes 3145728 | tf_op jit(solution)/shard_map/pallas_call | solution.py:202
  100.9 5.4 %shard_map.140.own_ref = bf16[8,512,128]{2,1,0:T(8,128)(2,1)S(1)} custom-call(s32[2]{0:T(128)S(1)} %pad_add_fusion.place_ref, bf16[8,8,64,256]{3,2,1,0:T(8,128)(2,1)} %bitcast.10.gathered_ref, bf16[8,8,80,256]{3,2,1,0:T(8,128)(2,1)S(1)} %bitcast.38, bf16[32,4096]{1,0:T(8,128)(2,1)S(1)} %reshape.40.weight_ref), custom_call_target="tpu_custom_call" | custom-call | flops 2147483648 | bytes 3145728 | tf_op jit(solution)/shard_map/pallas_call | solution.py:202
  106.3 4.7 %shard_map.142 = (bf16[8,512,128]{2,1,0:T(8,128)(2,1)S(1)}, bf16[8,512,128]{2,1,0:T(8,128)(2,1)S(1)}, bf16[128,16,512]{2,1,0:T(8,128)(2,1)S(1)}) custom-call(bf16[8,8,128,128]{3,2,1,0:T(8,128)(2,1)S(1)} %bitcast.32, bf16[8,512,128]{2,1,0:T(8,128)(2,1)S(1)} %shard_map.140.own_ref, bf16[8,512,128]{2,1,0:T(8,128)(2,1)S(1)} %collective-permute-done.1.arrived_ref, ...), custom_call_target="tpu_custom_call" | custom-call | flops 536870912 | bytes 9437184 | tf_op jit(solution)/shard_map/pallas_call | solution.py:282
  113.3 9.5 %all-to-all-done.1 = bf16[128,16,512]{2,1,0:T(8,128)(2,1)} async-done(((bf16[128,16,512]{2,1,0:T(8,128)(2,1)}), bf16[128,16,512]{2,1,0:T(8,128)(2,1)}, u32[]{:S(2)}, u32[]{:S(2)}) %all-to-all-start.1) | async-done | bytes 2097184 | tf_op jit(solution)/shard_map/all_to_all | solution.py:421
  122.8 4.4 %all-to-all-start.3 = ((bf16[128,16,512]{2,1,0:T(8,128)(2,1)}), bf16[128,16,512]{2,1,0:T(8,128)(2,1)S(1)}, u32[]{:S(2)}, u32[]{:S(2)}) async-start(bf16[128,16,512]{2,1,0:T(8,128)(2,1)} %copy-done.6), calls=%async_computation.3 | async-start | bytes 4194304 | tf_op jit(solution)/shard_map/all_to_all | solution.py:421
  127.2 4.1 %convolution_convert_fusion = bf16[1024,1024]{1,0:T(8,128)(2,1)} fusion(bf16[128,16,512]{2,1,0:T(8,128)(2,1)} %all-to-all-done.1), kind=kOutput, calls=%fused_computation.3 | convolution fusion | flops 1074790400 | bytes 4194304 | tf_op jit(solution)/shard_map/dot_general | solution.py:432
  131.4 26.6 %all-to-all-done.3 = bf16[128,16,512]{2,1,0:T(8,128)(2,1)S(1)} async-done(((bf16[128,16,512]{2,1,0:T(8,128)(2,1)}), bf16[128,16,512]{2,1,0:T(8,128)(2,1)S(1)}, u32[]{:S(2)}, u32[]{:S(2)}) %all-to-all-start.3) | async-done | bytes 2097184 | tf_op jit(solution)/shard_map/all_to_all | solution.py:421
  157.9 4.2 %fusion = bf16[128,8,1024]{2,1,0:T(8,128)(2,1)} fusion(bf16[1024,1024]{1,0:T(8,128)(2,1)} %convolution_convert_fusion, bf16[128,16,512]{2,1,0:T(8,128)(2,1)S(1)} %all-to-all-done.3), kind=kOutput, calls=%fused_computation.4 | convolution fusion | flops 1076887552 | bytes 6291456 | tf_op jit(solution)/shard_map/dot_general | solution.py:433
  162.2 4.4 %all-to-all-start.4 = ((bf16[128,8,1024]{2,1,0:T(8,128)(2,1)}), bf16[128,8,1024]{2,1,0:T(8,128)(2,1)S(1)}, u32[]{:S(2)}, u32[]{:S(2)}) async-start(bf16[128,8,1024]{2,1,0:T(8,128)(2,1)} %fusion), calls=%async_computation.4 | async-start | bytes 4194304 | tf_op jit(solution)/shard_map/all_to_all | solution.py:434
  167.3 1.7 divide_convert_fusion.refs_3_
  169.0 1.7 divide_convert_fusion.1.refs_1_
  170.7 26.7 %all-to-all-done.4.mixed_ref = bf16[128,8,1024]{2,1,0:T(8,128)(2,1)S(1)} async-done(((bf16[128,8,1024]{2,1,0:T(8,128)(2,1)}), bf16[128,8,1024]{2,1,0:T(8,128)(2,1)S(1)}, u32[]{:S(2)}, u32[]{:S(2)}) %all-to-all-start.4) | async-done | bytes 2097184 | tf_op jit(solution)/shard_map/all_to_all | solution.py:434
  198.8 6.4 %shard_map.143 = bf16[8,1024,128]{2,1,0:T(8,128)(2,1)} custom-call(bf16[128,8,1024]{2,1,0:T(8,128)(2,1)} %copy-done.16, bf16[8,512,128]{2,1,0:T(8,128)(2,1)} %copy-done.7, bf16[8,512,128]{2,1,0:T(8,128)(2,1)} %divide_convert_fusion.1.refs_1_, bf16[8,512,128]{2,1,0:T(8,128)(2,1)} %copy-done.8, bf16[8,512,128]{2,1,0:T(8,128)(2,1)} %divide_convert_fusion.refs_3_, ...), custom_call_target="tpu_custom_call" | custom-call | flops 268435456 | bytes 8388608 | tf_op jit(solution)/shard_map/pallas_call | solution.py:346
  (42 shorter events, 9.5 us)
Async XLA Ops:
  0.0 167.3 %copy-start = (bf16[128,128]{1,0:T(8,128)(2,1)S(1)}, bf16[128,128]{1,0:T(8,128)(2,1)}, u32[]{:S(2)}) copy-start(bf16[128,128]{1,0:T(8,128)(2,1)} %param.25) | copy-start | bytes 98308
  51.1 5.9 %copy-start.2 = (bf16[64,80,256]{2,1,0:T(8,128)(2,1)}, bf16[64,80,256]{2,1,0:T(8,128)(2,1)S(1)}, u32[]{:S(2)}) copy-start(bf16[64,80,256]{2,1,0:T(8,128)(2,1)S(1)} %all_to_all.25) | copy-start | bytes 7864324
  51.1 5.7 %copy-start.17 = (bf16[1024,128]{1,0:T(8,128)(2,1)S(1)}, bf16[1024,128]{1,0:T(8,128)(2,1)}, u32[]{:S(2)}) copy-start(bf16[1024,128]{1,0:T(8,128)(2,1)} %param.19) | copy-start | bytes 786436
  51.1 33.5 %all-to-all-start.2 = ((bf16[64,64,256]{2,1,0:T(8,128)(2,1)}), bf16[64,64,256]{2,1,0:T(8,128)(2,1)}, u32[]{:S(2)}, u32[]{:S(2)}) async-start(bf16[64,64,256]{2,1,0:T(8,128)(2,1)} %get-tuple-element.15), calls=%async_computation.2 | async-start | bytes 4194304 | tf_op jit(solution)/shard_map/all_to_all | solution.py:398
  62.0 8.8 %copy-start.1 = (bf16[8,1024,128]{2,1,0:T(8,128)(2,1)S(1)}, bf16[8,1024,128]{2,1,0:T(8,128)(2,1)}, u32[]{:S(2)}) copy-start(bf16[8,1024,128]{2,1,0:T(8,128)(2,1)} %param.15) | copy-start | bytes 6291460
  62.0 8.8 %collective-permute-start = (bf16[8,512,128]{2,1,0:T(8,128)(2,1)S(1)}, bf16[8,512,128]{2,1,0:T(8,128)(2,1)S(1)}, u32[]{:S(2)}, u32[]{:S(2)}) collective-permute-start(bf16[8,512,128]{2,1,0:T(8,128)(2,1)S(1)} %shard_map.138), channel_id=1, source_target_pairs={{0,1},{1,0},{2,3},{3,2},{4,5},{5,4},{6,7},{7,6},{8,9},{9,8},{10,11... | collective-permute-start | bytes 3145736 | tf_op jit(solution)/shard_map/ppermute | solution.py:412
  64.1 1.7 copy-start.3
  65.8 5.0 %copy-start.9 = (bf16[128,128]{1,0:T(8,128)(2,1)S(1)}, bf16[128,128]{1,0:T(8,128)(2,1)}, u32[]{:S(2)}) copy-start(bf16[128,128]{1,0:T(8,128)(2,1)} %rest_0_.3) | copy-start | bytes 98308
  65.8 5.0 %copy-start.10 = (bf16[128,128]{1,0:T(8,128)(2,1)S(1)}, bf16[128,128]{1,0:T(8,128)(2,1)}, u32[]{:S(2)}) copy-start(bf16[128,128]{1,0:T(8,128)(2,1)} %rest_1_.3) | copy-start | bytes 98308
  65.8 5.0 %copy-start.11 = (bf16[128,128]{1,0:T(8,128)(2,1)S(1)}, bf16[128,128]{1,0:T(8,128)(2,1)}, u32[]{:S(2)}) copy-start(bf16[128,128]{1,0:T(8,128)(2,1)} %rest_2_.3) | copy-start | bytes 98308
  65.8 5.0 %copy-start.12 = (bf16[128,128]{1,0:T(8,128)(2,1)S(1)}, bf16[128,128]{1,0:T(8,128)(2,1)}, u32[]{:S(2)}) copy-start(bf16[128,128]{1,0:T(8,128)(2,1)} %rest_3_.3) | copy-start | bytes 98308
  65.8 5.0 %copy-start.13 = (f32[128]{0:T(128)S(1)}, f32[128]{0:T(128)}, u32[]{:S(2)}) copy-start(f32[128]{0:T(128)} %param.20) | copy-start | bytes 1540
  75.5 1.4 copy-start.5
  77.9 1.0 copy-start.14
  84.7 38.1 %all-to-all-start.1 = ((bf16[128,16,512]{2,1,0:T(8,128)(2,1)}), bf16[128,16,512]{2,1,0:T(8,128)(2,1)}, u32[]{:S(2)}, u32[]{:S(2)}) async-start(bf16[128,16,512]{2,1,0:T(8,128)(2,1)} %copy-done.5), calls=%async_computation.1 | async-start | bytes 4194304 | tf_op jit(solution)/shard_map/all_to_all | solution.py:421
  92.3 1.7 copy-start.4
  99.4 6.9 %collective-permute-start.1 = (bf16[8,512,128]{2,1,0:T(8,128)(2,1)S(1)}, bf16[8,512,128]{2,1,0:T(8,128)(2,1)S(1)}, u32[]{:S(2)}, u32[]{:S(2)}) collective-permute-start(bf16[8,512,128]{2,1,0:T(8,128)(2,1)S(1)} %shard_map.141), channel_id=1, source_target_pairs={{0,1},{1,0},{2,3},{3,2},{4,5},{5,4},{6,7},{7,6},{8,9},{9,8},{10,11... | collective-permute-start | bytes 3145736 | tf_op jit(solution)/shard_map/ppermute | solution.py:412
  111.0 1.3 copy-start.6
  112.3 1.0 copy-start.8
  122.8 35.1 %all-to-all-start.3 = ((bf16[128,16,512]{2,1,0:T(8,128)(2,1)}), bf16[128,16,512]{2,1,0:T(8,128)(2,1)S(1)}, u32[]{:S(2)}, u32[]{:S(2)}) async-start(bf16[128,16,512]{2,1,0:T(8,128)(2,1)} %copy-done.6), calls=%async_computation.3 | async-start | bytes 4194304 | tf_op jit(solution)/shard_map/all_to_all | solution.py:421
  162.2 4.4 %copy-start.18 = (f32[128]{0:T(128)S(1)}, f32[128]{0:T(128)}, u32[]{:S(2)}) copy-start(f32[128]{0:T(128)} %param.26) | copy-start | bytes 1540
  162.2 35.2 %all-to-all-start.4 = ((bf16[128,8,1024]{2,1,0:T(8,128)(2,1)}), bf16[128,8,1024]{2,1,0:T(8,128)(2,1)S(1)}, u32[]{:S(2)}, u32[]{:S(2)}) async-start(bf16[128,8,1024]{2,1,0:T(8,128)(2,1)} %fusion), calls=%async_computation.4 | async-start | bytes 4194304 | tf_op jit(solution)/shard_map/all_to_all | solution.py:434
  167.3 1.7 copy-start.15
  197.4 1.3 copy-start.16
  (1 other events, 1.0 us)

commit v8 on v7

--- a/solution.py
+++ b/solution.py
@@ -352,7 +352,7 @@
         out_specs=pl.BlockSpec((rows, cols, width), lambda i: (0, i, 0)),
         out_shape=jax.ShapeDtypeStruct((rows, length, width), jnp.bfloat16),
         scratch_shapes=[pltpu.VMEM(((channels + 1) * rows, 128), jnp.float32)],
-        compiler_params=pltpu.CompilerParams(vmem_limit_bytes=56 * MIB),
+        compiler_params=pltpu.CompilerParams(vmem_limit_bytes=52 * MIB),
         cost_estimate=pl.CostEstimate(
             flops=2 * rows * length * width * channels,
             bytes_accessed=rows * length * width * 8,

time: 206 us -> 205 us (level)
    unnamed x38 -> x40, local copies, waits for them, and re-layouts: 10.5 us -> 9.14 us
where the time goes in v8:
time: 205 us; the launch traced here: 204 us
  waiting for transfers between devices  67.5 us (33%)
  blocking collectives  46.8 us (23%)
  Pallas kernels  40.5 us (20%)
  starting transfers between devices  26.8 us (13%)
  matrix products  13.1 us (6%)
  local copies, waits for them, and re-layouts  9.37 us (5%)
    all_to_all x1, blocking collectives, body(): lax.all_to_all(payload, ('dap', 'chip'), split_axis=0, concat_axis=0, til...  46.8 us
    all_to_all x2, waiting for transfers between devices, body(): lax.all_to_all(send, ALL, split_axis=0, concat_axis=0, tiled=True)  35 us
    all_to_all x1, waiting for transfers between devices, body(): lax.all_to_all(mixed.reshape(devices, rows, length), ALL, split_axis=0, c...  25.7 us
    pallas_call x4, Pallas kernels, opm_rows(): pl.pallas_call(functools.partial(opm_kernel, own), grid=(rows // step_row...  20.6 us
    all_to_all x2, starting transfers between devices, body(): lax.all_to_all(send, ALL, split_axis=0, concat_axis=0, tiled=True)  12 us
    pallas_call x2, Pallas kernels, pair_operands(): pl.pallas_call(functools.partial(pair_kernel, scale), grid=(length // col...  9.29 us
    unnamed x40, local copies, waits for them, and re-layouts  9.14 us
    all_to_all x1, waiting for transfers between devices, body(): lax.all_to_all(payload, ('dap', 'chip'), split_axis=0, concat_axis=0, til...  6.81 us
  transfers between devices with their start and end apart: 6, of which 4 were waited for; matrix products, arithmetic and copies ran while one was open for 4% of the time, Pallas kernels for 15%

profile of v8, /device:TPU:1, one launch (start us, length us, event | category | flops | bytes accessed | tf_op | source)
XLA Modules:
  0.0 204.4 jit_solution(16334060276175874642)
XLA Ops:
  0.0 4.4 %shard_map.136 = (bf16[64,80,256]{2,1,0:T(8,128)(2,1)}, bf16[64,64,256]{2,1,0:T(8,128)(2,1)}) custom-call(bf16[8,128,256]{2,1,0:T(8,128)(2,1)} %msa_ref.1, f32[1,256]{1,0:T(1,128)} %bitcast.43, bf16[32,256]{1,0:T(8,128)(2,1)} %bitcast.41, bf16[32,256]{1,0:T(8,128)(2,1)} %bitcast.42), custom_call_target="tpu_custom_call" | custom-call | tf_op jit(solution)/shard_map/pallas_call | solution.py:106
  4.4 46.8 %all_to_all.25 = bf16[64,80,256]{2,1,0:T(8,128)(2,1)S(1)} all-to-all(bf16[64,80,256]{2,1,0:T(8,128)(2,1)} %get-tuple-element.13), channel_id=1, replica_groups=mesh['dap'=8,'chip'=8,'core'=2] {'dap','chip'}, dimensions={0} | all-to-all | bytes 5242880 | tf_op jit(solution)/shard_map/all_to_all | solution.py:398
  51.2 5.7 %all-to-all-start.2 = ((bf16[64,64,256]{2,1,0:T(8,128)(2,1)}), bf16[64,64,256]{2,1,0:T(8,128)(2,1)}, u32[]{:S(2)}, u32[]{:S(2)}) async-start(bf16[64,64,256]{2,1,0:T(8,128)(2,1)} %get-tuple-element.15), calls=%async_computation.2 | async-start | bytes 4194304 | tf_op jit(solution)/shard_map/all_to_all | solution.py:398
  57.1 4.9 %shard_map.138 = bf16[8,512,128]{2,1,0:T(8,128)(2,1)S(1)} custom-call(s32[2]{0:T(128)S(1)} %pad_add_fusion.place_ref, bf16[8,8,80,256]{3,2,1,0:T(8,128)(2,1)S(1)} %bitcast.33, bf16[8,8,80,256]{3,2,1,0:T(8,128)(2,1)S(1)} %bitcast.34, bf16[32,4096]{1,0:T(8,128)(2,1)S(1)} %reshape.40.weight_ref), custom_call_target="tpu_custom_call" | custom-call | flops 2147483648 | bytes 3670016 | tf_op jit(solution)/shard_map/pallas_call | solution.py:202
  62.1 2.1 %collective-permute-start = (bf16[8,512,128]{2,1,0:T(8,128)(2,1)S(1)}, bf16[8,512,128]{2,1,0:T(8,128)(2,1)S(1)}, u32[]{:S(2)}, u32[]{:S(2)}) collective-permute-start(bf16[8,512,128]{2,1,0:T(8,128)(2,1)S(1)} %shard_map.138), channel_id=1, source_target_pairs={{0,1},{1,0},{2,3},{3,2},{4,5},{5,4},{6,7},{7,6},{8,9},{9,8},{10,11... | collective-permute-start | bytes 3145736 | tf_op jit(solution)/shard_map/ppermute | solution.py:412
  64.1 1.7 copy-done.3
  65.9 5.0 %shard_map.137.own_ref = bf16[8,512,128]{2,1,0:T(8,128)(2,1)S(1)} custom-call(s32[2]{0:T(128)S(1)} %pad_add_fusion.place_ref, bf16[8,8,80,256]{3,2,1,0:T(8,128)(2,1)S(1)} %bitcast.35, bf16[8,8,80,256]{3,2,1,0:T(8,128)(2,1)S(1)} %bitcast.36, bf16[32,4096]{1,0:T(8,128)(2,1)S(1)} %reshape.40.weight_ref), custom_call_target="tpu_custom_call" | custom-call | flops 2147483648 | bytes 3670016 | tf_op jit(solution)/shard_map/pallas_call | solution.py:202
  70.9 4.6 %shard_map.139 = (bf16[8,512,128]{2,1,0:T(8,128)(2,1)S(1)}, bf16[8,512,128]{2,1,0:T(8,128)(2,1)S(1)}, bf16[128,16,512]{2,1,0:T(8,128)(2,1)S(1)}) custom-call(bf16[8,8,128,128]{3,2,1,0:T(8,128)(2,1)S(1)} %bitcast.31, bf16[8,512,128]{2,1,0:T(8,128)(2,1)S(1)} %shard_map.137.own_ref, bf16[8,512,128]{2,1,0:T(8,128)(2,1)S(1)} %collective-permute-done.arrived_ref, ...), custom_call_target="tpu_custom_call" | custom-call | flops 536870912 | bytes 9437184 | tf_op jit(solution)/shard_map/pallas_call | solution.py:282
  77.9 6.8 %all-to-all-done.2 = bf16[64,64,256]{2,1,0:T(8,128)(2,1)} async-done(((bf16[64,64,256]{2,1,0:T(8,128)(2,1)}), bf16[64,64,256]{2,1,0:T(8,128)(2,1)}, u32[]{:S(2)}, u32[]{:S(2)}) %all-to-all-start.2) | async-done | bytes 2097184 | tf_op jit(solution)/shard_map/all_to_all | solution.py:398
  84.7 7.6 %all-to-all-start.1 = ((bf16[128,16,512]{2,1,0:T(8,128)(2,1)}), bf16[128,16,512]{2,1,0:T(8,128)(2,1)}, u32[]{:S(2)}, u32[]{:S(2)}) async-start(bf16[128,16,512]{2,1,0:T(8,128)(2,1)} %copy-done.5), calls=%async_computation.1 | async-start | bytes 4194304 | tf_op jit(solution)/shard_map/all_to_all | solution.py:421
  92.3 1.7 copy-done.4
  94.1 5.4 %shard_map.141 = bf16[8,512,128]{2,1,0:T(8,128)(2,1)S(1)} custom-call(s32[2]{0:T(128)S(1)} %pad_add_fusion.place_ref, bf16[8,8,64,256]{3,2,1,0:T(8,128)(2,1)} %bitcast.10.gathered_ref, bf16[8,8,80,256]{3,2,1,0:T(8,128)(2,1)S(1)} %bitcast.37, bf16[32,4096]{1,0:T(8,128)(2,1)S(1)} %reshape.40.weight_ref), custom_call_target="tpu_custom_call" | custom-call | flops 2147483648 | bytes 3145728 | tf_op jit(solution)/shard_map/pallas_call | solution.py:202
  101.0 5.4 %shard_map.140.own_ref = bf16[8,512,128]{2,1,0:T(8,128)(2,1)S(1)} custom-call(s32[2]{0:T(128)S(1)} %pad_add_fusion.place_ref, bf16[8,8,64,256]{3,2,1,0:T(8,128)(2,1)} %bitcast.10.gathered_ref, bf16[8,8,80,256]{3,2,1,0:T(8,128)(2,1)S(1)} %bitcast.38, bf16[32,4096]{1,0:T(8,128)(2,1)S(1)} %reshape.40.weight_ref), custom_call_target="tpu_custom_call" | custom-call | flops 2147483648 | bytes 3145728 | tf_op jit(solution)/shard_map/pallas_call | solution.py:202
  106.4 4.7 %shard_map.142 = (bf16[8,512,128]{2,1,0:T(8,128)(2,1)S(1)}, bf16[8,512,128]{2,1,0:T(8,128)(2,1)S(1)}, bf16[128,16,512]{2,1,0:T(8,128)(2,1)S(1)}) custom-call(bf16[8,8,128,128]{3,2,1,0:T(8,128)(2,1)S(1)} %bitcast.32, bf16[8,512,128]{2,1,0:T(8,128)(2,1)S(1)} %shard_map.140.own_ref, bf16[8,512,128]{2,1,0:T(8,128)(2,1)S(1)} %collective-permute-done.1.arrived_ref, ...), custom_call_target="tpu_custom_call" | custom-call | flops 536870912 | bytes 9437184 | tf_op jit(solution)/shard_map/pallas_call | solution.py:282
  114.3 8.5 %all-to-all-done.1 = bf16[128,16,512]{2,1,0:T(8,128)(2,1)} async-done(((bf16[128,16,512]{2,1,0:T(8,128)(2,1)}), bf16[128,16,512]{2,1,0:T(8,128)(2,1)}, u32[]{:S(2)}, u32[]{:S(2)}) %all-to-all-start.1) | async-done | bytes 2097184 | tf_op jit(solution)/shard_map/all_to_all | solution.py:421
  122.8 4.4 %all-to-all-start.3 = ((bf16[128,16,512]{2,1,0:T(8,128)(2,1)}), bf16[128,16,512]{2,1,0:T(8,128)(2,1)S(1)}, u32[]{:S(2)}, u32[]{:S(2)}) async-start(bf16[128,16,512]{2,1,0:T(8,128)(2,1)} %copy-done.6), calls=%async_computation.3 | async-start | bytes 4194304 | tf_op jit(solution)/shard_map/all_to_all | solution.py:421
  127.3 4.1 %convolution_convert_fusion = bf16[1024,1024]{1,0:T(8,128)(2,1)} fusion(bf16[128,16,512]{2,1,0:T(8,128)(2,1)} %all-to-all-done.1), kind=kOutput, calls=%fused_computation.3 | convolution fusion | flops 1074790400 | bytes 4194304 | tf_op jit(solution)/shard_map/dot_general | solution.py:432
  131.4 26.6 %all-to-all-done.3 = bf16[128,16,512]{2,1,0:T(8,128)(2,1)S(1)} async-done(((bf16[128,16,512]{2,1,0:T(8,128)(2,1)}), bf16[128,16,512]{2,1,0:T(8,128)(2,1)S(1)}, u32[]{:S(2)}, u32[]{:S(2)}) %all-to-all-start.3) | async-done | bytes 2097184 | tf_op jit(solution)/shard_map/all_to_all | solution.py:421
  158.0 4.3 %fusion = bf16[128,8,1024]{2,1,0:T(8,128)(2,1)} fusion(bf16[1024,1024]{1,0:T(8,128)(2,1)} %convolution_convert_fusion, bf16[128,16,512]{2,1,0:T(8,128)(2,1)S(1)} %all-to-all-done.3), kind=kOutput, calls=%fused_computation.4 | convolution fusion | flops 1076887552 | bytes 6291456 | tf_op jit(solution)/shard_map/dot_general | solution.py:433
  162.2 5.4 %all-to-all-start.4 = ((bf16[128,8,1024]{2,1,0:T(8,128)(2,1)}), bf16[128,8,1024]{2,1,0:T(8,128)(2,1)}, u32[]{:S(2)}, u32[]{:S(2)}) async-start(bf16[128,8,1024]{2,1,0:T(8,128)(2,1)} %fusion), calls=%async_computation.4 | async-start | bytes 4194304 | tf_op jit(solution)/shard_map/all_to_all | solution.py:434
  167.8 3.0 %divide_convert_fusion.refs_3_ = bf16[8,512,128]{2,1,0:T(8,128)(2,1)} fusion(bf16[8,512,128]{2,1,0:T(8,128)(2,1)} %copy-done.17, bf16[128,128]{1,0:T(8,128)(2,1)S(1)} %copy-done), kind=kOutput, calls=%fused_computation.1 | convolution fusion | flops 136314880 | bytes 2129920 | tf_op jit(solution)/shard_map/dot_general | solution.py:418
  170.8 1.7 divide_convert_fusion.1.refs_1_
  172.5 25.7 %all-to-all-done.4.mixed_ref = bf16[128,8,1024]{2,1,0:T(8,128)(2,1)} async-done(((bf16[128,8,1024]{2,1,0:T(8,128)(2,1)}), bf16[128,8,1024]{2,1,0:T(8,128)(2,1)}, u32[]{:S(2)}, u32[]{:S(2)}) %all-to-all-start.4) | async-done | bytes 2097184 | tf_op jit(solution)/shard_map/all_to_all | solution.py:434
  198.2 6.2 %shard_map.143 = bf16[8,1024,128]{2,1,0:T(8,128)(2,1)} custom-call(bf16[128,8,1024]{2,1,0:T(8,128)(2,1)} %all-to-all-done.4.mixed_ref, bf16[8,512,128]{2,1,0:T(8,128)(2,1)S(1)} %get-tuple-element.17.refs_0_, bf16[8,512,128]{2,1,0:T(8,128)(2,1)} %divide_convert_fusion.1.refs_1_, bf16[8,512,128]{2,1,0:T(8,128)(2,1)} %copy-done.7, ...), custom_call_target="tpu_custom_call" | custom-call | flops 268435456 | bytes 8388608 | tf_op jit(solution)/shard_map/pallas_call | solution.py:346
  (44 shorter events, 7.5 us)
Async XLA Ops:
  0.0 167.8 %copy-start = (bf16[128,128]{1,0:T(8,128)(2,1)S(1)}, bf16[128,128]{1,0:T(8,128)(2,1)}, u32[]{:S(2)}) copy-start(bf16[128,128]{1,0:T(8,128)(2,1)} %param.25) | copy-start | bytes 98308
  51.1 6.0 %copy-start.2 = (bf16[64,80,256]{2,1,0:T(8,128)(2,1)}, bf16[64,80,256]{2,1,0:T(8,128)(2,1)S(1)}, u32[]{:S(2)}) copy-start(bf16[64,80,256]{2,1,0:T(8,128)(2,1)S(1)} %all_to_all.25) | copy-start | bytes 7864324
  51.1 5.7 %copy-start.18 = (bf16[1024,128]{1,0:T(8,128)(2,1)S(1)}, bf16[1024,128]{1,0:T(8,128)(2,1)}, u32[]{:S(2)}) copy-start(bf16[1024,128]{1,0:T(8,128)(2,1)} %param.19) | copy-start | bytes 786436
  51.2 33.6 %all-to-all-start.2 = ((bf16[64,64,256]{2,1,0:T(8,128)(2,1)}), bf16[64,64,256]{2,1,0:T(8,128)(2,1)}, u32[]{:S(2)}, u32[]{:S(2)}) async-start(bf16[64,64,256]{2,1,0:T(8,128)(2,1)} %get-tuple-element.15), calls=%async_computation.2 | async-start | bytes 4194304 | tf_op jit(solution)/shard_map/all_to_all | solution.py:398
  62.1 8.8 %copy-start.1 = (bf16[8,1024,128]{2,1,0:T(8,128)(2,1)S(1)}, bf16[8,1024,128]{2,1,0:T(8,128)(2,1)}, u32[]{:S(2)}) copy-start(bf16[8,1024,128]{2,1,0:T(8,128)(2,1)} %param.15) | copy-start | bytes 6291460
  62.1 8.8 %collective-permute-start = (bf16[8,512,128]{2,1,0:T(8,128)(2,1)S(1)}, bf16[8,512,128]{2,1,0:T(8,128)(2,1)S(1)}, u32[]{:S(2)}, u32[]{:S(2)}) collective-permute-start(bf16[8,512,128]{2,1,0:T(8,128)(2,1)S(1)} %shard_map.138), channel_id=1, source_target_pairs={{0,1},{1,0},{2,3},{3,2},{4,5},{5,4},{6,7},{7,6},{8,9},{9,8},{10,11... | collective-permute-start | bytes 3145736 | tf_op jit(solution)/shard_map/ppermute | solution.py:412
  64.1 1.7 copy-start.3
  65.9 5.0 %copy-start.8 = (bf16[128,128]{1,0:T(8,128)(2,1)S(1)}, bf16[128,128]{1,0:T(8,128)(2,1)}, u32[]{:S(2)}) copy-start(bf16[128,128]{1,0:T(8,128)(2,1)} %rest_0_.3) | copy-start | bytes 98308
  65.9 5.0 %copy-start.9 = (bf16[128,128]{1,0:T(8,128)(2,1)S(1)}, bf16[128,128]{1,0:T(8,128)(2,1)}, u32[]{:S(2)}) copy-start(bf16[128,128]{1,0:T(8,128)(2,1)} %rest_1_.3) | copy-start | bytes 98308
  65.9 5.0 %copy-start.10 = (bf16[128,128]{1,0:T(8,128)(2,1)S(1)}, bf16[128,128]{1,0:T(8,128)(2,1)}, u32[]{:S(2)}) copy-start(bf16[128,128]{1,0:T(8,128)(2,1)} %rest_2_.3) | copy-start | bytes 98308
  65.9 5.0 %copy-start.11 = (bf16[128,128]{1,0:T(8,128)(2,1)S(1)}, bf16[128,128]{1,0:T(8,128)(2,1)}, u32[]{:S(2)}) copy-start(bf16[128,128]{1,0:T(8,128)(2,1)} %rest_3_.3) | copy-start | bytes 98308
  65.9 5.0 %copy-start.14 = (f32[128]{0:T(128)S(1)}, f32[128]{0:T(128)}, u32[]{:S(2)}) copy-start(f32[128]{0:T(128)} %param.20) | copy-start | bytes 1540
  75.6 1.3 copy-start.5
  84.7 38.1 %all-to-all-start.1 = ((bf16[128,16,512]{2,1,0:T(8,128)(2,1)}), bf16[128,16,512]{2,1,0:T(8,128)(2,1)}, u32[]{:S(2)}, u32[]{:S(2)}) async-start(bf16[128,16,512]{2,1,0:T(8,128)(2,1)} %copy-done.5), calls=%async_computation.1 | async-start | bytes 4194304 | tf_op jit(solution)/shard_map/all_to_all | solution.py:421
  92.3 1.7 copy-start.4
  99.4 6.9 %copy-start.12 = (bf16[128,128]{1,0:T(8,128)(2,1)S(1)}, bf16[128,128]{1,0:T(8,128)(2,1)}, u32[]{:S(2)}) copy-start(bf16[128,128]{1,0:T(8,128)(2,1)} %rest_3_.3) | copy-start | bytes 98308
  99.4 6.9 %collective-permute-start.1 = (bf16[8,512,128]{2,1,0:T(8,128)(2,1)S(1)}, bf16[8,512,128]{2,1,0:T(8,128)(2,1)S(1)}, u32[]{:S(2)}, u32[]{:S(2)}) collective-permute-start(bf16[8,512,128]{2,1,0:T(8,128)(2,1)S(1)} %shard_map.141), channel_id=1, source_target_pairs={{0,1},{1,0},{2,3},{3,2},{4,5},{5,4},{6,7},{7,6},{8,9},{9,8},{10,11... | collective-permute-start | bytes 3145736 | tf_op jit(solution)/shard_map/ppermute | solution.py:412
  111.0 1.3 copy-start.6
  113.3 1.0 copy-start.17
  122.8 35.1 %all-to-all-start.3 = ((bf16[128,16,512]{2,1,0:T(8,128)(2,1)}), bf16[128,16,512]{2,1,0:T(8,128)(2,1)S(1)}, u32[]{:S(2)}, u32[]{:S(2)}) async-start(bf16[128,16,512]{2,1,0:T(8,128)(2,1)} %copy-done.6), calls=%async_computation.3 | async-start | bytes 4194304 | tf_op jit(solution)/shard_map/all_to_all | solution.py:421
  162.2 5.5 %copy-start.19 = (f32[128]{0:T(128)S(1)}, f32[128]{0:T(128)}, u32[]{:S(2)}) copy-start(f32[128]{0:T(128)} %param.26) | copy-start | bytes 1540
  162.2 35.9 %all-to-all-start.4 = ((bf16[128,8,1024]{2,1,0:T(8,128)(2,1)}), bf16[128,8,1024]{2,1,0:T(8,128)(2,1)}, u32[]{:S(2)}, u32[]{:S(2)}) async-start(bf16[128,8,1024]{2,1,0:T(8,128)(2,1)} %fusion), calls=%async_computation.4 | async-start | bytes 4194304 | tf_op jit(solution)/shard_map/all_to_all | solution.py:434
  167.8 3.0 %copy-start.16 = (bf16[8,512,128]{2,1,0:T(8,128)(2,1)S(1)}, bf16[8,512,128]{2,1,0:T(8,128)(2,1)}, u32[]{:S(2)}) copy-start(bf16[8,512,128]{2,1,0:T(8,128)(2,1)} %copy-done.15) | copy-start | bytes 3145732
  170.8 27.4 %copy-start.13 = (bf16[128,128]{1,0:T(8,128)(2,1)S(1)}, bf16[128,128]{1,0:T(8,128)(2,1)}, u32[]{:S(2)}) copy-start(bf16[128,128]{1,0:T(8,128)(2,1)} %refs_5_.1) | copy-start | bytes 98308
  (2 other events, 2.0 us)
